TPU v7x, 32 devices: a whole 2x2x4 slice. The times are simulated.
32 devices in a mesh: groups: 2 (over x), tiles: 16 (over z, y, core).
Axes of the slice: x: 2, y: 2, z: 4, core: 2. Of those that a mesh axis runs over, the one named last changes fastest.
Arguments:
- input_field: bfloat16 [64, 32, 32, 256], P(('groups', 'tiles')), parts along dimension 0, may hold values from -6 to 6
- cotangent: bfloat16 [64, 32, 32, 256], P(('groups', 'tiles')), parts along dimension 0, may hold values from -6 to 6
- weight: bfloat16 [9, 256, 256], replicated, may hold values from -0.125 to 0.125
- neighbours: int32 [32, 8], P('tiles'), may hold values from -1 to 31, as said below
- land_mask: int32 [32, 32, 32], P('tiles'), may hold values from 0 to 1, as said below
Outputs:
- layer_output: bfloat16 [64, 32, 32, 256], P(('groups', 'tiles')), parts along dimension 0
- input_grad: bfloat16 [64, 32, 32, 256], P(('groups', 'tiles')), parts along dimension 0
- weight_grad: float32 [512, 2304], P(('groups', 'tiles')), parts along dimension 0
There are 2 independent parts, one for each index of `groups`. A program takes and returns all parts, laid end to end along the dimension named above; an argument that names none is the same for every part. Nothing has to cross between parts.
Inputs may be any that keep to these rules, and one draw needn't show every extreme that they name: Device i of the tile axis holds the ocean tiles of tile column i of a band of 4 tile rows, in its first slots, 1 to 2 of them; the last device holds 2; other slots are empty. A row lists the global slot (device index times 2 plus slot) of the tile's neighbours in the order north, south, west, east, north-west, north-east, south-west, south-east, or -1 where there is none (land tile, edge of the band, or an empty slot). West and east wrap around the columns, so every neighbour lies on the same device (north, south) or on the device of index one lower (west side) or one higher (east side), wrapping. `land_mask`: all zero in empty slots.
All inputs are finite; a program needn't handle non-finite values.
Results may differ from a plain program's by a relative error of at most 0.0032.
Values may be sent and summed in bfloat16 or wider, within the bound.
No kernel may reach another device: no remote copies, remote signals or barrier semaphores. Data moves between devices by JAX's collectives and lax.ppermute only.
A program may use at most 128 MiB of HBM per device.

v0:
```python
import math

import jax
import jax.numpy as jnp
from jax import lax
from jax.sharding import PartitionSpec as P

DILATION_STEP = 2


GELU_SCALE = math.sqrt(2.0 / math.pi)
GELU_CUBIC = 0.044715
FORWARD_FORM = "sabc,cd->sabd"
BACKWARD_FORM = "sabd,cd->sabc"


def from_behind(value, axis, steps):
    count = lax.axis_size(axis)
    pairs = [(source, (source + steps) % count) for source in range(count)]
    return lax.ppermute(value, axis, pairs)


def gelu_pair(hidden_state):
    tanh_arg = GELU_SCALE * (hidden_state + GELU_CUBIC * hidden_state * hidden_state * hidden_state)
    tanh_value = jnp.tanh(tanh_arg)
    activated = 0.5 * hidden_state * (1.0 + tanh_value)
    derivative = 0.5 * (1.0 + tanh_value) + 0.5 * hidden_state * (
        1.0 - tanh_value * tanh_value
    ) * GELU_SCALE * (1.0 + 3.0 * GELU_CUBIC * hidden_state * hidden_state)
    return (activated, derivative)


def tap_displacements(dilation):
    return [
        ((row_step - 1) * dilation, (col_step - 1) * dilation)
        for row_step in range(3)
        for col_step in range(3)
    ]


def swap_edges(east_columns, west_columns):
    from_west = from_behind(east_columns, "tiles", 1)
    from_east = from_behind(west_columns, "tiles", -1)
    return (from_west, from_east)


def select_tiles(source_pool, local_ids, present):
    chosen = jnp.take(source_pool, local_ids, axis=0)
    return chosen * present[:, None, None, None].astype(source_pool.dtype)


def pad_tiles(own_tiles, from_west, from_east, neighbours, halo_margin_width, device, device_count):
    slot_count = own_tiles.shape[0]
    tile_edge = own_tiles.shape[1]
    inner_cut = tile_edge - halo_margin_width
    present = neighbours >= 0
    base_here = device * slot_count
    base_west = (device - 1) % device_count * slot_count
    base_east = (device + 1) % device_count * slot_count

    def local_ids(column, base_slot):
        return jnp.clip(neighbours[:, column] - base_slot, 0, slot_count - 1)

    north_strip = select_tiles(own_tiles[:, inner_cut:], local_ids(0, base_here), present[:, 0])
    south_strip = select_tiles(
        own_tiles[:, :halo_margin_width], local_ids(1, base_here), present[:, 1]
    )
    west_strip = select_tiles(from_west, local_ids(2, base_west), present[:, 2])
    east_strip = select_tiles(from_east, local_ids(3, base_east), present[:, 3])
    north_west = select_tiles(from_west[:, inner_cut:], local_ids(4, base_west), present[:, 4])
    north_east = select_tiles(from_east[:, inner_cut:], local_ids(5, base_east), present[:, 5])
    south_west = select_tiles(
        from_west[:, :halo_margin_width], local_ids(6, base_west), present[:, 6]
    )
    south_east = select_tiles(
        from_east[:, :halo_margin_width], local_ids(7, base_east), present[:, 7]
    )
    upper_band = jnp.concatenate([north_west, north_strip, north_east], axis=2)
    middle = jnp.concatenate([west_strip, own_tiles, east_strip], axis=2)
    lower_band = jnp.concatenate([south_west, south_strip, south_east], axis=2)
    return jnp.concatenate([upper_band, middle, lower_band], axis=1)


def conv_taps(haloed_field, weight, start, span, offsets, form):
    accumulated = None
    for tap_index, (row_displacement, column_shift) in enumerate(offsets):
        shifted_window = haloed_field[
            :,
            start + row_displacement : start + row_displacement + span,
            start + column_shift : start + column_shift + span,
        ]
        product_term = jnp.einsum(
            form, shifted_window, weight[tap_index], preferred_element_type=jnp.float32
        )
        accumulated = product_term if accumulated is None else accumulated + product_term
    return accumulated


def shards(input_field, cotangent, weight, neighbours, land_mask):
    device = lax.axis_index("tiles")
    device_count = lax.axis_size("tiles")
    slot_count = input_field.shape[0]
    tile_edge = input_field.shape[1]
    channels = input_field.shape[3]
    halo_margin_width = DILATION_STEP
    ocean_half = land_mask.astype(jnp.bfloat16)[..., None]
    ocean_full = land_mask.astype(jnp.float32)[..., None]
    ocean_masked_input = input_field * ocean_half
    masked_cotangent = cotangent * ocean_half
    forward_tap_list = tap_displacements(DILATION_STEP)
    backward_tap_list = [
        (-row_displacement, -column_shift) for row_displacement, column_shift in forward_tap_list
    ]
    inner_cut = tile_edge - halo_margin_width
    from_west, from_east = swap_edges(
        ocean_masked_input[:, :, inner_cut:], ocean_masked_input[:, :, :halo_margin_width]
    )
    haloed_input = pad_tiles(
        ocean_masked_input,
        from_west,
        from_east,
        neighbours,
        halo_margin_width,
        device,
        device_count,
    )
    hidden_state = conv_taps(
        haloed_input, weight, halo_margin_width, tile_edge, forward_tap_list, FORWARD_FORM
    )
    activated, derivative = gelu_pair(hidden_state)
    hidden_gradient = (masked_cotangent.astype(jnp.float32) * derivative).astype(jnp.bfloat16)
    grad_west, grad_east = swap_edges(
        hidden_gradient[:, :, inner_cut:], hidden_gradient[:, :, :halo_margin_width]
    )
    haloed_gradient = pad_tiles(
        hidden_gradient, grad_west, grad_east, neighbours, halo_margin_width, device, device_count
    )
    layer_output = (ocean_full * (input_field.astype(jnp.float32) + activated)).astype(jnp.bfloat16)
    backward_pass = conv_taps(
        haloed_gradient, weight, halo_margin_width, tile_edge, backward_tap_list, BACKWARD_FORM
    )
    input_grad = (ocean_full * (cotangent.astype(jnp.float32) + backward_pass)).astype(jnp.bfloat16)
    scale_factor = 1.0 / (tile_edge * math.sqrt(slot_count * device_count))
    own_rows = channels // device_count
    pieces = []
    for row_displacement, column_shift in forward_tap_list:
        shifted_window = haloed_input[
            :,
            halo_margin_width + row_displacement : halo_margin_width + row_displacement + tile_edge,
            halo_margin_width + column_shift : halo_margin_width + column_shift + tile_edge,
        ]
        pieces.append(
            jnp.einsum(
                "sabo,sabc->oc", hidden_gradient, shifted_window, preferred_element_type=jnp.float32
            )
        )
    summed = lax.psum(jnp.concatenate(pieces, axis=1) * scale_factor, "tiles")
    weight_grad = lax.dynamic_slice_in_dim(summed, device * own_rows, own_rows, 0)
    return (layer_output, input_grad, weight_grad)


def solution(mesh):
    return jax.shard_map(
        shards,
        mesh=mesh,
        in_specs=(
            P(("groups", "tiles"), None, None, None),
            P(("groups", "tiles"), None, None, None),
            P(),
            P("tiles", None),
            P("tiles", None, None),
        ),
        out_specs=(
            P(("groups", "tiles"), None, None, None),
            P(("groups", "tiles"), None, None, None),
            P(("groups", "tiles"), None),
        ),
        check_vma=False,
    )
```

profile of v0, /device:TPU:0, one launch (start us, length us, event | category | flops | bytes accessed | tf_op | source)
XLA Modules:
  0.0 163.8 jit_solution(5020012455985592514)
XLA Ops:
  7.2 0.8 fusion.132
  8.1 1.6 broadcast_multiply_fusion.1
  10.2 5.1 %collective-permute-start.1 = (bf16[2,32,2,256]{3,2,1,0:T(2,128)(2,1)S(1)}, bf16[2,32,2,256]{3,2,1,0:T(2,128)(2,1)S(1)}, u32[]{:S(2)}, u32[]{:S(2)}) collective-permute-start(bf16[2,32,2,256]{3,2,1,0:T(2,128)(2,1)S(1)} %get-tuple-element.46), channel_id=1, source_target_pairs={{0,15},{1,0},{2,1},{3,2},{4,3},{5,4},{6,5},{7,6},{8,7},{9,8},{10,9... | collective-permute-start | bytes 196616 | tf_op jit(solution)/shard_map/ppermute | solution.py:20
  17.9 0.8 fusion.106
  19.4 0.6 pad_clamp_fusion.7
  20.0 2.7 %fusion.53 = f32[2,32,32,256]{3,2,1,0:T(8,128)} fusion(bf16[2,32,32,256]{3,2,1,0:T(8,128)(2,1)S(1)} %broadcast_multiply_fusion.1, bf16[9,256,256]{2,1,0:T(8,128)(2,1)} %param.13), kind=kOutput, calls=%fused_computation.93 | convolution fusion | flops 268435456 | bytes 3276800 | tf_op jit(solution)/shard_map/sabc,cd->sabd/dot_general | solution.py:92
  24.0 0.6 pad_clamp_fusion.5
  24.6 0.7 gather_fusion.3
  25.4 0.7 gather_fusion.4
  26.3 1.1 pad_maximum_fusion.5
  27.4 0.8 fusion.130
  28.8 0.7 gather_fusion.7
  29.5 0.7 gather_fusion
  30.2 0.7 gather_fusion.2
  30.9 0.8 fusion.102
  31.7 0.7 fusion.104
  32.5 0.7 fusion.98
  33.2 0.8 fusion.100
  34.0 2.0 %maximum_maximum_fusion = (bf16[2,34,36,256]{3,2,1,0:T(8,128)(2,1)S(1)}, bf16[2,34,36,256]{3,2,1,0:T(8,128)(2,1)S(1)}) fusion(bf16[2,32,2,256]{3,2,1,0:T(2,128)(2,1)S(1)} %fusion.87, bf16[2,32,32,256]{3,2,1,0:T(8,128)(2,1)S(1)} %broadcast_multiply_fusion.1, bf16[2,32,2,256]{3,2,1,0:T(2,128)(2,1)S(1)} %fusion.85, bf16[2,2,2,256]{3,2,1,0:T(2,128)(2,1)S(1)} %fusion.100, ...), kind=kLoop, calls=%fused_computation.28 | loop fusion | flops 15040512 | bytes 3833856 | tf_op jit(solution)/shard_map/concatenate | solution.py:81
  38.2 0.8 fusion.123
  39.0 0.8 fusion.122
  40.7 1.1 copy-done.3
  42.4 3.7 %fusion.6 = (bf16[2,32,32,256]{3,2,1,0:T(8,128)(2,1)S(1)}, bf16[2,32,32,256]{3,2,1,0:T(8,128)(2,1)}) fusion(bf16[2,32,32,256]{3,2,1,0:T(8,128)(2,1)S(1)} %copy-done.4, bf16[2,32,32]{2,1,0:T(8,128)(2,1)S(1)} %get-tuple-element.56, bf16[2,32,32,256]{3,2,1,0:T(8,128)(2,1)S(1)} %copy-done.6, f32[2,32,32]{2,1,0:T(8,128)S(1)} %get-tuple-element.55, ...), kind=kOutput, calls=%fused_computation.24 | convolution fusion | flops 286261248 | bytes 22200320 | tf_op jit(solution)/shard_map/sabc,cd->sabd/dot_general | solution.py:92
  46.1 0.7 fusion.125
  46.9 1.8 %fusion.51 = f32[2,32,32,256]{3,2,1,0:T(8,128)} fusion(bf16[2,32,32,256]{3,2,1,0:T(8,128)(2,1)S(1)} %get-tuple-element.25, bf16[9,256,256]{2,1,0:T(8,128)(2,1)S(1)} %copy-done.7), kind=kOutput, calls=%fused_computation.91 | convolution fusion | flops 268435456 | bytes 3276800 | tf_op jit(solution)/shard_map/sabd,cd->sabc/dot_general | solution.py:92
  50.4 0.7 copy-done.1
  54.3 1.6 %broadcast_multiply_fusion = f32[256,2304]{0,1:T(8,128)} fusion(f32[256,2304]{0,1:T(8,128)S(1)} %fusion.7), kind=kLoop, calls=%fused_computation.32 | loop fusion | flops 589824 | bytes 4718592 | tf_op jit(solution)/shard_map/mul | solution.py:157
  56.0 0.7 collective-permute-start.3
  58.1 0.8 collective-permute-done.3
  58.9 0.7 gather_fusion.9
  59.8 1.4 fusion.23
  61.2 2.0 %collective-permute-done.2 = bf16[2,32,2,256]{3,2,1,0:T(2,128)(2,1)} collective-permute-done((bf16[2,32,2,256]{3,2,1,0:T(2,128)(2,1)S(1)}, bf16[2,32,2,256]{3,2,1,0:T(2,128)(2,1)}, u32[]{:S(2)}, u32[]{:S(2)}) %collective-permute-start.2) | collective-permute-done | bytes 65568 | tf_op jit(solution)/shard_map/ppermute | solution.py:20
  63.2 1.5 gather_fusion.8
  64.9 0.7 fusion.129
  65.6 0.7 gather_fusion.15
  66.3 0.8 fusion.101
  67.1 0.7 fusion.128
  67.8 0.7 gather_fusion.13
  68.5 0.7 fusion.99
  69.2 0.7 gather_fusion.10
  69.9 0.7 fusion.103
  70.6 0.7 gather_fusion.12
  71.4 1.8 %maximum_maximum_fusion.2 = (bf16[2,34,36,256]{3,2,1,0:T(8,128)(2,1)S(1)}, bf16[2,34,36,256]{3,2,1,0:T(8,128)(2,1)S(1)}) fusion(bf16[2,2,2,256]{3,2,1,0:T(2,128)(2,1)S(1)} %fusion.105, bf16[2,2,32,256]{3,2,1,0:T(8,128)(2,1)S(1)} %select_multiply_fusion.1, bf16[2,2,2,256]{3,2,1,0:T(2,128)(2,1)S(1)} %fusion.103, bf16[2,32,2,256]{3,2,1,0:T(2,128)(2,1)S(1)} %fusion.88, ...), kind=kLoop, calls=%fused_computation.30 | loop fusion | flops 15040512 | bytes 3833856 | tf_op jit(solution)/shard_map/concatenate | solution.py:81
  76.2 1.1 copy-done.2
  77.5 2.3 %multiply_convert_fusion = bf16[2,32,32,256]{3,2,1,0:T(8,128)(2,1)} fusion(f32[2,32,32,256]{3,2,1,0:T(8,128)S(1)} %fusion.17, f32[2,32,32,256]{3,2,1,0:T(8,128)S(1)} %fusion.19, f32[2,32,32,256]{3,2,1,0:T(8,128)S(1)} %fusion.21, f32[2,32,32,256]{3,2,1,0:T(8,128)S(1)} %copy-done.2, f32[2,32,32,256]{3,2,1,0:T(8,128)S(1)} %fusion.23, ...), kind=kOutput, calls=%fused_computation.25 | convolution fusion | flops 274726912 | bytes 20086784 | tf_op jit(solution)/shard_map/sabd,cd->sabc/dot_general | solution.py:92
  79.8 74.5 %all-reduce.2.cloned.1.call-done = f32[256,2304]{0,1:T(8,128)} async-done(((f32[256,2304]{0,1:T(8,128)}), f32[256,2304]{0,1:T(8,128)}) %all-reduce.2.cloned.1.call-update) | async-done | bytes 2359312 | tf_op jit(solution)/shard_map/psum | solution.py:157
  154.3 1.6 constant_dynamic-slice_fusion
  156.0 1.0 copy.26
  (126 shorter events, 19.3 us)
Async XLA Ops:
  7.2 8.2 %copy-start.11 = (s32[2,8]{1,0:T(2,128)S(1)}, s32[2,8]{1,0:T(2,128)}, u32[]{:S(2)}) copy-start(s32[2,8]{1,0:T(2,128)} %param.14) | copy-start | bytes 196
  7.2 147.2 %all-reduce.2.cloned.1.call-start = ((), (), s32[]{:S(2)}) async-start(), calls=%async_computation | async-start | bytes 4718592 | tf_op jit(solution)/shard_map/psum | solution.py:157
  9.7 14.9 %collective-permute-start = (bf16[2,32,2,256]{3,2,1,0:T(2,128)(2,1)S(1)}, bf16[2,32,2,256]{3,2,1,0:T(2,128)(2,1)S(1)}, u32[]{:S(2)}, u32[]{:S(2)}) collective-permute-start(bf16[2,32,2,256]{3,2,1,0:T(2,128)(2,1)S(1)} %get-tuple-element.45), channel_id=1, source_target_pairs={{0,1},{1,2},{2,3},{3,4},{4,5},{5,6},{6,7},{7,8},{8,9},{9,10},{10,1... | collective-permute-start | bytes 196616 | tf_op jit(solution)/shard_map/ppermute | solution.py:20
  10.2 15.2 %collective-permute-start.1 = (bf16[2,32,2,256]{3,2,1,0:T(2,128)(2,1)S(1)}, bf16[2,32,2,256]{3,2,1,0:T(2,128)(2,1)S(1)}, u32[]{:S(2)}, u32[]{:S(2)}) collective-permute-start(bf16[2,32,2,256]{3,2,1,0:T(2,128)(2,1)S(1)} %get-tuple-element.46), channel_id=1, source_target_pairs={{0,15},{1,0},{2,1},{3,2},{4,3},{5,4},{6,5},{7,6},{8,7},{9,8},{10,9... | collective-permute-start | bytes 196616 | tf_op jit(solution)/shard_map/ppermute | solution.py:20
  16.3 7.6 %copy-start.25 = (pred[2]{0:T(512)(128)(4,1)}, pred[2]{0:T(512)(128)(4,1)S(1)}, u32[]{:S(2)}) copy-start(pred[2]{0:T(512)(128)(4,1)S(1)} %get-tuple-element.69) | copy-start | bytes 10
  16.8 7.0 %copy-start.27 = (pred[2]{0:T(512)(128)(4,1)}, pred[2]{0:T(512)(128)(4,1)S(1)}, u32[]{:S(2)}) copy-start(pred[2]{0:T(512)(128)(4,1)S(1)} %get-tuple-element.64) | copy-start | bytes 10
  17.3 8.8 %copy-start.23 = (pred[2]{0:T(512)(128)(4,1)}, pred[2]{0:T(512)(128)(4,1)S(1)}, u32[]{:S(2)}) copy-start(pred[2]{0:T(512)(128)(4,1)S(1)} %get-tuple-element.66) | copy-start | bytes 10
  17.9 7.4 %copy-start.21 = (pred[2]{0:T(512)(128)(4,1)}, pred[2]{0:T(512)(128)(4,1)S(1)}, u32[]{:S(2)}) copy-start(pred[2]{0:T(512)(128)(4,1)S(1)} %get-tuple-element.67) | copy-start | bytes 10
  18.7 5.0 %copy-start.17 = (bf16[2]{0:T(256)(128)(2,1)}, bf16[2]{0:T(256)(128)(2,1)S(1)}, u32[]{:S(2)}) copy-start(bf16[2]{0:T(256)(128)(2,1)S(1)} %get-tuple-element.19) | copy-start | bytes 16
  18.7 5.2 %copy-start.19 = (bf16[2]{0:T(256)(128)(2,1)}, bf16[2]{0:T(256)(128)(2,1)S(1)}, u32[]{:S(2)}) copy-start(bf16[2]{0:T(256)(128)(2,1)S(1)} %get-tuple-element.24) | copy-start | bytes 16
  18.8 6.5 %copy-start.13 = (bf16[2]{0:T(256)(128)(2,1)}, bf16[2]{0:T(256)(128)(2,1)S(1)}, u32[]{:S(2)}) copy-start(bf16[2]{0:T(256)(128)(2,1)S(1)} %get-tuple-element.22) | copy-start | bytes 16
  18.8 7.4 %copy-start.15 = (bf16[2]{0:T(256)(128)(2,1)}, bf16[2]{0:T(256)(128)(2,1)S(1)}, u32[]{:S(2)}) copy-start(bf16[2]{0:T(256)(128)(2,1)S(1)} %get-tuple-element.21) | copy-start | bytes 16
  18.8 9.4 %copy-start.12 = (s32[1024]{0:T(1024)}, s32[1024]{0:T(1024)S(1)}, u32[]{:S(2)}) copy-start(s32[1024]{0:T(1024)S(1)} %pad_clamp_fusion.2) | copy-start | bytes 12292
  24.6 1.6 copy-start.9
  27.4 12.8 %copy-start = (bf16[2,32,32,256]{3,2,1,0:T(8,128)(2,1)}, bf16[2,32,32,256]{3,2,1,0:T(8,128)(2,1)S(1)}, u32[]{:S(2)}) copy-start(bf16[2,32,32,256]{3,2,1,0:T(8,128)(2,1)S(1)} %get-tuple-element.43) | copy-start | bytes 3145732
  30.9 5.1 %copy-start.7 = (bf16[9,256,256]{2,1,0:T(8,128)(2,1)S(1)}, bf16[9,256,256]{2,1,0:T(8,128)(2,1)}, u32[]{:S(2)}) copy-start(bf16[9,256,256]{2,1,0:T(8,128)(2,1)} %param.13) | copy-start | bytes 3538948
  40.2 1.6 copy-start.3
  40.2 1.8 %copy-start.4 = (bf16[2,32,32,256]{3,2,1,0:T(8,128)(2,1)S(1)}, bf16[2,32,32,256]{3,2,1,0:T(8,128)(2,1)}, u32[]{:S(2)}) copy-start(bf16[2,32,32,256]{3,2,1,0:T(8,128)(2,1)} %param.12) | copy-start | bytes 3145732
  40.2 2.1 %copy-start.6 = (bf16[2,32,32,256]{3,2,1,0:T(8,128)(2,1)S(1)}, bf16[2,32,32,256]{3,2,1,0:T(8,128)(2,1)}, u32[]{:S(2)}) copy-start(bf16[2,32,32,256]{3,2,1,0:T(8,128)(2,1)} %param.11) | copy-start | bytes 3145732
  49.8 1.2 copy-start.1
  55.9 1.3 copy-start.20
  55.9 1.4 copy-start.26
  55.9 2.1 %copy-start.18 = (bf16[2]{0:T(256)(128)(2,1)S(1)}, bf16[2]{0:T(256)(128)(2,1)}, u32[]{:S(2)}) copy-start(bf16[2]{0:T(256)(128)(2,1)} %copy-done.17) | copy-start | bytes 16
  55.9 2.1 %copy-start.28 = (pred[2]{0:T(512)(128)(4,1)S(1)}, pred[2]{0:T(512)(128)(4,1)}, u32[]{:S(2)}) copy-start(pred[2]{0:T(512)(128)(4,1)} %copy-done.27) | copy-start | bytes 10
  55.9 3.7 %copy-start.16 = (bf16[2]{0:T(256)(128)(2,1)S(1)}, bf16[2]{0:T(256)(128)(2,1)}, u32[]{:S(2)}) copy-start(bf16[2]{0:T(256)(128)(2,1)} %copy-done.15) | copy-start | bytes 16
  55.9 3.7 %copy-start.24 = (pred[2]{0:T(512)(128)(4,1)S(1)}, pred[2]{0:T(512)(128)(4,1)}, u32[]{:S(2)}) copy-start(pred[2]{0:T(512)(128)(4,1)} %copy-done.23) | copy-start | bytes 10
  56.0 2.9 %collective-permute-start.3 = (bf16[2,32,2,256]{3,2,1,0:T(2,128)(2,1)}, bf16[2,32,2,256]{3,2,1,0:T(2,128)(2,1)S(1)}, u32[]{:S(2)}, u32[]{:S(2)}) collective-permute-start(bf16[2,32,2,256]{3,2,1,0:T(2,128)(2,1)} %get-tuple-element.40), channel_id=1, source_target_pairs={{0,15},{1,0},{2,1},{3,2},{4,3},{5,4},{6,5},{7,6},{8,7},{9,8},{10,9... | collective-permute-start | bytes 196616 | tf_op jit(solution)/shard_map/ppermute | solution.py:20
  56.7 6.6 %collective-permute-start.2 = (bf16[2,32,2,256]{3,2,1,0:T(2,128)(2,1)S(1)}, bf16[2,32,2,256]{3,2,1,0:T(2,128)(2,1)}, u32[]{:S(2)}, u32[]{:S(2)}) collective-permute-start(bf16[2,32,2,256]{3,2,1,0:T(2,128)(2,1)S(1)} %get-tuple-element.39), channel_id=1, source_target_pairs={{0,1},{1,2},{2,3},{3,4},{4,5},{5,6},{6,7},{7,8},{8,9},{9,10},{10,1... | collective-permute-start | bytes 196616 | tf_op jit(solution)/shard_map/ppermute | solution.py:20
  57.3 7.5 %copy-start.14 = (bf16[2]{0:T(256)(128)(2,1)S(1)}, bf16[2]{0:T(256)(128)(2,1)}, u32[]{:S(2)}) copy-start(bf16[2]{0:T(256)(128)(2,1)} %copy-done.13) | copy-start | bytes 16
  57.3 7.5 %copy-start.22 = (pred[2]{0:T(512)(128)(4,1)S(1)}, pred[2]{0:T(512)(128)(4,1)}, u32[]{:S(2)}) copy-start(pred[2]{0:T(512)(128)(4,1)} %copy-done.21) | copy-start | bytes 10
  57.4 11.1 %copy-start.31 = (bf16[2]{0:T(256)(128)(2,1)S(1)}, bf16[2]{0:T(256)(128)(2,1)}, u32[]{:S(2)}) copy-start(bf16[2]{0:T(256)(128)(2,1)} %get-tuple-element.17) | copy-start | bytes 16
  57.4 12.6 %copy-start.30 = (bf16[2]{0:T(256)(128)(2,1)S(1)}, bf16[2]{0:T(256)(128)(2,1)}, u32[]{:S(2)}) copy-start(bf16[2]{0:T(256)(128)(2,1)} %get-tuple-element.20) | copy-start | bytes 16
  57.4 13.9 %copy-start.29 = (bf16[2]{0:T(256)(128)(2,1)S(1)}, bf16[2]{0:T(256)(128)(2,1)}, u32[]{:S(2)}) copy-start(bf16[2]{0:T(256)(128)(2,1)} %get-tuple-element.18) | copy-start | bytes 16
  58.0 13.3 %copy-start.32 = (pred[2]{0:T(512)(128)(4,1)S(1)}, pred[2]{0:T(512)(128)(4,1)}, u32[]{:S(2)}) copy-start(pred[2]{0:T(512)(128)(4,1)} %get-tuple-element.63) | copy-start | bytes 10
  58.9 0.7 copy-start.10
  71.3 1.9 %copy-start.8 = (bf16[9,256,256]{2,1,0:T(8,128)(2,1)S(1)}, bf16[9,256,256]{2,1,0:T(8,128)(2,1)}, u32[]{:S(2)}) copy-start(bf16[9,256,256]{2,1,0:T(8,128)(2,1)} %param.13) | copy-start | bytes 3538948
  75.6 1.6 copy-start.2
  75.6 1.9 %copy-start.5 = (bf16[2,32,32,256]{3,2,1,0:T(8,128)(2,1)S(1)}, bf16[2,32,32,256]{3,2,1,0:T(8,128)(2,1)}, u32[]{:S(2)}) copy-start(bf16[2,32,32,256]{3,2,1,0:T(8,128)(2,1)} %param.12) | copy-start | bytes 3145732
Sparse Core Ops, SparseCore 0:
  56.1 98.2 all-reduce.1
where the time goes:
time: 164 us
  waiting for transfers between devices  77.4 us (47%)
  matrix products  22.8 us (14%)
  local copies, waits for them, and re-layouts  22.3 us (14%)
  other arithmetic  20.3 us (12%)
  between operations  14.7 us (9%)
  starting transfers between devices  6.33 us (4%)
    psum x1, waiting for transfers between devices, shards(): summed = lax.psum(jnp.concatenate(pieces, axis=1) * scale_factor, 'tiles')  74.5 us
    dot_general x18, matrix products, conv_taps(): jnp.einsum(form, shifted_window, weight[tap_index], preferred_element_typ...  18 us
    gather x16, local copies, waits for them, and re-layouts, select_tiles(): chosen = jnp.take(source_pool, local_ids, axis=0)  11.2 us
    ppermute x4, starting transfers between devices, from_behind(): return lax.ppermute(value, axis, pairs)  6.29 us
    mul x16, other arithmetic, select_tiles(): return chosen * present[:, None, None, None].astype(source_pool.dtype)  6.17 us
    unnamed x67, local copies, waits for them, and re-layouts  4.89 us
    dot_general x9, matrix products, shards(): jnp.einsum('sabo,sabc->oc', hidden_gradient, shifted_window, preferred_el...  4.8 us
    concatenate x2, other arithmetic, pad_tiles(): return jnp.concatenate([upper_band, middle, lower_band], axis=1)  3.77 us
  transfers between devices with their start and end apart: 5, of which 3 were waited for; matrix products, arithmetic and copies ran while one was open for 17% of the time, Pallas kernels for 0%

commit v1 on v0

v1 whole, which is shorter than its diff:
```python
import functools
import math

import jax
import jax.numpy as jnp
from jax import lax
from jax.experimental import pallas as pl
from jax.experimental.pallas import tpu as pltpu
from jax.sharding import PartitionSpec as P

STEP = 2
BF16 = jnp.bfloat16
F32 = jnp.float32
GELU_SCALE = math.sqrt(2.0 / math.pi)
GELU_CUBIC = 0.044715
VMEM_BYTES = 16 << 20

SMEM = pl.BlockSpec(memory_space=pltpu.SMEM)
VMEM = pl.BlockSpec(memory_space=pltpu.VMEM)


def gelu_pair(h):
    h2 = h * h
    t = jnp.tanh(h * (GELU_SCALE + (GELU_SCALE * GELU_CUBIC) * h2))
    half_up = 0.5 + 0.5 * t
    activated = h * half_up
    derivative = half_up + h * (0.5 - 0.5 * t * t) * (
        GELU_SCALE + (3.0 * GELU_CUBIC * GELU_SCALE) * h2
    )
    return activated, derivative


def present_bf16(entry):
    return jnp.where(entry >= 0, 1.0, 0.0).astype(BF16)


def column_masks(mask):
    turned = mask.astype(F32).T
    side = turned.shape[0]
    return [
        jnp.broadcast_to(turned[:, r : r + 1], (side, 256)).astype(BF16)
        for r in range(turned.shape[1])
    ]


def edge_selector(rows, cols, picked):
    shape = (len(picked) * rows, rows * cols)
    out = lax.broadcasted_iota(jnp.int32, shape, 0)
    src = lax.broadcasted_iota(jnp.int32, shape, 1)
    want_row = out % rows
    want_col = picked[0] + out // rows
    return jnp.where(src == want_row * cols + want_col, 1.0, 0.0).astype(BF16)


def dot(a, b):
    return jnp.dot(a, b, preferred_element_type=F32)


def interior_kernel(
    local_ref, x_ref, cot_ref, w_ref, mask_ref,
    out_ref, grad_ref, dw_ref, xe_ref, cote_ref,
    xc, mk, gt,
):
    slots, rows, cols, ch = x_ref.shape
    zeros = jnp.zeros((rows, STEP, ch), BF16)
    half = cols // 2
    for s in range(slots):
        for r, line in enumerate(column_masks(mask_ref[s])):
            mk[s, r] = line
        xm = x_ref[s] * mk[s]
        xc[s, STEP : rows + STEP, :, ch : 2 * ch] = xm
        xc[s, STEP : rows + STEP, :, 0:ch] = jnp.concatenate(
            [zeros, xm[:, : cols - STEP]], axis=1
        )
        xc[s, STEP : rows + STEP, :, 2 * ch :] = jnp.concatenate([xm[:, STEP:], zeros], axis=1)
    for s in range(slots):
        north, south = local_ref[s, 0], local_ref[s, 1]
        xc[s, 0:STEP] = xc[jnp.maximum(north, 0), rows : rows + STEP] * present_bf16(north)
        xc[s, rows + STEP :] = xc[jnp.maximum(south, 0), STEP : 2 * STEP] * present_bf16(south)

    block = 8
    column = lax.broadcasted_iota(jnp.int32, (block, cols, ch), 1)
    inside = jnp.where((column >= STEP) & (column < cols - STEP), 1.0, 0.0).astype(BF16)
    for s in range(slots):
        for r0 in range(0, rows, block):
            acc = None
            for a in range(3):
                window = xc[s, r0 + STEP * a : r0 + STEP * a + block].reshape(block * cols, 3 * ch)
                term = dot(window, w_ref[a])
                acc = term if acc is None else acc + term
            activated, derivative = gelu_pair(acc)
            ocean = mk[s, r0 : r0 + block]
            xm = xc[s, r0 + STEP : r0 + STEP + block, :, ch : 2 * ch].reshape(block * cols, ch)
            out = (xm.astype(F32) + activated).astype(BF16).reshape(block, cols, ch)
            out_ref[s, r0 : r0 + block] = out * ocean
            cot = (cot_ref[s, r0 : r0 + block] * ocean) * inside
            g = (cot.reshape(block * cols, ch).astype(F32) * derivative).astype(BF16)
            grad_ref[s, r0 : r0 + block] = g.reshape(block, cols, ch)
            gt[s, :, r0 * cols : (r0 + block) * cols] = g.T

    for a in range(3):
        total = None
        for s in range(slots):
            window = xc[s, STEP * a : STEP * a + rows].reshape(rows * cols, 3 * ch)
            term = dot(gt[s], window)
            total = term if total is None else total + term
        dw_ref[:, a * 3 * ch : (a + 1) * 3 * ch] = total

    for s in range(slots):
        for side, picked in ((0, range(0, 4)), (1, range(half - 4, half))):
            lo = side * half
            xm = xc[s, STEP : rows + STEP, lo : lo + half, ch : 2 * ch].reshape(rows * half, ch)
            sel = edge_selector(rows, half, list(picked))
            xe_ref[s, side * 4 : side * 4 + 4] = (
                dot(sel, xm).astype(BF16).reshape(4, rows, ch)
            )
            cot = (cot_ref[s, :, lo : lo + half] * mk[s, :, lo : lo + half]).reshape(
                rows * half, ch
            )
            outer = sel[: 2 * rows] if side == 0 else sel[2 * rows :]
            cote_ref[side, s] = dot(outer, cot).astype(BF16).reshape(2, rows, ch)


def stack_rows(own, north, south, entry_n, entry_s):
    rows = own.shape[1]
    above = north[:, rows - STEP :] * present_bf16(entry_n)
    below = south[:, :STEP] * present_bf16(entry_s)
    return jnp.concatenate([above, own, below], axis=1)


def edge_kernel(
    local_ref, fw_ref, fe_ref, xe_ref, cote_ref, w_ref, dwi_ref,
    ge_ref, oe_ref, dw_ref,
    win, gt,
):
    slots, _, rows, ch = xe_ref.shape
    for s in range(slots):
        for side in range(2):
            for b in range(3):
                halo = (side == 0 and b == 0) or (side == 1 and b == 2)
                if halo:
                    src = fw_ref if side == 0 else fe_ref
                    mid, top, low = (2, 4, 6) if side == 0 else (3, 5, 7)
                    e_mid, e_top, e_low = local_ref[s, mid], local_ref[s, top], local_ref[s, low]
                    own = src[jnp.maximum(e_mid, 0)] * present_bf16(e_mid)
                    north = src[jnp.maximum(e_top, 0)]
                    south = src[jnp.maximum(e_low, 0)]
                else:
                    first = 2 * (b - 1) if side == 0 else 4 + 2 * b
                    e_top, e_low = local_ref[s, 0], local_ref[s, 1]
                    own = xe_ref[s, first : first + 2]
                    north = xe_ref[jnp.maximum(e_top, 0), first : first + 2]
                    south = xe_ref[jnp.maximum(e_low, 0), first : first + 2]
                tall = stack_rows(own, north, south, e_top, e_low)
                for a in range(3):
                    win[a, side, s, :, :, b * ch : (b + 1) * ch] = tall[
                        :, STEP * a : STEP * a + rows
                    ]
    cells = 2 * slots * 2 * rows
    acc = None
    for a in range(3):
        term = dot(win[a].reshape(cells, 3 * ch), w_ref[a])
        acc = term if acc is None else acc + term
    activated, derivative = gelu_pair(acc)
    x_own = win[1, :, :, :, :, ch : 2 * ch].reshape(cells, ch)
    oe_ref[...] = (x_own.astype(F32) + activated).astype(BF16).reshape(oe_ref.shape)
    g = (cote_ref[...].reshape(cells, ch).astype(F32) * derivative).astype(BF16)
    ge_ref[...] = g.reshape(ge_ref.shape)
    gt[...] = g.T
    for a in range(3):
        span = slice(a * 3 * ch, (a + 1) * 3 * ch)
        dw_ref[:, span] = dwi_ref[:, span] + dot(gt[...], win[a].reshape(cells, 3 * ch))


def spread_selector(rows, cols, first):
    shape = (rows * cols, 2 * rows)
    out = lax.broadcasted_iota(jnp.int32, shape, 0)
    src = lax.broadcasted_iota(jnp.int32, shape, 1)
    want = (out % cols - first) * rows + out // cols
    return jnp.where((src == want) & (out % cols >= first) & (out % cols < first + 2), 1.0, 0.0).astype(BF16)


def input_grad_kernel(
    local_ref, gi_ref, oi_ref, ge_ref, oe_ref, hw_ref, he_ref, cot_ref, w_ref, mask_ref,
    out_ref, ig_ref,
    gc, mk, hs,
):
    slots, rows, cols, ch = gi_ref.shape
    half = cols // 2
    zeros = jnp.zeros((rows, STEP, ch), BF16)
    low = spread_selector(rows, half, 0)
    high = spread_selector(rows, half, half - 2)

    def spread(sel, edge):
        return dot(sel, edge.reshape(2 * rows, ch)).astype(BF16).reshape(rows, half, ch)

    column = lax.broadcasted_iota(jnp.int32, (rows, half, ch), 1)
    for s in range(slots):
        for r, line in enumerate(column_masks(mask_ref[s])):
            mk[s, r] = line
        out_low = jnp.where(column < STEP, spread(low, oe_ref[0, s]), oi_ref[s, :, :half])
        out_ref[s, :, :half] = out_low * mk[s, :, :half]
        out_high = jnp.where(
            column >= half - STEP, spread(high, oe_ref[1, s]), oi_ref[s, :, half:]
        )
        out_ref[s, :, half:] = out_high * mk[s, :, half:]
        g = jnp.concatenate(
            [
                gi_ref[s, :, :half] + spread(low, ge_ref[0, s]),
                gi_ref[s, :, half:] + spread(high, ge_ref[1, s]),
            ],
            axis=1,
        )
        gc[s, STEP : rows + STEP, :, ch : 2 * ch] = g
        gc[s, STEP : rows + STEP, :, 2 * ch :] = jnp.concatenate(
            [zeros, g[:, : cols - STEP]], axis=1
        )
        gc[s, STEP : rows + STEP, :, 0:ch] = jnp.concatenate([g[:, STEP:], zeros], axis=1)
        hs[0, s] = spread(low, hw_ref[s])
        hs[1, s] = spread(high, he_ref[s])
    for s in range(slots):
        north, south = local_ref[s, 0], local_ref[s, 1]
        gc[s, 0:STEP] = gc[jnp.maximum(north, 0), rows : rows + STEP] * present_bf16(north)
        gc[s, rows + STEP :] = gc[jnp.maximum(south, 0), STEP : 2 * STEP] * present_bf16(south)
    for s in range(slots):
        for side, (mid, top, low_entry), lanes, lo in (
            (0, (2, 4, 6), 2 * ch, 0),
            (1, (3, 5, 7), 0, half),
        ):
            def piece(entry, first, count):
                entry = local_ref[s, entry]
                return hs[side, jnp.maximum(entry, 0), first : first + count] * present_bf16(entry)

            halo = jnp.concatenate(
                [piece(top, rows - STEP, STEP), piece(mid, 0, rows), piece(low_entry, 0, STEP)],
                axis=0,
            )
            gc[s, :, lo : lo + half, lanes : lanes + ch] += halo
    block = 8
    for s in range(slots):
        for r0 in range(0, rows, block):
            acc = None
            for a in range(3):
                first = r0 + STEP * (2 - a)
                for b in range(3):
                    window = gc[s, first : first + block, :, b * ch : (b + 1) * ch].reshape(
                        block * cols, ch
                    )
                    term = lax.dot_general(
                        window,
                        w_ref[a, b * ch : (b + 1) * ch],
                        (((1,), (1,)), ((), ())),
                        preferred_element_type=F32,
                    )
                    acc = term if acc is None else acc + term
            cot = cot_ref[s, r0 : r0 + block].reshape(block * cols, ch).astype(F32)
            ig = (cot + acc).astype(BF16).reshape(block, cols, ch)
            ig_ref[s, r0 : r0 + block] = ig * mk[s, r0 : r0 + block]


def permute(value, pairs_of):
    count = lax.axis_size("tiles")
    return lax.ppermute(value, "tiles", [(i, pairs_of(i, count)) for i in range(count)])


def stage_sizes(count):
    rest = count // 2
    middle = 1
    while middle * middle * 4 <= rest:
        middle *= 2
    return rest // middle, middle, 2


def exchange_sum(total, axis, position, size, stride):
    acc = lax.dynamic_index_in_dim(total, position, axis, False)
    parts = []
    for k in range(1, size):
        other = lax.dynamic_index_in_dim(total, position ^ k, axis, False).astype(BF16)
        parts.append(permute(other, lambda i, n: i ^ (k * stride)))
    for part in parts:
        acc = acc + part.astype(F32)
    return acc


def scatter_sum(dw, device):
    count = lax.axis_size("tiles")
    outer, middle, core = stage_sizes(count)
    own_rows = dw.shape[0] // count
    total = dw.reshape(outer, middle, core, own_rows, dw.shape[1])
    c, y, z = device % core, device // core % middle, device // (core * middle)
    total = exchange_sum(total, 2, c, core, 1)
    total = exchange_sum(total, 1, y, middle, core)
    return exchange_sum(total, 0, z, outer, core * middle)


def turned_edge(field, mask, first):
    edge = field[:, :, first : first + STEP] * mask[:, :, first : first + STEP, None].astype(BF16)
    return edge.transpose(0, 2, 1, 3)


def shards(input_field, cotangent, weight, neighbours, land_mask):
    device = lax.axis_index("tiles")
    count = lax.axis_size("tiles")
    slots, rows, cols, ch = input_field.shape
    taps = weight.reshape(3, 3 * ch, ch)
    bases = jnp.stack(
        [device, device, (device - 1) % count, (device + 1) % count] + [(device - 1) % count, (device + 1) % count] * 2
    ) * slots
    local = jnp.where(neighbours >= 0, jnp.clip(neighbours - bases[None, :], 0, slots - 1), -1)
    params = pltpu.CompilerParams(vmem_limit_bytes=VMEM_BYTES)

    east_edge = turned_edge(input_field, land_mask, cols - STEP)
    west_edge = turned_edge(input_field, land_mask, 0)
    from_west = permute(east_edge, lambda i, n: (i + 1) % n)
    from_east = permute(west_edge, lambda i, n: (i - 1) % n)

    edge = (2, slots, STEP, rows, ch)
    out_inner, grad_inner, dw_inner, x_edge, cot_edge = pl.pallas_call(
        interior_kernel,
        out_shape=(
            jax.ShapeDtypeStruct(input_field.shape, BF16),
            jax.ShapeDtypeStruct(input_field.shape, BF16),
            jax.ShapeDtypeStruct((ch, 9 * ch), F32),
            jax.ShapeDtypeStruct((slots, 8, rows, ch), BF16),
            jax.ShapeDtypeStruct(edge, BF16),
        ),
        in_specs=[SMEM, VMEM, VMEM, VMEM, VMEM],
        out_specs=(VMEM,) * 5,
        scratch_shapes=[
            pltpu.VMEM((slots, rows + 2 * STEP, cols, 3 * ch), BF16),
            pltpu.VMEM((slots, rows, cols, ch), BF16),
            pltpu.VMEM((slots, ch, rows * cols), BF16),
        ],
        compiler_params=params,
        cost_estimate=pl.CostEstimate(
            flops=4 * 9 * slots * rows * cols * ch * ch, bytes_accessed=8 << 20, transcendentals=0
        ),
        name="interior",
    )(local, input_field, cotangent, taps, land_mask)

    grad_edge, out_edge, dw = pl.pallas_call(
        edge_kernel,
        out_shape=(
            jax.ShapeDtypeStruct(edge, BF16),
            jax.ShapeDtypeStruct(edge, BF16),
            jax.ShapeDtypeStruct((ch, 9 * ch), F32),
        ),
        in_specs=[SMEM] + [VMEM] * 6,
        out_specs=(VMEM,) * 3,
        scratch_shapes=[
            pltpu.VMEM((3, 2, slots, STEP, rows, 3 * ch), BF16),
            pltpu.VMEM((ch, 4 * slots * rows), BF16),
        ],
        compiler_params=params,
        cost_estimate=pl.CostEstimate(
            flops=4 * 9 * slots * rows * 4 * ch * ch, bytes_accessed=6 << 20, transcendentals=0
        ),
        name="edges",
    )(local, from_west, from_east, x_edge, cot_edge, taps, dw_inner)

    grad_west = permute(grad_edge[1], lambda i, n: (i + 1) % n)
    grad_east = permute(grad_edge[0], lambda i, n: (i - 1) % n)
    summed = scatter_sum(dw, device)

    layer_output, input_grad = pl.pallas_call(
        input_grad_kernel,
        out_shape=(
            jax.ShapeDtypeStruct(input_field.shape, BF16),
            jax.ShapeDtypeStruct(input_field.shape, BF16),
        ),
        in_specs=[SMEM] + [VMEM] * 9,
        out_specs=(VMEM,) * 2,
        scratch_shapes=[
            pltpu.VMEM((slots, rows + 2 * STEP, cols, 3 * ch), BF16),
            pltpu.VMEM((slots, rows, cols, ch), BF16),
            pltpu.VMEM((2, slots, rows, cols // 2, ch), BF16),
        ],
        compiler_params=params,
        cost_estimate=pl.CostEstimate(
            flops=2 * 9 * slots * rows * cols * ch * ch, bytes_accessed=8 << 20, transcendentals=0
        ),
        name="input_grad",
    )(local, grad_inner, out_inner, grad_edge, out_edge, grad_west, grad_east, cotangent, taps, land_mask)

    scale_factor = 1.0 / (rows * math.sqrt(slots * count))
    return layer_output, input_grad, summed * scale_factor


def solution(mesh):
    return jax.shard_map(
        shards,
        mesh=mesh,
        in_specs=(
            P(("groups", "tiles"), None, None, None),
            P(("groups", "tiles"), None, None, None),
            P(),
            P("tiles", None),
            P("tiles", None, None),
        ),
        out_specs=(
            P(("groups", "tiles"), None, None, None),
            P(("groups", "tiles"), None, None, None),
            P(("groups", "tiles"), None),
        ),
        check_vma=False,
    )
```

time: 164 us -> 60.3 us (0.37)
  waiting for transfers between devices: 77.4 us -> 7.13 us
  matrix products: 22.8 us -> 0 us
  Pallas kernels: 0 us -> 14.8 us
  other arithmetic: 20.3 us -> 6.15 us
  between operations: 14.7 us -> 0.93 us
  starting transfers between devices: 6.33 us -> 14.5 us
  local copies, waits for them, and re-layouts: 22.3 us -> 16.1 us
    psum x1 -> x0, waiting for transfers between devices: 74.5 us -> none  [shards(): summed = lax.psum(jnp.concatenate(pieces, axis=1) * scale_factor, 'tiles')]
    dot_general x27 -> x0, matrix products: 22.8 us -> none  [the longest x18 18 us: conv_taps(): jnp.einsum(form, shifted_window, weight[tap_index], preferred_element_typ...]
    pallas_call x0 -> x3, Pallas kernels: none -> 14.8 us  [the longest x1 7 us: shards(): pl.pallas_call(interior_kernel, out_shape=(jax.ShapeDtypeStruct(input_fie...]
    gather x16 -> x0, local copies, waits for them, and re-layouts: 11.2 us -> none  [select_tiles(): chosen = jnp.take(source_pool, local_ids, axis=0)]
    unnamed x67 -> x42, local copies, waits for them, and re-layouts: 4.89 us -> 14.5 us
    mul x18 -> x2, other arithmetic: 9.37 us -> 0.71 us  [the longest x1 0.71 us: shards(): return (layer_output, input_grad, summed * scale_factor)]
    ppermute x4 -> x9, starting transfers between devices: 6.29 us -> 14.5 us  [permute(): lax.ppermute(value, 'tiles', [(i, pairs_of(i, count)) for i in range(coun...]
    concatenate x3 -> x0, other arithmetic: 4.87 us -> none  [the longest x2 3.77 us: pad_tiles(): return jnp.concatenate([upper_band, middle, lower_band], axis=1)]
  transfers between devices with their start and end apart: 5 -> 9, of which waited for: 3 -> 2; matrix products, arithmetic and copies ran while one was open for 17% -> 5% of each run, Pallas kernels for 0% -> 21%
where the time goes in v1:
time: 60.3 us; the launch traced here: 59.7 us
  local copies, waits for them, and re-layouts  16.1 us (27%)
  Pallas kernels  14.8 us (25%)
  starting transfers between devices  14.5 us (24%)
  waiting for transfers between devices  7.13 us (12%)
  other arithmetic  6.15 us (10%)
  between operations  0.93 us (2%)
    ppermute x9, starting transfers between devices, permute(): lax.ppermute(value, 'tiles', [(i, pairs_of(i, count)) for i in range(coun...  14.5 us
    unnamed x42, local copies, waits for them, and re-layouts  14.5 us
    ppermute x9, waiting for transfers between devices, permute(): lax.ppermute(value, 'tiles', [(i, pairs_of(i, count)) for i in range(coun...  7.13 us
    pallas_call x1, Pallas kernels, shards(): pl.pallas_call(interior_kernel, out_shape=(jax.ShapeDtypeStruct(input_fie...  7 us
    pallas_call x1, Pallas kernels, shards(): pl.pallas_call(input_grad_kernel, out_shape=(jax.ShapeDtypeStruct(input_f...  5.29 us
    add x2, other arithmetic, exchange_sum(): acc = acc + part.astype(F32)  2.53 us
    pallas_call x1, Pallas kernels, shards(): pl.pallas_call(edge_kernel, out_shape=(jax.ShapeDtypeStruct(edge, BF16),...  2.52 us
    transpose x2, other arithmetic, turned_edge(): return edge.transpose(0, 2, 1, 3)  1.45 us
  transfers between devices with their start and end apart: 9, of which 2 were waited for; matrix products, arithmetic and copies ran while one was open for 5% of the time, Pallas kernels for 21%

profile of v1, /device:TPU:0, one launch (start us, length us, event | category | flops | bytes accessed | tf_op | source)
XLA Modules:
  0.0 59.7 jit_solution(11205347985987034614)
XLA Ops:
  0.6 1.1 %fusion.10 = (bf16[2,32,2,256]{3,2,1,0:T(2,128)(2,1)S(1)}, bf16[2,32,2,256]{3,2,1,0:T(2,128)(2,1)S(1)}) fusion(bf16[2,32,32,256]{3,2,1,0:T(8,128)(2,1)} %x_ref.1), kind=kLoop, calls=%fused_computation.26 | loop fusion | bytes 262144 | tf_op jit(solution)/shard_map/slice | solution.py:297
  1.8 0.8 %convert.4 = bf16[2,32,32]{2,1,0:T(8,128)(2,1)S(1)} convert(s32[2,32,32]{2,1,0:T(8,128)} %mask_ref.3) | non-fusion elementwise | flops 2048 | bytes 12288 | tf_op jit(solution)/shard_map/convert.1
  2.5 0.1 fusion.11
  2.6 0.1 copy.9
  2.7 0.7 %fusion.9 = bf16[2,2,32,256]{3,2,1,0:T(8,128)(2,1)} fusion(bf16[2,32,2,256]{3,2,1,0:T(2,128)(2,1)S(1)} %get-tuple-element.24, bf16[2,32,2]{1,2,0:T(2,128)(2,1)S(1)} %copy.9), kind=kLoop, calls=%fused_computation.19 | loop fusion | flops 32768 | bytes 131328 | tf_op jit(solution)/shard_map/transpose | solution.py:298
  3.4 0.5 collective-permute-start
  3.9 0.1 copy.11
  4.0 0.7 %fusion.8 = bf16[2,2,32,256]{3,2,1,0:T(8,128)(2,1)} fusion(bf16[2,32,2,256]{3,2,1,0:T(2,128)(2,1)S(1)} %get-tuple-element.23, bf16[2,32,2]{1,2,0:T(2,128)(2,1)S(1)} %copy.11), kind=kLoop, calls=%fused_computation.17 | loop fusion | flops 32768 | bytes 131328 | tf_op jit(solution)/shard_map/transpose | solution.py:298
  4.7 5.0 %collective-permute-start.1 = (bf16[2,2,32,256]{3,2,1,0:T(8,128)(2,1)}, bf16[2,2,32,256]{3,2,1,0:T(8,128)(2,1)}, u32[]{:S(2)}, u32[]{:S(2)}) collective-permute-start(bf16[2,2,32,256]{3,2,1,0:T(8,128)(2,1)} %fusion.8), channel_id=1, source_target_pairs={{0,15},{1,0},{2,1},{3,2},{4,3},{5,4},{6,5},{7,6},{8,7},{9,8},{10,9... | collective-permute-start | bytes 196616 | tf_op jit(solution)/shard_map/ppermute | solution.py:263
  9.7 0.1 stack.20
  9.8 0.7 %compare_select_fusion.local_ref = s32[2,8]{1,0:T(2,128)S(1)} fusion(s32[2,8]{1,0:T(2,128)} %param.8, s32[8]{0:T(128)S(1)} %broadcast_multiply_fusion), kind=kLoop, calls=%fused_computation.24 | loop fusion | flops 64 | bytes 160 | tf_op jit(solution)/shard_map/jit(_where)/select_n | solution.py:309
  10.5 1.3 %copy-done.1 = bf16[9,256,256]{2,1,0:T(8,128)(2,1)S(1)} copy-done((bf16[9,256,256]{2,1,0:T(8,128)(2,1)S(1)}, bf16[9,256,256]{2,1,0:T(8,128)(2,1)}, u32[]{:S(2)}) %copy-start.1) | copy-done | bytes 1179672
  11.8 0.8 %copy-done.9 = s32[2,32,32]{2,1,0:T(8,128)S(1)} copy-done((s32[2,32,32]{2,1,0:T(8,128)S(1)}, s32[2,32,32]{2,1,0:T(8,128)}, u32[]{:S(2)}) %copy-start.9) | copy-done | bytes 8216
  12.5 1.2 %copy-done.11 = bf16[2,32,32,256]{3,2,1,0:T(8,128)(2,1)S(1)} copy-done((bf16[2,32,32,256]{3,2,1,0:T(8,128)(2,1)S(1)}, bf16[2,32,32,256]{3,2,1,0:T(8,128)(2,1)}, u32[]{:S(2)}) %copy-start.11) | copy-done | bytes 1048600
  13.7 1.2 %copy-done.12 = bf16[2,32,32,256]{3,2,1,0:T(8,128)(2,1)S(1)} copy-done((bf16[2,32,32,256]{3,2,1,0:T(8,128)(2,1)S(1)}, bf16[2,32,32,256]{3,2,1,0:T(8,128)(2,1)}, u32[]{:S(2)}) %copy-start.12) | copy-done | bytes 1048600
  15.0 7.0 %interior.1 = (bf16[2,32,32,256]{3,2,1,0:T(8,128)(2,1)S(1)}, bf16[2,32,32,256]{3,2,1,0:T(8,128)(2,1)S(1)}, f32[256,2304]{1,0:T(8,128)S(1)}, bf16[2,8,32,256]{3,2...) custom-call(s32[2,8]{1,0:T(2,128)S(1)} %compare_select_fusion.local_ref, bf16[2,32,32,256]{3,2,1,0:T(8,128)(2,1)S(1)} %copy-done.11, ...), custom_call_target="tpu_custom_call" | custom-call | flops 4831838208 | bytes 8388608 | tf_op jit(solution)/shard_map/interior/pallas_call | solution.py:318
  22.0 0.7 %copy-done.3 = bf16[2,8,32,256]{3,2,1,0:T(8,128)(2,1)} copy-done((bf16[2,8,32,256]{3,2,1,0:T(8,128)(2,1)}, bf16[2,8,32,256]{3,2,1,0:T(8,128)(2,1)S(1)}, u32[]{:S(2)}) %copy-start.3) | copy-done | bytes 262168
  22.7 0.7 %copy-done.5 = bf16[2,2,2,32,256]{4,3,2,1,0:T(8,128)(2,1)} copy-done((bf16[2,2,2,32,256]{4,3,2,1,0:T(8,128)(2,1)}, bf16[2,2,2,32,256]{4,3,2,1,0:T(8,128)(2,1)S(1)}, u32[]{:S(2)}) %copy-start.5) | copy-done | bytes 131096
  23.3 1.0 %copy-done.16 = bf16[2,32,32,256]{3,2,1,0:T(8,128)(2,1)} copy-done((bf16[2,32,32,256]{3,2,1,0:T(8,128)(2,1)}, bf16[2,32,32,256]{3,2,1,0:T(8,128)(2,1)S(1)}, u32[]{:S(2)}) %copy-start.16) | copy-done | bytes 1048600
  24.3 1.0 %copy-done.18 = bf16[2,32,32,256]{3,2,1,0:T(8,128)(2,1)} copy-done((bf16[2,32,32,256]{3,2,1,0:T(8,128)(2,1)}, bf16[2,32,32,256]{3,2,1,0:T(8,128)(2,1)S(1)}, u32[]{:S(2)}) %copy-start.18) | copy-done | bytes 1048600
  25.3 0.0 collective-permute-done.1.fe_ref
  25.3 0.9 %copy-done.4 = bf16[2,8,32,256]{3,2,1,0:T(8,128)(2,1)S(1)} copy-done((bf16[2,8,32,256]{3,2,1,0:T(8,128)(2,1)S(1)}, bf16[2,8,32,256]{3,2,1,0:T(8,128)(2,1)}, u32[]{:S(2)}) %copy-start.4) | copy-done | bytes 262168
  26.2 0.9 %copy-done.6 = bf16[2,2,2,32,256]{4,3,2,1,0:T(8,128)(2,1)S(1)} copy-done((bf16[2,2,2,32,256]{4,3,2,1,0:T(8,128)(2,1)S(1)}, bf16[2,2,2,32,256]{4,3,2,1,0:T(8,128)(2,1)}, u32[]{:S(2)}) %copy-start.6) | copy-done | bytes 131096
  27.1 2.5 %edges.1 = (bf16[2,2,2,32,256]{4,3,2,1,0:T(8,128)(2,1)S(1)}, bf16[2,2,2,32,256]{4,3,2,1,0:T(8,128)(2,1)S(1)}, f32[256,2304]{1,0:T(8,128)S(1)}) custom-call(s32[2,8]{1,0:T(2,128)S(1)} %compare_select_fusion.local_ref, bf16[2,2,32,256]{3,2,1,0:T(8,128)(2,1)} %collective-permute-done.fw_ref, bf16[2,2,32,256]{3,2,1,0:T(8,128)(2,1)} %collective-permute-done.1.fe_ref, ...), custom_call_target="tpu_custom_call" | custom-call | flops 603979776 | bytes 6291456 | tf_op jit(solution)/shard_map/edges/pallas_call | solution.py:341
  29.7 0.0 copy-start.7
  29.7 1.4 %copy-done = f32[256,2304]{1,0:T(8,128)} copy-done((f32[256,2304]{1,0:T(8,128)}, f32[256,2304]{1,0:T(8,128)S(1)}, u32[]{:S(2)}) %copy-start) | copy-done | bytes 2359320
  31.1 0.1 fusion
  31.2 0.1 collective-permute-start.4
  31.3 0.0 copy-start.8
  31.3 1.9 %collective-permute-done.4 = bf16[4,2,16,2304]{3,2,0,1:T(8,128)(2,1)S(1)} collective-permute-done((bf16[4,2,16,2304]{3,2,0,1:T(8,128)(2,1)S(1)}, bf16[4,2,16,2304]{3,2,0,1:T(8,128)(2,1)S(1)}, u32[]{:S(2)}, u32[]{:S(2)}) %collective-permute-start.4) | collective-permute-done | bytes 589856 | tf_op jit(solution)/shard_map/ppermute | solution.py:263
  33.2 1.4 %bitcast_add_fusion = f32[4,2,16,2304]{3,2,0,1:T(8,128)S(1)} fusion(bf16[4,2,16,2304]{3,2,0,1:T(8,128)(2,1)S(1)} %collective-permute-done.4, f32[4,2,2,16,2304]{4,3,2,1,0:T(8,128)} %bitcast.36, s32[]{:T(128)S(6)} %select_n.65), kind=kLoop, calls=%fused_computation.1 | loop fusion | flops 589824 | bytes 2949124 | tf_op jit(solution)/shard_map/add | solution.py:281
  34.7 1.0 %copy-done.20 = f32[4,2,16,2304]{3,2,0,1:T(8,128)} copy-done((f32[4,2,16,2304]{3,2,0,1:T(8,128)}, f32[4,2,16,2304]{3,2,0,1:T(8,128)S(1)}, u32[]{:S(2)}) %copy-start.20) | copy-done | bytes 1179672
  35.7 0.0 copy-start.10
  35.7 0.0 copy-start.13
  35.7 0.1 collective-permute-start.5
  35.9 0.2 collective-permute-start.2
  36.1 4.3 %collective-permute-start.3 = (bf16[2,2,32,256]{3,2,1,0:T(8,128)(2,1)S(1)}, bf16[2,2,32,256]{3,2,1,0:T(8,128)(2,1)S(1)}, u32[]{:S(2)}, u32[]{:S(2)}) collective-permute-start(bf16[2,2,32,256]{3,2,1,0:T(8,128)(2,1)S(1)} %get-tuple-element.28), channel_id=1, source_target_pairs={{0,15},{1,0},{2,1},{3,2},{4,3},{5,4},{6,5},{7,6},{8,7},{9,8},{10,9... | collective-permute-start | bytes 196616 | tf_op jit(solution)/shard_map/ppermute | solution.py:263
  40.4 5.2 %collective-permute-done.5 = bf16[4,16,2304]{2,1,0:T(8,128)(2,1)S(1)} collective-permute-done((bf16[4,16,2304]{2,1,0:T(8,128)(2,1)S(1)}, bf16[4,16,2304]{2,1,0:T(8,128)(2,1)S(1)}, u32[]{:S(2)}, u32[]{:S(2)}) %collective-permute-start.5) | collective-permute-done | bytes 294944 | tf_op jit(solution)/shard_map/ppermute | solution.py:263
  45.6 1.1 %bitcast_add_fusion.1 = f32[4,16,2304]{2,1,0:T(8,128)S(1)} fusion(bf16[4,16,2304]{2,1,0:T(8,128)(2,1)S(1)} %collective-permute-done.5, f32[4,2,16,2304]{3,2,0,1:T(8,128)} %copy-done.20, s32[]{:T(128)S(6)} %select_n.69), kind=kLoop, calls=%fused_computation.3 | loop fusion | flops 294912 | bytes 1474564 | tf_op jit(solution)/shard_map/add | solution.py:281
  46.7 2.3 %collective-permute-start.8 = (bf16[16,2304]{1,0:T(8,128)(2,1)S(1)}, bf16[16,2304]{1,0:T(8,128)(2,1)S(1)}, u32[]{:S(2)}, u32[]{:S(2)}) collective-permute-start(bf16[16,2304]{1,0:T(8,128)(2,1)S(1)} %get-tuple-element.26), channel_id=1, source_target_pairs={{0,12},{1,13},{2,14},{3,15},{4,8},{5,9},{6,10},{7,11},{8,4},{9,5},... | collective-permute-start | bytes 221192 | tf_op jit(solution)/shard_map/ppermute | solution.py:263
  49.0 0.0 collective-permute-start.7
  49.0 2.1 %collective-permute-start.6 = (bf16[16,2304]{1,0:T(8,128)(2,1)S(1)}, bf16[16,2304]{1,0:T(8,128)(2,1)S(1)}, u32[]{:S(2)}, u32[]{:S(2)}) collective-permute-start(bf16[16,2304]{1,0:T(8,128)(2,1)S(1)} %get-tuple-element.25), channel_id=1, source_target_pairs={{0,4},{1,5},{2,6},{3,7},{4,0},{5,1},{6,2},{7,3},{8,12},{9,13},{10,... | collective-permute-start | bytes 221192 | tf_op jit(solution)/shard_map/ppermute | solution.py:263
  51.2 0.0 copy-start.17
  51.2 1.2 %copy-done.17 = bf16[2,32,32,256]{3,2,1,0:T(8,128)(2,1)S(1)} copy-done((bf16[2,32,32,256]{3,2,1,0:T(8,128)(2,1)S(1)}, bf16[2,32,32,256]{3,2,1,0:T(8,128)(2,1)}, u32[]{:S(2)}) %copy-start.17) | copy-done | bytes 1048600
  52.4 1.2 %copy-done.19 = bf16[2,32,32,256]{3,2,1,0:T(8,128)(2,1)S(1)} copy-done((bf16[2,32,32,256]{3,2,1,0:T(8,128)(2,1)S(1)}, bf16[2,32,32,256]{3,2,1,0:T(8,128)(2,1)}, u32[]{:S(2)}) %copy-start.19) | copy-done | bytes 1048600
  53.7 5.3 %input_grad.1 = (bf16[2,32,32,256]{3,2,1,0:T(8,128)(2,1)}, bf16[2,32,32,256]{3,2,1,0:T(8,128)(2,1)}) custom-call(s32[2,8]{1,0:T(2,128)S(1)} %compare_select_fusion.local_ref, bf16[2,32,32,256]{3,2,1,0:T(8,128)(2,1)S(1)} %copy-done.19, bf16[2,32,32,256]{3,2,1,0:T(8,128)(2,1)S(1)} %copy-done.17, bf16[2,2,2,32,256]{4,3,2,1,0:T(8,128)(2,1)S(1)} %copy-done.8, ...), custom_call_target="tpu_custom_call" | custom-call | flops 2415919104 | bytes 8388608 | tf_op jit(solution)/shard_map/input_grad/pallas_call | solution.py:365
  59.0 0.0 collective-permute-done.8
  59.0 0.7 %fusion.4 = f32[16,2304]{1,0:T(8,128)} fusion(bf16[16,2304]{1,0:T(8,128)(2,1)S(1)} %collective-permute-done.8, bf16[16,2304]{1,0:T(8,128)(2,1)S(1)} %collective-permute-done.7, bf16[16,2304]{1,0:T(8,128)(2,1)S(1)} %collective-permute-done.6, f32[4,16,2304]{2,1,0:T(8,128)S(1)} %bitcast_add_fusion.1, s32[]{:T(128)S(6)} %select_n.72), kind=kLoop, calls=%fused_computation.9 | loop fusion | flops 258048 | bytes 516100 | tf_op jit(solution)/shard_map/mul | solution.py:386
  (32 shorter events, 0.1 us)
Async XLA Ops:
  3.4 21.8 %collective-permute-start = (bf16[2,2,32,256]{3,2,1,0:T(8,128)(2,1)}, bf16[2,2,32,256]{3,2,1,0:T(8,128)(2,1)}, u32[]{:S(2)}, u32[]{:S(2)}) collective-permute-start(bf16[2,2,32,256]{3,2,1,0:T(8,128)(2,1)} %fusion.9), channel_id=1, source_target_pairs={{0,1},{1,2},{2,3},{3,4},{4,5},{5,6},{6,7},{7,8},{8,9},{9,10},{10,1... | collective-permute-start | bytes 196616 | tf_op jit(solution)/shard_map/ppermute | solution.py:263
  4.7 20.6 %collective-permute-start.1 = (bf16[2,2,32,256]{3,2,1,0:T(8,128)(2,1)}, bf16[2,2,32,256]{3,2,1,0:T(8,128)(2,1)}, u32[]{:S(2)}, u32[]{:S(2)}) collective-permute-start(bf16[2,2,32,256]{3,2,1,0:T(8,128)(2,1)} %fusion.8), channel_id=1, source_target_pairs={{0,15},{1,0},{2,1},{3,2},{4,3},{5,4},{6,5},{7,6},{8,7},{9,8},{10,9... | collective-permute-start | bytes 196616 | tf_op jit(solution)/shard_map/ppermute | solution.py:263
  10.5 1.3 %copy-start.1 = (bf16[9,256,256]{2,1,0:T(8,128)(2,1)S(1)}, bf16[9,256,256]{2,1,0:T(8,128)(2,1)}, u32[]{:S(2)}) copy-start(bf16[9,256,256]{2,1,0:T(8,128)(2,1)} %param.7) | copy-start | bytes 3538948
  11.8 0.8 %copy-start.9 = (s32[2,32,32]{2,1,0:T(8,128)S(1)}, s32[2,32,32]{2,1,0:T(8,128)}, u32[]{:S(2)}) copy-start(s32[2,32,32]{2,1,0:T(8,128)} %mask_ref.3) | copy-start | bytes 24580
  12.5 1.2 %copy-start.11 = (bf16[2,32,32,256]{3,2,1,0:T(8,128)(2,1)S(1)}, bf16[2,32,32,256]{3,2,1,0:T(8,128)(2,1)}, u32[]{:S(2)}) copy-start(bf16[2,32,32,256]{3,2,1,0:T(8,128)(2,1)} %x_ref.1) | copy-start | bytes 3145732
  13.7 1.2 %copy-start.12 = (bf16[2,32,32,256]{3,2,1,0:T(8,128)(2,1)S(1)}, bf16[2,32,32,256]{3,2,1,0:T(8,128)(2,1)}, u32[]{:S(2)}) copy-start(bf16[2,32,32,256]{3,2,1,0:T(8,128)(2,1)} %cot_ref.3) | copy-start | bytes 3145732
  15.0 10.3 %copy-start.2 = (bf16[9,256,256]{2,1,0:T(8,128)(2,1)S(1)}, bf16[9,256,256]{2,1,0:T(8,128)(2,1)}, u32[]{:S(2)}) copy-start(bf16[9,256,256]{2,1,0:T(8,128)(2,1)} %param.7) | copy-start | bytes 3538948
  22.0 0.7 %copy-start.3 = (bf16[2,8,32,256]{3,2,1,0:T(8,128)(2,1)}, bf16[2,8,32,256]{3,2,1,0:T(8,128)(2,1)S(1)}, u32[]{:S(2)}) copy-start(bf16[2,8,32,256]{3,2,1,0:T(8,128)(2,1)S(1)} %get-tuple-element.15.xe_ref) | copy-start | bytes 786436
  22.7 0.7 %copy-start.5 = (bf16[2,2,2,32,256]{4,3,2,1,0:T(8,128)(2,1)}, bf16[2,2,2,32,256]{4,3,2,1,0:T(8,128)(2,1)S(1)}, u32[]{:S(2)}) copy-start(bf16[2,2,2,32,256]{4,3,2,1,0:T(8,128)(2,1)S(1)} %get-tuple-element.16.cote_ref) | copy-start | bytes 393220
  23.3 1.0 %copy-start.16 = (bf16[2,32,32,256]{3,2,1,0:T(8,128)(2,1)}, bf16[2,32,32,256]{3,2,1,0:T(8,128)(2,1)S(1)}, u32[]{:S(2)}) copy-start(bf16[2,32,32,256]{3,2,1,0:T(8,128)(2,1)S(1)} %get-tuple-element.14.oi_ref) | copy-start | bytes 3145732
  24.3 1.0 %copy-start.18 = (bf16[2,32,32,256]{3,2,1,0:T(8,128)(2,1)}, bf16[2,32,32,256]{3,2,1,0:T(8,128)(2,1)S(1)}, u32[]{:S(2)}) copy-start(bf16[2,32,32,256]{3,2,1,0:T(8,128)(2,1)S(1)} %get-tuple-element.13.gi_ref) | copy-start | bytes 3145732
  25.3 1.0 %copy-start.4 = (bf16[2,8,32,256]{3,2,1,0:T(8,128)(2,1)S(1)}, bf16[2,8,32,256]{3,2,1,0:T(8,128)(2,1)}, u32[]{:S(2)}) copy-start(bf16[2,8,32,256]{3,2,1,0:T(8,128)(2,1)} %copy-done.3) | copy-start | bytes 786436
  26.2 0.9 %copy-start.6 = (bf16[2,2,2,32,256]{4,3,2,1,0:T(8,128)(2,1)S(1)}, bf16[2,2,2,32,256]{4,3,2,1,0:T(8,128)(2,1)}, u32[]{:S(2)}) copy-start(bf16[2,2,2,32,256]{4,3,2,1,0:T(8,128)(2,1)} %copy-done.5) | copy-start | bytes 393220
  29.7 1.4 %copy-start = (f32[256,2304]{1,0:T(8,128)}, f32[256,2304]{1,0:T(8,128)S(1)}, u32[]{:S(2)}) copy-start(f32[256,2304]{1,0:T(8,128)S(1)} %get-tuple-element.22) | copy-start | bytes 7077892
  29.7 1.5 %copy-start.7 = (bf16[2,2,2,32,256]{4,3,2,1,0:T(8,128)(2,1)}, bf16[2,2,2,32,256]{4,3,2,1,0:T(8,128)(2,1)S(1)}, u32[]{:S(2)}) copy-start(bf16[2,2,2,32,256]{4,3,2,1,0:T(8,128)(2,1)S(1)} %get-tuple-element.18.ge_ref) | copy-start | bytes 393220
  29.7 1.5 %copy-start.14 = (bf16[2,2,2,32,256]{4,3,2,1,0:T(8,128)(2,1)}, bf16[2,2,2,32,256]{4,3,2,1,0:T(8,128)(2,1)S(1)}, u32[]{:S(2)}) copy-start(bf16[2,2,2,32,256]{4,3,2,1,0:T(8,128)(2,1)S(1)} %get-tuple-element.19.oe_ref) | copy-start | bytes 393220
  31.2 2.1 %collective-permute-start.4 = (bf16[4,2,16,2304]{3,2,0,1:T(8,128)(2,1)S(1)}, bf16[4,2,16,2304]{3,2,0,1:T(8,128)(2,1)S(1)}, u32[]{:S(2)}, u32[]{:S(2)}) collective-permute-start(bf16[4,2,16,2304]{3,2,0,1:T(8,128)(2,1)S(1)} %fusion), channel_id=1, source_target_pairs={{0,1},{1,0},{2,3},{3,2},{4,5},{5,4},{6,7},{7,6},{8,9},{9,8},{10,11... | collective-permute-start | bytes 1769480 | tf_op jit(solution)/shard_map/ppermute | solution.py:263
  31.3 4.6 %copy-start.8 = (bf16[2,2,2,32,256]{4,3,2,1,0:T(8,128)(2,1)S(1)}, bf16[2,2,2,32,256]{4,3,2,1,0:T(8,128)(2,1)}, u32[]{:S(2)}) copy-start(bf16[2,2,2,32,256]{4,3,2,1,0:T(8,128)(2,1)} %copy-done.7) | copy-start | bytes 393220
  34.6 1.0 %copy-start.20 = (f32[4,2,16,2304]{3,2,0,1:T(8,128)}, f32[4,2,16,2304]{3,2,0,1:T(8,128)S(1)}, u32[]{:S(2)}) copy-start(f32[4,2,16,2304]{3,2,0,1:T(8,128)S(1)} %bitcast_add_fusion) | copy-start | bytes 3538948
  35.7 15.5 %copy-start.10 = (s32[2,32,32]{2,1,0:T(8,128)S(1)}, s32[2,32,32]{2,1,0:T(8,128)}, u32[]{:S(2)}) copy-start(s32[2,32,32]{2,1,0:T(8,128)} %mask_ref.3) | copy-start | bytes 24580
  35.7 15.5 %copy-start.13 = (bf16[2,32,32,256]{3,2,1,0:T(8,128)(2,1)S(1)}, bf16[2,32,32,256]{3,2,1,0:T(8,128)(2,1)}, u32[]{:S(2)}) copy-start(bf16[2,32,32,256]{3,2,1,0:T(8,128)(2,1)} %cot_ref.3) | copy-start | bytes 3145732
  35.7 15.5 %copy-start.15 = (bf16[2,2,2,32,256]{4,3,2,1,0:T(8,128)(2,1)S(1)}, bf16[2,2,2,32,256]{4,3,2,1,0:T(8,128)(2,1)}, u32[]{:S(2)}) copy-start(bf16[2,2,2,32,256]{4,3,2,1,0:T(8,128)(2,1)} %copy-done.14) | copy-start | bytes 393220
  35.7 9.8 %collective-permute-start.5 = (bf16[4,16,2304]{2,1,0:T(8,128)(2,1)S(1)}, bf16[4,16,2304]{2,1,0:T(8,128)(2,1)S(1)}, u32[]{:S(2)}, u32[]{:S(2)}) collective-permute-start(bf16[4,16,2304]{2,1,0:T(8,128)(2,1)S(1)} %fusion.1), channel_id=1, source_target_pairs={{0,2},{1,3},{2,0},{3,1},{4,6},{5,7},{6,4},{7,5},{8,10},{9,11},{10,... | collective-permute-start | bytes 884744 | tf_op jit(solution)/shard_map/ppermute | solution.py:263
  35.9 15.3 %collective-permute-start.2 = (bf16[2,2,32,256]{3,2,1,0:T(8,128)(2,1)S(1)}, bf16[2,2,32,256]{3,2,1,0:T(8,128)(2,1)S(1)}, u32[]{:S(2)}, u32[]{:S(2)}) collective-permute-start(bf16[2,2,32,256]{3,2,1,0:T(8,128)(2,1)S(1)} %get-tuple-element.29), channel_id=1, source_target_pairs={{0,1},{1,2},{2,3},{3,4},{4,5},{5,6},{6,7},{7,8},{8,9},{9,10},{10,1... | collective-permute-start | bytes 196616 | tf_op jit(solution)/shard_map/ppermute | solution.py:263
  36.1 15.1 %collective-permute-start.3 = (bf16[2,2,32,256]{3,2,1,0:T(8,128)(2,1)S(1)}, bf16[2,2,32,256]{3,2,1,0:T(8,128)(2,1)S(1)}, u32[]{:S(2)}, u32[]{:S(2)}) collective-permute-start(bf16[2,2,32,256]{3,2,1,0:T(8,128)(2,1)S(1)} %get-tuple-element.28), channel_id=1, source_target_pairs={{0,15},{1,0},{2,1},{3,2},{4,3},{5,4},{6,5},{7,6},{8,7},{9,8},{10,9... | collective-permute-start | bytes 196616 | tf_op jit(solution)/shard_map/ppermute | solution.py:263
  46.7 12.2 %collective-permute-start.8 = (bf16[16,2304]{1,0:T(8,128)(2,1)S(1)}, bf16[16,2304]{1,0:T(8,128)(2,1)S(1)}, u32[]{:S(2)}, u32[]{:S(2)}) collective-permute-start(bf16[16,2304]{1,0:T(8,128)(2,1)S(1)} %get-tuple-element.26), channel_id=1, source_target_pairs={{0,12},{1,13},{2,14},{3,15},{4,8},{5,9},{6,10},{7,11},{8,4},{9,5},... | collective-permute-start | bytes 221192 | tf_op jit(solution)/shard_map/ppermute | solution.py:263
  49.0 9.9 %collective-permute-start.7 = (bf16[16,2304]{1,0:T(8,128)(2,1)S(1)}, bf16[16,2304]{1,0:T(8,128)(2,1)S(1)}, u32[]{:S(2)}, u32[]{:S(2)}) collective-permute-start(bf16[16,2304]{1,0:T(8,128)(2,1)S(1)} %get-tuple-element.27), channel_id=1, source_target_pairs={{0,8},{1,9},{2,10},{3,11},{4,12},{5,13},{6,14},{7,15},{8,0},{9,1},... | collective-permute-start | bytes 221192 | tf_op jit(solution)/shard_map/ppermute | solution.py:263
  49.0 9.9 %collective-permute-start.6 = (bf16[16,2304]{1,0:T(8,128)(2,1)S(1)}, bf16[16,2304]{1,0:T(8,128)(2,1)S(1)}, u32[]{:S(2)}, u32[]{:S(2)}) collective-permute-start(bf16[16,2304]{1,0:T(8,128)(2,1)S(1)} %get-tuple-element.25), channel_id=1, source_target_pairs={{0,4},{1,5},{2,6},{3,7},{4,0},{5,1},{6,2},{7,3},{8,12},{9,13},{10,... | collective-permute-start | bytes 221192 | tf_op jit(solution)/shard_map/ppermute | solution.py:263
  51.2 1.2 %copy-start.17 = (bf16[2,32,32,256]{3,2,1,0:T(8,128)(2,1)S(1)}, bf16[2,32,32,256]{3,2,1,0:T(8,128)(2,1)}, u32[]{:S(2)}) copy-start(bf16[2,32,32,256]{3,2,1,0:T(8,128)(2,1)} %copy-done.16) | copy-start | bytes 3145732
  52.4 1.2 %copy-start.19 = (bf16[2,32,32,256]{3,2,1,0:T(8,128)(2,1)S(1)}, bf16[2,32,32,256]{3,2,1,0:T(8,128)(2,1)}, u32[]{:S(2)}) copy-start(bf16[2,32,32,256]{3,2,1,0:T(8,128)(2,1)} %copy-done.18) | copy-start | bytes 3145732

commit v2 on v1

--- a/solution.py
+++ b/solution.py
@@ -14,9 +14,11 @@
 GELU_SCALE = math.sqrt(2.0 / math.pi)
 GELU_CUBIC = 0.044715
 VMEM_BYTES = 16 << 20
+LOAD_BYTES = 101 << 19
 
 SMEM = pl.BlockSpec(memory_space=pltpu.SMEM)
 VMEM = pl.BlockSpec(memory_space=pltpu.VMEM)
+HBM = pl.BlockSpec(memory_space=pltpu.HBM)
 
 
 def gelu_pair(h):
@@ -56,17 +58,83 @@
     return jnp.dot(a, b, preferred_element_type=F32)
 
 
+def local_id(entry, slots):
+    return jnp.where(entry < 0, -1, lax.rem(entry, slots))
+
+
+def start_all(copies):
+    for copy in copies:
+        copy.start()
+    return copies
+
+
+def is_even():
+    return lax.rem(lax.axis_index("tiles"), 2) == 0
+
+
+def split_sides(west, east, across_ref, pair_ref):
+    even = is_even()
+    across_ref[...] = jnp.where(even, west, east).reshape(across_ref.shape)
+    pair_ref[...] = jnp.where(even, east, west).reshape(pair_ref.shape)
+
+
+def join_sides(across, pair):
+    even = is_even()
+    return jnp.where(even, across, pair), jnp.where(even, pair, across)
+
+
+def load_kernel(
+    x_hbm, cot_hbm, mask_hbm,
+    across_ref, pair_ref, xe_ref, cote_ref, x_ref, cot_ref,
+    ms, sems,
+):
+    slots, rows, cols, ch = x_ref.shape
+    half = cols // 2
+    loads = start_all(
+        [pltpu.make_async_copy(mask_hbm, ms, sems.at[0])]
+        + [
+            pltpu.make_async_copy(src.at[s], dst.at[s], sems.at[1 + i * slots + s])
+            for i, (src, dst) in enumerate(((x_hbm, x_ref), (cot_hbm, cot_ref)))
+            for s in range(slots)
+        ]
+    )
+    sel = [
+        edge_selector(rows, half, list(range(0, 4))),
+        edge_selector(rows, half, list(range(half - 4, half))),
+    ]
+    for copy in loads:
+        copy.wait()
+    for s in range(slots):
+        mask = ms[s].astype(F32)
+        for side in range(2):
+            lo = 0 if side == 0 else cols - 4
+            tiles = slice(side * half, side * half + half)
+            ocean = jnp.stack(
+                [
+                    jnp.broadcast_to(mask[:, lo + k : lo + k + 1], (rows, ch)).astype(BF16)
+                    for k in range(4)
+                ]
+            )
+            x = dot(sel[side], x_ref[s, :, tiles].reshape(rows * half, ch)).astype(BF16)
+            xe_ref[s, side * 4 : side * 4 + 4] = x.reshape(4, rows, ch) * ocean
+            outer = slice(0, 2) if side == 0 else slice(2, 4)
+            pick = sel[side][: 2 * rows] if side == 0 else sel[side][2 * rows :]
+            c = dot(pick, cot_ref[s, :, tiles].reshape(rows * half, ch)).astype(BF16)
+            cote_ref[side, s] = c.reshape(2, rows, ch) * ocean[outer]
+    split_sides(xe_ref[:, 0:2], xe_ref[:, 6:8], across_ref, pair_ref)
+
+
 def interior_kernel(
-    local_ref, x_ref, cot_ref, w_ref, mask_ref,
-    out_ref, grad_ref, dw_ref, xe_ref, cote_ref,
+    own, nbr_ref, x_ref, cot_ref, w_ref, ms,
+    out_ref, grad_ref, dw_ref,
     xc, mk, gt,
 ):
     slots, rows, cols, ch = x_ref.shape
     zeros = jnp.zeros((rows, STEP, ch), BF16)
-    half = cols // 2
-    for s in range(slots):
-        for r, line in enumerate(column_masks(mask_ref[s])):
+    for s in range(slots):
+        for r, line in enumerate(column_masks(ms[s])):
             mk[s, r] = line
+    for s in range(slots):
         xm = x_ref[s] * mk[s]
         xc[s, STEP : rows + STEP, :, ch : 2 * ch] = xm
         xc[s, STEP : rows + STEP, :, 0:ch] = jnp.concatenate(
@@ -74,7 +142,7 @@
         )
         xc[s, STEP : rows + STEP, :, 2 * ch :] = jnp.concatenate([xm[:, STEP:], zeros], axis=1)
     for s in range(slots):
-        north, south = local_ref[s, 0], local_ref[s, 1]
+        north, south = local_id(nbr_ref[s, 0], slots), local_id(nbr_ref[s, 1], slots)
         xc[s, 0:STEP] = xc[jnp.maximum(north, 0), rows : rows + STEP] * present_bf16(north)
         xc[s, rows + STEP :] = xc[jnp.maximum(south, 0), STEP : 2 * STEP] * present_bf16(south)
 
@@ -96,7 +164,7 @@
             cot = (cot_ref[s, r0 : r0 + block] * ocean) * inside
             g = (cot.reshape(block * cols, ch).astype(F32) * derivative).astype(BF16)
             grad_ref[s, r0 : r0 + block] = g.reshape(block, cols, ch)
-            gt[s, :, r0 * cols : (r0 + block) * cols] = g.T
+            turn_rows(gt.at[s], g, r0 * cols, own)
 
     for a in range(3):
         total = None
@@ -104,21 +172,18 @@
             window = xc[s, STEP * a : STEP * a + rows].reshape(rows * cols, 3 * ch)
             term = dot(gt[s], window)
             total = term if total is None else total + term
-        dw_ref[:, a * 3 * ch : (a + 1) * 3 * ch] = total
-
-    for s in range(slots):
-        for side, picked in ((0, range(0, 4)), (1, range(half - 4, half))):
-            lo = side * half
-            xm = xc[s, STEP : rows + STEP, lo : lo + half, ch : 2 * ch].reshape(rows * half, ch)
-            sel = edge_selector(rows, half, list(picked))
-            xe_ref[s, side * 4 : side * 4 + 4] = (
-                dot(sel, xm).astype(BF16).reshape(4, rows, ch)
-            )
-            cot = (cot_ref[s, :, lo : lo + half] * mk[s, :, lo : lo + half]).reshape(
-                rows * half, ch
-            )
-            outer = sel[: 2 * rows] if side == 0 else sel[2 * rows :]
-            cote_ref[side, s] = dot(outer, cot).astype(BF16).reshape(2, rows, ch)
+        dw_ref[:, :, a * 3 * ch : (a + 1) * 3 * ch] = total.reshape(dw_ref.shape[0], -1, 3 * ch)
+
+
+def turn_rows(gt, g, first, own):
+    turned = g.T
+    ch, cells = turned.shape
+    if own is None:
+        gt[:, first : first + cells] = turned
+        return
+    for j in range(ch // own):
+        to = (j % 2) * (ch // 2) + (j // 2) * own
+        gt[to : to + own, first : first + cells] = turned[j * own : (j + 1) * own]
 
 
 def stack_rows(own, north, south, entry_n, entry_s):
@@ -129,29 +194,35 @@
 
 
 def edge_kernel(
-    local_ref, fw_ref, fe_ref, xe_ref, cote_ref, w_ref, dwi_ref,
-    ge_ref, oe_ref, dw_ref,
-    win, gt,
+    own, nbr_ref, across_ref, pair_ref, xe_ref, cote_ref, w_ref, dwi_ref,
+    gacross_ref, gpair_ref, ge_ref, oe_ref, *outs,
 ):
+    *dw_refs, sides, win, gt = outs
     slots, _, rows, ch = xe_ref.shape
+    device = lax.axis_index("tiles")
+    sides[0], sides[1] = join_sides(across_ref[...], pair_ref[...])
+
+    def local(s, column):
+        return local_id(nbr_ref[s, column], slots)
+
     for s in range(slots):
         for side in range(2):
             for b in range(3):
                 halo = (side == 0 and b == 0) or (side == 1 and b == 2)
                 if halo:
-                    src = fw_ref if side == 0 else fe_ref
+                    src = sides.at[side]
                     mid, top, low = (2, 4, 6) if side == 0 else (3, 5, 7)
-                    e_mid, e_top, e_low = local_ref[s, mid], local_ref[s, top], local_ref[s, low]
-                    own = src[jnp.maximum(e_mid, 0)] * present_bf16(e_mid)
+                    e_mid, e_top, e_low = local(s, mid), local(s, top), local(s, low)
+                    middle = src[jnp.maximum(e_mid, 0)] * present_bf16(e_mid)
                     north = src[jnp.maximum(e_top, 0)]
                     south = src[jnp.maximum(e_low, 0)]
                 else:
-                    first = 2 * (b - 1) if side == 0 else 4 + 2 * b
-                    e_top, e_low = local_ref[s, 0], local_ref[s, 1]
-                    own = xe_ref[s, first : first + 2]
-                    north = xe_ref[jnp.maximum(e_top, 0), first : first + 2]
-                    south = xe_ref[jnp.maximum(e_low, 0), first : first + 2]
-                tall = stack_rows(own, north, south, e_top, e_low)
+                    at = 2 * (b - 1) if side == 0 else 4 + 2 * b
+                    e_top, e_low = local(s, 0), local(s, 1)
+                    middle = xe_ref[s, at : at + 2]
+                    north = xe_ref[jnp.maximum(e_top, 0), at : at + 2]
+                    south = xe_ref[jnp.maximum(e_low, 0), at : at + 2]
+                tall = stack_rows(middle, north, south, e_top, e_low)
                 for a in range(3):
                     win[a, side, s, :, :, b * ch : (b + 1) * ch] = tall[
                         :, STEP * a : STEP * a + rows
@@ -166,10 +237,25 @@
     oe_ref[...] = (x_own.astype(F32) + activated).astype(BF16).reshape(oe_ref.shape)
     g = (cote_ref[...].reshape(cells, ch).astype(F32) * derivative).astype(BF16)
     ge_ref[...] = g.reshape(ge_ref.shape)
-    gt[...] = g.T
+    split_sides(g[: cells // 2], g[cells // 2 :], gacross_ref, gpair_ref)
+    turn_rows(gt, g, 0, own)
+    if own is None:
+        (dw_ref,) = dw_refs
+        for a in range(3):
+            span = slice(a * 3 * ch, (a + 1) * 3 * ch)
+            dw_ref[:, span] = dwi_ref[0, :, span] + dot(gt[...], win[a].reshape(cells, 3 * ch))
+        return
+    keep_ref, send_ref = dw_refs
+    core = lax.rem(device, 2)
+    rank = ch // 2
+    keep_rows = gt[pl.ds(pl.multiple_of(core * rank, rank), rank), :]
+    send_rows = gt[pl.ds(pl.multiple_of((1 - core) * rank, rank), rank), :]
+    turned = jnp.concatenate([keep_rows, send_rows], axis=0)
     for a in range(3):
         span = slice(a * 3 * ch, (a + 1) * 3 * ch)
-        dw_ref[:, span] = dwi_ref[:, span] + dot(gt[...], win[a].reshape(cells, 3 * ch))
+        term = dot(turned, win[a].reshape(cells, 3 * ch))
+        keep_ref[:, span] = dwi_ref[core, :, span] + term[:rank]
+        send_ref[:, span] = (dwi_ref[1 - core, :, span] + term[rank:]).astype(BF16)
 
 
 def spread_selector(rows, cols, first):
@@ -181,15 +267,16 @@
 
 
 def input_grad_kernel(
-    local_ref, gi_ref, oi_ref, ge_ref, oe_ref, hw_ref, he_ref, cot_ref, w_ref, mask_ref,
-    out_ref, ig_ref,
-    gc, mk, hs,
+    nbr_ref, gi_ref, oi_ref, ge_ref, oe_ref, across_ref, pair_ref, cot_ref, w_ref, mask_ref,
+    out_hbm, ig_hbm,
+    out_ref, ig_ref, gc, mk, hs, sems,
 ):
     slots, rows, cols, ch = gi_ref.shape
     half = cols // 2
     zeros = jnp.zeros((rows, STEP, ch), BF16)
     low = spread_selector(rows, half, 0)
     high = spread_selector(rows, half, half - 2)
+    halos = join_sides(across_ref[...], pair_ref[...])
 
     def spread(sel, edge):
         return dot(sel, edge.reshape(2 * rows, ch)).astype(BF16).reshape(rows, half, ch)
@@ -216,10 +303,13 @@
             [zeros, g[:, : cols - STEP]], axis=1
         )
         gc[s, STEP : rows + STEP, :, 0:ch] = jnp.concatenate([g[:, STEP:], zeros], axis=1)
-        hs[0, s] = spread(low, hw_ref[s])
-        hs[1, s] = spread(high, he_ref[s])
-    for s in range(slots):
-        north, south = local_ref[s, 0], local_ref[s, 1]
+        hs[0, s] = spread(low, halos[0][s])
+        hs[1, s] = spread(high, halos[1][s])
+    stores = start_all(
+        [pltpu.make_async_copy(out_ref.at[s], out_hbm.at[s], sems.at[s]) for s in range(slots)]
+    )
+    for s in range(slots):
+        north, south = local_id(nbr_ref[s, 0], slots), local_id(nbr_ref[s, 1], slots)
         gc[s, 0:STEP] = gc[jnp.maximum(north, 0), rows : rows + STEP] * present_bf16(north)
         gc[s, rows + STEP :] = gc[jnp.maximum(south, 0), STEP : 2 * STEP] * present_bf16(south)
     for s in range(slots):
@@ -228,7 +318,7 @@
             (1, (3, 5, 7), 0, half),
         ):
             def piece(entry, first, count):
-                entry = local_ref[s, entry]
+                entry = local_id(nbr_ref[s, entry], slots)
                 return hs[side, jnp.maximum(entry, 0), first : first + count] * present_bf16(entry)
 
             halo = jnp.concatenate(
@@ -256,11 +346,21 @@
             cot = cot_ref[s, r0 : r0 + block].reshape(block * cols, ch).astype(F32)
             ig = (cot + acc).astype(BF16).reshape(block, cols, ch)
             ig_ref[s, r0 : r0 + block] = ig * mk[s, r0 : r0 + block]
+        stores += start_all(
+            [pltpu.make_async_copy(ig_ref.at[s], ig_hbm.at[s], sems.at[slots + s])]
+        )
+    for copy in stores:
+        copy.wait()
 
 
 def permute(value, pairs_of):
     count = lax.axis_size("tiles")
     return lax.ppermute(value, "tiles", [(i, pairs_of(i, count)) for i in range(count)])
+
+
+def swap_halos(across, pair):
+    across = permute(across, lambda i, n: (i - 1 if i % 2 == 0 else i + 1) % n)
+    return across, permute(pair, lambda i, n: i ^ 1)
 
 
 def stage_sizes(count):
@@ -293,9 +393,47 @@
     return exchange_sum(total, 0, z, outer, core * middle)
 
 
-def turned_edge(field, mask, first):
-    edge = field[:, :, first : first + STEP] * mask[:, :, first : first + STEP, None].astype(BF16)
-    return edge.transpose(0, 2, 1, 3)
+def split_kernel(stride, keep_ref, *refs):
+    size = keep_ref.shape[1]
+    count = len(refs) - size
+    recvs, keep_out, sends = refs[:count], refs[count], refs[count + 1 :]
+    place = lax.rem(lax.axis_index("tiles") // stride, size)
+    for i in range(keep_ref.shape[0]):
+        for k in range(size):
+            acc = keep_ref[i, place ^ k]
+            for recv in recvs:
+                acc = acc + recv[i, place ^ k].astype(F32)
+            if k == 0:
+                keep_out[i] = acc
+            else:
+                sends[k - 1][i] = acc.astype(BF16)
+
+
+def last_kernel(scale, keep_ref, *refs):
+    *recvs, out_ref = refs
+    acc = keep_ref[...]
+    for recv in recvs:
+        acc = acc + recv[...].astype(F32)
+    out_ref[...] = acc * scale
+
+
+def small_call(kernel, out_shapes, name, *args):
+    return pl.pallas_call(
+        kernel,
+        out_shape=out_shapes,
+        in_specs=[VMEM] * len(args),
+        out_specs=tuple(VMEM for _ in out_shapes),
+        compiler_params=pltpu.CompilerParams(vmem_limit_bytes=8 << 20),
+        name=name,
+    )(*args)
+
+
+def shape_f32(*dims):
+    return jax.ShapeDtypeStruct(dims, F32)
+
+
+def shape_bf16(*dims):
+    return jax.ShapeDtypeStruct(dims, BF16)
 
 
 def shards(input_field, cotangent, weight, neighbours, land_mask):
@@ -303,32 +441,46 @@
     count = lax.axis_size("tiles")
     slots, rows, cols, ch = input_field.shape
     taps = weight.reshape(3, 3 * ch, ch)
-    bases = jnp.stack(
-        [device, device, (device - 1) % count, (device + 1) % count] + [(device - 1) % count, (device + 1) % count] * 2
-    ) * slots
-    local = jnp.where(neighbours >= 0, jnp.clip(neighbours - bases[None, :], 0, slots - 1), -1)
     params = pltpu.CompilerParams(vmem_limit_bytes=VMEM_BYTES)
-
-    east_edge = turned_edge(input_field, land_mask, cols - STEP)
-    west_edge = turned_edge(input_field, land_mask, 0)
-    from_west = permute(east_edge, lambda i, n: (i + 1) % n)
-    from_east = permute(west_edge, lambda i, n: (i - 1) % n)
-
-    edge = (2, slots, STEP, rows, ch)
-    out_inner, grad_inner, dw_inner, x_edge, cot_edge = pl.pallas_call(
-        interior_kernel,
+    side_columns = (slots, STEP, rows, ch)
+    field = input_field.shape
+    own = ch // count if ch // count % 16 == 0 else None
+    outer, middle, _ = stage_sizes(count)
+
+    across, pair, x_edge, cot_edge, field_in, cot_in = pl.pallas_call(
+        load_kernel,
         out_shape=(
-            jax.ShapeDtypeStruct(input_field.shape, BF16),
-            jax.ShapeDtypeStruct(input_field.shape, BF16),
-            jax.ShapeDtypeStruct((ch, 9 * ch), F32),
-            jax.ShapeDtypeStruct((slots, 8, rows, ch), BF16),
-            jax.ShapeDtypeStruct(edge, BF16),
+            shape_bf16(*side_columns),
+            shape_bf16(*side_columns),
+            shape_bf16(slots, 8, rows, ch),
+            shape_bf16(2, *side_columns),
+            shape_bf16(*field),
+            shape_bf16(*field),
         ),
-        in_specs=[SMEM, VMEM, VMEM, VMEM, VMEM],
-        out_specs=(VMEM,) * 5,
+        in_specs=[HBM] * 3,
+        out_specs=(VMEM,) * 6,
+        scratch_shapes=[
+            pltpu.VMEM((slots, rows, cols), jnp.int32),
+            pltpu.SemaphoreType.DMA((1 + 2 * slots,)),
+        ],
+        compiler_params=pltpu.CompilerParams(vmem_limit_bytes=LOAD_BYTES),
+        name="load",
+    )(input_field, cotangent, land_mask)
+    across, pair = swap_halos(across, pair)
+
+    cores = 1 if own is None else 2
+    out_inner, grad_inner, dw_inner = pl.pallas_call(
+        functools.partial(interior_kernel, own),
+        out_shape=(
+            shape_bf16(*field),
+            shape_bf16(*field),
+            shape_f32(cores, ch // cores, 9 * ch),
+        ),
+        in_specs=[SMEM] + [VMEM] * 4,
+        out_specs=(VMEM,) * 3,
         scratch_shapes=[
             pltpu.VMEM((slots, rows + 2 * STEP, cols, 3 * ch), BF16),
-            pltpu.VMEM((slots, rows, cols, ch), BF16),
+            pltpu.VMEM(field, BF16),
             pltpu.VMEM((slots, ch, rows * cols), BF16),
         ],
         compiler_params=params,
@@ -336,18 +488,25 @@
             flops=4 * 9 * slots * rows * cols * ch * ch, bytes_accessed=8 << 20, transcendentals=0
         ),
         name="interior",
-    )(local, input_field, cotangent, taps, land_mask)
-
-    grad_edge, out_edge, dw = pl.pallas_call(
-        edge_kernel,
+    )(neighbours, field_in, cot_in, taps, land_mask)
+
+    if own is None:
+        dw_shapes = (shape_f32(ch, 9 * ch),)
+    else:
+        dw_shapes = (shape_f32(ch // 2, 9 * ch), shape_bf16(ch // 2, 9 * ch))
+    grad_across, grad_pair, grad_edge, out_edge, *dw = pl.pallas_call(
+        functools.partial(edge_kernel, own),
         out_shape=(
-            jax.ShapeDtypeStruct(edge, BF16),
-            jax.ShapeDtypeStruct(edge, BF16),
-            jax.ShapeDtypeStruct((ch, 9 * ch), F32),
+            shape_bf16(*side_columns),
+            shape_bf16(*side_columns),
+            shape_bf16(2, *side_columns),
+            shape_bf16(2, *side_columns),
+            *dw_shapes,
         ),
         in_specs=[SMEM] + [VMEM] * 6,
-        out_specs=(VMEM,) * 3,
+        out_specs=(VMEM,) * (4 + len(dw_shapes)),
         scratch_shapes=[
+            pltpu.VMEM((2, *side_columns), BF16),
             pltpu.VMEM((3, 2, slots, STEP, rows, 3 * ch), BF16),
             pltpu.VMEM((ch, 4 * slots * rows), BF16),
         ],
@@ -356,34 +515,69 @@
             flops=4 * 9 * slots * rows * 4 * ch * ch, bytes_accessed=6 << 20, transcendentals=0
         ),
         name="edges",
-    )(local, from_west, from_east, x_edge, cot_edge, taps, dw_inner)
-
-    grad_west = permute(grad_edge[1], lambda i, n: (i + 1) % n)
-    grad_east = permute(grad_edge[0], lambda i, n: (i - 1) % n)
-    summed = scatter_sum(dw, device)
-
-    layer_output, input_grad = pl.pallas_call(
-        input_grad_kernel,
-        out_shape=(
-            jax.ShapeDtypeStruct(input_field.shape, BF16),
-            jax.ShapeDtypeStruct(input_field.shape, BF16),
-        ),
-        in_specs=[SMEM] + [VMEM] * 9,
-        out_specs=(VMEM,) * 2,
-        scratch_shapes=[
-            pltpu.VMEM((slots, rows + 2 * STEP, cols, 3 * ch), BF16),
-            pltpu.VMEM((slots, rows, cols, ch), BF16),
-            pltpu.VMEM((2, slots, rows, cols // 2, ch), BF16),
-        ],
-        compiler_params=params,
-        cost_estimate=pl.CostEstimate(
-            flops=2 * 9 * slots * rows * cols * ch * ch, bytes_accessed=8 << 20, transcendentals=0
-        ),
-        name="input_grad",
-    )(local, grad_inner, out_inner, grad_edge, out_edge, grad_west, grad_east, cotangent, taps, land_mask)
+    )(neighbours, across, pair, x_edge, cot_edge, taps, dw_inner)
+
+    grad_across, grad_pair = swap_halos(grad_across, grad_pair)
+
+    def input_grad_call():
+        return pl.pallas_call(
+            input_grad_kernel,
+            out_shape=(shape_bf16(*field), shape_bf16(*field)),
+            in_specs=[SMEM] + [VMEM] * 9,
+            out_specs=(HBM, HBM),
+            scratch_shapes=[pltpu.VMEM(field, BF16)] * 2
+            + [
+                pltpu.VMEM((slots, rows + 2 * STEP, cols, 3 * ch), BF16),
+                pltpu.VMEM(field, BF16),
+                pltpu.VMEM((2, slots, rows, cols // 2, ch), BF16),
+                pltpu.SemaphoreType.DMA((2 * slots,)),
+            ],
+            compiler_params=params,
+            cost_estimate=pl.CostEstimate(
+                flops=2 * 9 * slots * rows * cols * ch * ch,
+                bytes_accessed=8 << 20,
+                transcendentals=0,
+            ),
+            name="input_grad",
+        )(
+            neighbours, grad_inner, out_inner, grad_edge, out_edge,
+            grad_across, grad_pair, cot_in, taps, land_mask,
+        )
 
     scale_factor = 1.0 / (rows * math.sqrt(slots * count))
-    return layer_output, input_grad, summed * scale_factor
+    if own is None:
+        summed = scatter_sum(dw[0], device)
+        return *input_grad_call(), summed * scale_factor
+
+    keep, send = dw
+    wide = 9 * ch
+    recv = permute(send, lambda i, n: i ^ 1)
+    whole = (outer, middle, own, wide)
+    keep, *sends = small_call(
+        functools.partial(split_kernel, 2),
+        (shape_f32(outer, own, wide), *[shape_bf16(outer, own, wide)] * (middle - 1)),
+        "middle_terms", keep.reshape(whole), recv.reshape(whole),
+    )
+    recvs = [permute(sends[k - 1], lambda i, n, k=k: i ^ (k * 2)) for k in range(1, middle)]
+    layer_output, input_grad = input_grad_call()
+    keep, *recvs, layer_output, input_grad = lax.optimization_barrier(
+        (keep, *recvs, layer_output, input_grad)
+    )
+    keep, *sends = small_call(
+        functools.partial(split_kernel, 2 * middle),
+        (shape_f32(1, own, wide), *[shape_bf16(1, own, wide)] * (outer - 1)),
+        "outer_terms", keep[None], *[recv[None] for recv in recvs],
+    )
+    recvs = [
+        permute(sends[k - 1], lambda i, n, k=k: i ^ (k * 2 * middle))
+        for k in reversed(range(1, outer))
+    ]
+    (summed,) = small_call(
+        functools.partial(last_kernel, scale_factor),
+        (shape_f32(1, own, wide),),
+        "last_sum", keep, *recvs,
+    )
+    return layer_output, input_grad, summed[0]
 
 
 def solution(mesh):

time: 60.3 us -> 42.9 us (0.71)
  the two profiles are of different devices: /device:TPU:0 before, /device:TPU:1 now
where the time goes in v2:
time: 42.9 us; the launch traced here: 42.7 us
  Pallas kernels  17.1 us (40%)
  waiting for transfers between devices  12.7 us (30%)
  starting transfers between devices  11.5 us (27%)
  local copies, waits for them, and re-layouts  0.76 us (2%)
  between operations  0.72 us (2%)
    ppermute x9, waiting for transfers between devices, permute(): lax.ppermute(value, 'tiles', [(i, pairs_of(i, count)) for i in range(coun...  12.7 us
    ppermute x9, starting transfers between devices, permute(): lax.ppermute(value, 'tiles', [(i, pairs_of(i, count)) for i in range(coun...  11.5 us
    pallas_call x1, Pallas kernels, shards(): pl.pallas_call(functools.partial(interior_kernel, own), out_shape=(shape_...  6.71 us
    pallas_call x1, Pallas kernels, input_grad_call(): pl.pallas_call(input_grad_kernel, out_shape=(shape_bf16(*field), shape_bf...  5.08 us
    pallas_call x1, Pallas kernels, shards(): pl.pallas_call(functools.partial(edge_kernel, own), out_shape=(shape_bf16...  2.22 us
    pallas_call x1, Pallas kernels, shards(): pl.pallas_call(load_kernel, out_shape=(shape_bf16(*side_columns), shape_b...  2.14 us
    pallas_call x3, Pallas kernels, small_call(): pl.pallas_call(kernel, out_shape=out_shapes, in_specs=[VMEM] * len(args),...  0.91 us
  transfers between devices with their start and end apart: 9, of which 4 were waited for; matrix products, arithmetic and copies ran while one was open for 0% of the time, Pallas kernels for 28%

profile of v2, /device:TPU:1, one launch (start us, length us, event | category | flops | bytes accessed | tf_op | source)
XLA Modules:
  0.0 42.7 jit_solution(10762901404678606868)
XLA Ops:
  0.6 0.0 copy-start.1
  0.6 0.7 %copy-done.1 = s32[2,32,32]{2,1,0:T(8,128)S(1)} copy-done((s32[2,32,32]{2,1,0:T(8,128)S(1)}, s32[2,32,32]{2,1,0:T(8,128)}, u32[]{:S(2)}) %copy-start.1) | copy-done | bytes 8216
  1.4 0.0 copy-start
  1.4 0.0 copy-start.2
  1.4 2.1 %load.1 = (bf16[2,2,32,256]{3,2,1,0:T(8,128)(2,1)S(1)}, bf16[2,2,32,256]{3,2,1,0:T(8,128)(2,1)S(1)}, bf16[2,8,32,256]{3,2,1,0:T(8,128)(2,1)S(1)}, bf16[2,2,2,32,...) custom-call(bf16[2,32,32,256]{3,2,1,0:T(8,128)(2,1)} %x_hbm.1, ...), custom_call_target="tpu_custom_call" | custom-call | tf_op jit(solution)/shard_map/load/pallas_call | solution.py:450
  3.5 2.7 %collective-permute-start = (bf16[2,2,32,256]{3,2,1,0:T(8,128)(2,1)S(1)}, bf16[2,2,32,256]{3,2,1,0:T(8,128)(2,1)S(1)}, u32[]{:S(2)}, u32[]{:S(2)}) collective-permute-start(bf16[2,2,32,256]{3,2,1,0:T(8,128)(2,1)S(1)} %get-tuple-element.30), channel_id=1, source_target_pairs={{0,15},{1,2},{2,1},{3,4},{4,3},{5,6},{6,5},{7,8},{8,7},{9,10},{10,... | collective-permute-start | bytes 196616 | tf_op jit(solution)/shard_map/ppermute | solution.py:358
  6.2 2.9 %collective-permute-start.1 = (bf16[2,2,32,256]{3,2,1,0:T(8,128)(2,1)S(1)}, bf16[2,2,32,256]{3,2,1,0:T(8,128)(2,1)S(1)}, u32[]{:S(2)}, u32[]{:S(2)}) collective-permute-start(bf16[2,2,32,256]{3,2,1,0:T(8,128)(2,1)S(1)} %get-tuple-element.31), channel_id=1, source_target_pairs={{0,1},{1,0},{2,3},{3,2},{4,5},{5,4},{6,7},{7,6},{8,9},{9,8},{10,11... | collective-permute-start | bytes 196616 | tf_op jit(solution)/shard_map/ppermute | solution.py:358
  9.1 0.0 copy-done
  9.1 0.0 copy-done.2
  9.1 6.7 %interior.1 = (bf16[2,32,32,256]{3,2,1,0:T(8,128)(2,1)S(1)}, bf16[2,32,32,256]{3,2,1,0:T(8,128)(2,1)S(1)}, f32[2,128,2304]{2,1,0:T(8,128)S(1)}) custom-call(s32[2,8]{1,0:T(2,128)S(1)} %copy-done.2, bf16[2,32,32,256]{3,2,1,0:T(8,128)(2,1)S(1)} %get-tuple-element.34.x_ref, bf16[2,32,32,256]{3,2,1,0:T(8,128)(2,1)S(1)} %get-tuple-element.35.cot_ref, ...), custom_call_target="tpu_custom_call" | custom-call | flops 4831838208 | bytes 8388608 | tf_op jit(solution)/shard_map/interior/pallas_call | solution.py:472
  15.8 0.0 collective-permute-done.across_ref
  15.8 0.0 collective-permute-done.1.pair_ref
  15.9 2.2 %edges.1 = (bf16[2,2,32,256]{3,2,1,0:T(8,128)(2,1)S(1)}, bf16[2,2,32,256]{3,2,1,0:T(8,128)(2,1)S(1)}, bf16[2,2,2,32,256]{4,3,2,1,0:T(8,128)(2,1)S(1)}, bf16[2,2,...) custom-call(s32[2,8]{1,0:T(2,128)S(1)} %copy-done.2, ...), custom_call_target="tpu_custom_call" | custom-call | flops 603979776 | bytes 6291456 | tf_op jit(solution)/shard_map/edges/pallas_call | solution.py:497
  18.1 0.1 collective-permute-start.2
  18.2 2.0 %collective-permute-done.2 = bf16[128,2304]{1,0:T(8,128)(2,1)S(1)} collective-permute-done((bf16[128,2304]{1,0:T(8,128)(2,1)S(1)}, bf16[128,2304]{1,0:T(8,128)(2,1)S(1)}, u32[]{:S(2)}, u32[]{:S(2)}) %collective-permute-start.2) | collective-permute-done | bytes 589856 | tf_op jit(solution)/shard_map/ppermute | solution.py:358
  20.2 0.1 middle_terms.1
  20.3 0.1 collective-permute-start.3
  20.4 1.8 %collective-permute-start.4 = (bf16[2,2,32,256]{3,2,1,0:T(8,128)(2,1)S(1)}, bf16[2,2,32,256]{3,2,1,0:T(8,128)(2,1)S(1)}, u32[]{:S(2)}, u32[]{:S(2)}) collective-permute-start(bf16[2,2,32,256]{3,2,1,0:T(8,128)(2,1)S(1)} %get-tuple-element.45), channel_id=1, source_target_pairs={{0,15},{1,2},{2,1},{3,4},{4,3},{5,6},{6,5},{7,8},{8,7},{9,10},{10,... | collective-permute-start | bytes 196616 | tf_op jit(solution)/shard_map/ppermute | solution.py:358
  22.1 0.4 collective-permute-start.5
  22.5 8.0 %collective-permute-done.4.across_ref = bf16[2,2,32,256]{3,2,1,0:T(8,128)(2,1)S(1)} collective-permute-done((bf16[2,2,32,256]{3,2,1,0:T(8,128)(2,1)S(1)}, bf16[2,2,32,256]{3,2,1,0:T(8,128)(2,1)S(1)}, u32[]{:S(2)}, u32[]{:S(2)}) %collective-permute-start.4) | collective-permute-done | bytes 65568 | tf_op jit(solution)/shard_map/ppermute | solution.py:358
  30.5 0.0 collective-permute-done.5.pair_ref
  30.5 5.1 %input_grad.1 = (bf16[2,32,32,256]{3,2,1,0:T(8,128)(2,1)}, bf16[2,32,32,256]{3,2,1,0:T(8,128)(2,1)}) custom-call(s32[2,8]{1,0:T(2,128)S(1)} %copy-done.2, bf16[2,32,32,256]{3,2,1,0:T(8,128)(2,1)S(1)} %get-tuple-element.41.gi_ref, bf16[2,32,32,256]{3,2,1,0:T(8,128)(2,1)S(1)} %get-tuple-element.42.oi_ref, ...), custom_call_target="tpu_custom_call" | custom-call | flops 2415919104 | bytes 8388608 | tf_op jit(solution)/shard_map/input_grad/pallas_call | solution.py:523
  35.6 0.0 collective-permute-done.3
  35.6 0.1 outer_terms.1
  35.7 0.7 %collective-permute-start.6 = (bf16[1,16,2304]{2,1,0:T(8,128)(2,1)S(1)}, bf16[1,16,2304]{2,1,0:T(8,128)(2,1)S(1)}, u32[]{:S(2)}, u32[]{:S(2)}) collective-permute-start(bf16[1,16,2304]{2,1,0:T(8,128)(2,1)S(1)} %get-tuple-element.54), channel_id=1, source_target_pairs={{0,12},{1,13},{2,14},{3,15},{4,8},{5,9},{6,10},{7,11},{8,4},{9,5},... | collective-permute-start | bytes 221192 | tf_op jit(solution)/shard_map/ppermute | solution.py:358
  36.3 0.0 collective-permute-start.7
  36.3 3.0 %collective-permute-start.8 = (bf16[1,16,2304]{2,1,0:T(8,128)(2,1)S(1)}, bf16[1,16,2304]{2,1,0:T(8,128)(2,1)S(1)}, u32[]{:S(2)}, u32[]{:S(2)}) collective-permute-start(bf16[1,16,2304]{2,1,0:T(8,128)(2,1)S(1)} %get-tuple-element.56), channel_id=1, source_target_pairs={{0,4},{1,5},{2,6},{3,7},{4,0},{5,1},{6,2},{7,3},{8,12},{9,13},{10,... | collective-permute-start | bytes 221192 | tf_op jit(solution)/shard_map/ppermute | solution.py:358
  39.3 1.6 %collective-permute-done.6.refs_0_ = bf16[1,16,2304]{2,1,0:T(8,128)(2,1)S(1)} collective-permute-done((bf16[1,16,2304]{2,1,0:T(8,128)(2,1)S(1)}, bf16[1,16,2304]{2,1,0:T(8,128)(2,1)S(1)}, u32[]{:S(2)}, u32[]{:S(2)}) %collective-permute-start.6) | collective-permute-done | bytes 73760 | tf_op jit(solution)/shard_map/ppermute | solution.py:358
  40.9 1.1 %collective-permute-done.7.refs_1_ = bf16[1,16,2304]{2,1,0:T(8,128)(2,1)S(1)} collective-permute-done((bf16[1,16,2304]{2,1,0:T(8,128)(2,1)S(1)}, bf16[1,16,2304]{2,1,0:T(8,128)(2,1)S(1)}, u32[]{:S(2)}, u32[]{:S(2)}) %collective-permute-start.7) | collective-permute-done | bytes 73760 | tf_op jit(solution)/shard_map/ppermute | solution.py:358
  42.0 0.0 collective-permute-done.8.refs_2_
  42.0 0.7 %last_sum.1 = f32[1,16,2304]{2,1,0:T(8,128)} custom-call(f32[1,16,2304]{2,1,0:T(8,128)S(1)} %get-tuple-element.53.keep_ref, bf16[1,16,2304]{2,1,0:T(8,128)(2,1)S(1)} %collective-permute-done.6.refs_0_, bf16[1,16,2304]{2,1,0:T(8,128)(2,1)S(1)} %collective-permute-done.7.refs_1_, bf16[1,16,2304]{2,1,0:T(8,128)(2,1)S(1)} %collective-permute-done.8.refs_2_), custom_call_target="tpu_custom_call" | custom-call | tf_op jit(solution)/shard_map/last_sum/pallas_call | solution.py:421
Async XLA Ops:
  0.6 0.8 %copy-start.1 = (s32[2,32,32]{2,1,0:T(8,128)S(1)}, s32[2,32,32]{2,1,0:T(8,128)}, u32[]{:S(2)}) copy-start(s32[2,32,32]{2,1,0:T(8,128)} %mask_ref.1) | copy-start | bytes 24580
  1.4 7.7 %copy-start = (bf16[9,256,256]{2,1,0:T(8,128)(2,1)S(1)}, bf16[9,256,256]{2,1,0:T(8,128)(2,1)}, u32[]{:S(2)}) copy-start(bf16[9,256,256]{2,1,0:T(8,128)(2,1)} %param.7) | copy-start | bytes 3538948
  1.4 7.7 %copy-start.2 = (s32[2,8]{1,0:T(2,128)S(1)}, s32[2,8]{1,0:T(2,128)}, u32[]{:S(2)}) copy-start(s32[2,8]{1,0:T(2,128)} %nbr_ref.5) | copy-start | bytes 196
  3.5 12.3 %collective-permute-start = (bf16[2,2,32,256]{3,2,1,0:T(8,128)(2,1)S(1)}, bf16[2,2,32,256]{3,2,1,0:T(8,128)(2,1)S(1)}, u32[]{:S(2)}, u32[]{:S(2)}) collective-permute-start(bf16[2,2,32,256]{3,2,1,0:T(8,128)(2,1)S(1)} %get-tuple-element.30), channel_id=1, source_target_pairs={{0,15},{1,2},{2,1},{3,4},{4,3},{5,6},{6,5},{7,8},{8,7},{9,10},{10,... | collective-permute-start | bytes 196616 | tf_op jit(solution)/shard_map/ppermute | solution.py:358
  6.2 9.6 %collective-permute-start.1 = (bf16[2,2,32,256]{3,2,1,0:T(8,128)(2,1)S(1)}, bf16[2,2,32,256]{3,2,1,0:T(8,128)(2,1)S(1)}, u32[]{:S(2)}, u32[]{:S(2)}) collective-permute-start(bf16[2,2,32,256]{3,2,1,0:T(8,128)(2,1)S(1)} %get-tuple-element.31), channel_id=1, source_target_pairs={{0,1},{1,0},{2,3},{3,2},{4,5},{5,4},{6,7},{7,6},{8,9},{9,8},{10,11... | collective-permute-start | bytes 196616 | tf_op jit(solution)/shard_map/ppermute | solution.py:358
  18.1 2.1 %collective-permute-start.2 = (bf16[128,2304]{1,0:T(8,128)(2,1)S(1)}, bf16[128,2304]{1,0:T(8,128)(2,1)S(1)}, u32[]{:S(2)}, u32[]{:S(2)}) collective-permute-start(bf16[128,2304]{1,0:T(8,128)(2,1)S(1)} %get-tuple-element.38), channel_id=1, source_target_pairs={{0,1},{1,0},{2,3},{3,2},{4,5},{5,4},{6,7},{7,6},{8,9},{9,8},{10,11... | collective-permute-start | bytes 1769480 | tf_op jit(solution)/shard_map/ppermute | solution.py:358
  20.3 15.3 %collective-permute-start.3 = (bf16[4,16,2304]{2,1,0:T(8,128)(2,1)S(1)}, bf16[4,16,2304]{2,1,0:T(8,128)(2,1)S(1)}, u32[]{:S(2)}, u32[]{:S(2)}) collective-permute-start(bf16[4,16,2304]{2,1,0:T(8,128)(2,1)S(1)} %get-tuple-element.40), channel_id=1, source_target_pairs={{0,2},{1,3},{2,0},{3,1},{4,6},{5,7},{6,4},{7,5},{8,10},{9,11},{10,... | collective-permute-start | bytes 884744 | tf_op jit(solution)/shard_map/ppermute | solution.py:358
  20.4 10.1 %collective-permute-start.4 = (bf16[2,2,32,256]{3,2,1,0:T(8,128)(2,1)S(1)}, bf16[2,2,32,256]{3,2,1,0:T(8,128)(2,1)S(1)}, u32[]{:S(2)}, u32[]{:S(2)}) collective-permute-start(bf16[2,2,32,256]{3,2,1,0:T(8,128)(2,1)S(1)} %get-tuple-element.45), channel_id=1, source_target_pairs={{0,15},{1,2},{2,1},{3,4},{4,3},{5,6},{6,5},{7,8},{8,7},{9,10},{10,... | collective-permute-start | bytes 196616 | tf_op jit(solution)/shard_map/ppermute | solution.py:358
  22.1 8.4 %collective-permute-start.5 = (bf16[2,2,32,256]{3,2,1,0:T(8,128)(2,1)S(1)}, bf16[2,2,32,256]{3,2,1,0:T(8,128)(2,1)S(1)}, u32[]{:S(2)}, u32[]{:S(2)}) collective-permute-start(bf16[2,2,32,256]{3,2,1,0:T(8,128)(2,1)S(1)} %get-tuple-element.46), channel_id=1, source_target_pairs={{0,1},{1,0},{2,3},{3,2},{4,5},{5,4},{6,7},{7,6},{8,9},{9,8},{10,11... | collective-permute-start | bytes 196616 | tf_op jit(solution)/shard_map/ppermute | solution.py:358
  35.7 5.2 %collective-permute-start.6 = (bf16[1,16,2304]{2,1,0:T(8,128)(2,1)S(1)}, bf16[1,16,2304]{2,1,0:T(8,128)(2,1)S(1)}, u32[]{:S(2)}, u32[]{:S(2)}) collective-permute-start(bf16[1,16,2304]{2,1,0:T(8,128)(2,1)S(1)} %get-tuple-element.54), channel_id=1, source_target_pairs={{0,12},{1,13},{2,14},{3,15},{4,8},{5,9},{6,10},{7,11},{8,4},{9,5},... | collective-permute-start | bytes 221192 | tf_op jit(solution)/shard_map/ppermute | solution.py:358
  36.3 5.7 %collective-permute-start.7 = (bf16[1,16,2304]{2,1,0:T(8,128)(2,1)S(1)}, bf16[1,16,2304]{2,1,0:T(8,128)(2,1)S(1)}, u32[]{:S(2)}, u32[]{:S(2)}) collective-permute-start(bf16[1,16,2304]{2,1,0:T(8,128)(2,1)S(1)} %get-tuple-element.55), channel_id=1, source_target_pairs={{0,8},{1,9},{2,10},{3,11},{4,12},{5,13},{6,14},{7,15},{8,0},{9,1},... | collective-permute-start | bytes 221192 | tf_op jit(solution)/shard_map/ppermute | solution.py:358
  36.3 5.7 %collective-permute-start.8 = (bf16[1,16,2304]{2,1,0:T(8,128)(2,1)S(1)}, bf16[1,16,2304]{2,1,0:T(8,128)(2,1)S(1)}, u32[]{:S(2)}, u32[]{:S(2)}) collective-permute-start(bf16[1,16,2304]{2,1,0:T(8,128)(2,1)S(1)} %get-tuple-element.56), channel_id=1, source_target_pairs={{0,4},{1,5},{2,6},{3,7},{4,0},{5,1},{6,2},{7,3},{8,12},{9,13},{10,... | collective-permute-start | bytes 221192 | tf_op jit(solution)/shard_map/ppermute | solution.py:358

commit v3 on v2

--- a/solution.py
+++ b/solution.py
@@ -85,49 +85,58 @@
 
 def load_kernel(
     x_hbm, cot_hbm, mask_hbm,
-    across_ref, pair_ref, xe_ref, cote_ref, x_ref, cot_ref,
-    ms, sems,
+    across_ref, pair_ref, xe_ref, cote_ref, x_ref, cot_ref, ms,
+    sems,
 ):
     slots, rows, cols, ch = x_ref.shape
     half = cols // 2
-    loads = start_all(
-        [pltpu.make_async_copy(mask_hbm, ms, sems.at[0])]
-        + [
-            pltpu.make_async_copy(src.at[s], dst.at[s], sems.at[1 + i * slots + s])
-            for i, (src, dst) in enumerate(((x_hbm, x_ref), (cot_hbm, cot_ref)))
-            for s in range(slots)
-        ]
+    mask_in = start_all([pltpu.make_async_copy(mask_hbm, ms, sems.at[0])])
+    x_in, cot_in = (
+        start_all(
+            [
+                pltpu.make_async_copy(src.at[s], dst.at[s], sems.at[1 + i * slots + s])
+                for s in range(slots)
+            ]
+        )
+        for i, (src, dst) in enumerate(((x_hbm, x_ref), (cot_hbm, cot_ref)))
     )
     sel = [
         edge_selector(rows, half, list(range(0, 4))),
         edge_selector(rows, half, list(range(half - 4, half))),
     ]
-    for copy in loads:
-        copy.wait()
+    mask_in[0].wait()
+    oceans = {}
     for s in range(slots):
         mask = ms[s].astype(F32)
         for side in range(2):
             lo = 0 if side == 0 else cols - 4
-            tiles = slice(side * half, side * half + half)
-            ocean = jnp.stack(
+            oceans[s, side] = jnp.stack(
                 [
                     jnp.broadcast_to(mask[:, lo + k : lo + k + 1], (rows, ch)).astype(BF16)
                     for k in range(4)
                 ]
             )
+    for s in range(slots):
+        x_in[s].wait()
+        for side in range(2):
+            tiles = slice(side * half, side * half + half)
             x = dot(sel[side], x_ref[s, :, tiles].reshape(rows * half, ch)).astype(BF16)
-            xe_ref[s, side * 4 : side * 4 + 4] = x.reshape(4, rows, ch) * ocean
+            xe_ref[s, side * 4 : side * 4 + 4] = x.reshape(4, rows, ch) * oceans[s, side]
+    split_sides(xe_ref[:, 0:2], xe_ref[:, 6:8], across_ref, pair_ref)
+    for s in range(slots):
+        cot_in[s].wait()
+        for side in range(2):
+            tiles = slice(side * half, side * half + half)
             outer = slice(0, 2) if side == 0 else slice(2, 4)
             pick = sel[side][: 2 * rows] if side == 0 else sel[side][2 * rows :]
             c = dot(pick, cot_ref[s, :, tiles].reshape(rows * half, ch)).astype(BF16)
-            cote_ref[side, s] = c.reshape(2, rows, ch) * ocean[outer]
-    split_sides(xe_ref[:, 0:2], xe_ref[:, 6:8], across_ref, pair_ref)
+            cote_ref[side, s] = c.reshape(2, rows, ch) * oceans[s, side][outer]
 
 
 def interior_kernel(
     own, nbr_ref, x_ref, cot_ref, w_ref, ms,
-    out_ref, grad_ref, dw_ref,
-    xc, mk, gt,
+    out_ref, grad_ref, dw_ref, xc, gt,
+    mk,
 ):
     slots, rows, cols, ch = x_ref.shape
     zeros = jnp.zeros((rows, STEP, ch), BF16)
@@ -166,13 +175,31 @@
             grad_ref[s, r0 : r0 + block] = g.reshape(block, cols, ch)
             turn_rows(gt.at[s], g, r0 * cols, own)
 
+    rank = dw_ref.shape[0]
+    place = 0 if own is None else other_half(rank)
     for a in range(3):
-        total = None
-        for s in range(slots):
-            window = xc[s, STEP * a : STEP * a + rows].reshape(rows * cols, 3 * ch)
-            term = dot(gt[s], window)
-            total = term if total is None else total + term
-        dw_ref[:, :, a * 3 * ch : (a + 1) * 3 * ch] = total.reshape(dw_ref.shape[0], -1, 3 * ch)
+        dw_ref[:, a * 3 * ch : (a + 1) * 3 * ch] = tap_terms(gt, xc, a, place, rank)
+
+
+def half_of(core, rank):
+    return pl.multiple_of(core * rank, rank)
+
+
+def own_half(rank):
+    return half_of(lax.rem(lax.axis_index("tiles"), 2), rank)
+
+
+def other_half(rank):
+    return half_of(1 - lax.rem(lax.axis_index("tiles"), 2), rank)
+
+
+def tap_terms(gt, xc, a, place, rank):
+    slots, _, cells = gt.shape
+    rows = xc.shape[1] - 2 * STEP
+    wide = xc.shape[3]
+    grads = [gt[s, pl.ds(place, rank), :] for s in range(slots)]
+    windows = [xc[s, STEP * a : STEP * a + rows].reshape(cells, wide) for s in range(slots)]
+    return dot(jnp.concatenate(grads, axis=1), jnp.concatenate(windows, axis=0))
 
 
 def turn_rows(gt, g, first, own):
@@ -195,11 +222,10 @@
 
 def edge_kernel(
     own, nbr_ref, across_ref, pair_ref, xe_ref, cote_ref, w_ref, dwi_ref,
-    gacross_ref, gpair_ref, ge_ref, oe_ref, *outs,
+    gacross_ref, gpair_ref, ge_ref, oe_ref, dw_ref, win, gt,
+    sides,
 ):
-    *dw_refs, sides, win, gt = outs
     slots, _, rows, ch = xe_ref.shape
-    device = lax.axis_index("tiles")
     sides[0], sides[1] = join_sides(across_ref[...], pair_ref[...])
 
     def local(s, column):
@@ -239,23 +265,23 @@
     ge_ref[...] = g.reshape(ge_ref.shape)
     split_sides(g[: cells // 2], g[cells // 2 :], gacross_ref, gpair_ref)
     turn_rows(gt, g, 0, own)
-    if own is None:
-        (dw_ref,) = dw_refs
-        for a in range(3):
-            span = slice(a * 3 * ch, (a + 1) * 3 * ch)
-            dw_ref[:, span] = dwi_ref[0, :, span] + dot(gt[...], win[a].reshape(cells, 3 * ch))
-        return
-    keep_ref, send_ref = dw_refs
-    core = lax.rem(device, 2)
-    rank = ch // 2
-    keep_rows = gt[pl.ds(pl.multiple_of(core * rank, rank), rank), :]
-    send_rows = gt[pl.ds(pl.multiple_of((1 - core) * rank, rank), rank), :]
-    turned = jnp.concatenate([keep_rows, send_rows], axis=0)
+    rank = dw_ref.shape[0]
+    place = 0 if own is None else other_half(rank)
+    turned = gt[pl.ds(place, rank), :]
     for a in range(3):
         span = slice(a * 3 * ch, (a + 1) * 3 * ch)
-        term = dot(turned, win[a].reshape(cells, 3 * ch))
-        keep_ref[:, span] = dwi_ref[core, :, span] + term[:rank]
-        send_ref[:, span] = (dwi_ref[1 - core, :, span] + term[rank:]).astype(BF16)
+        total = dwi_ref[:, span] + dot(turned, win[a].reshape(cells, 3 * ch))
+        dw_ref[:, span] = total.astype(dw_ref.dtype)
+
+
+def keep_kernel(xc, gt, win, edge_gt, keep_ref):
+    rank = keep_ref.shape[0]
+    wide = xc.shape[3]
+    place = own_half(rank)
+    turned = edge_gt[pl.ds(place, rank), :]
+    for a in range(3):
+        edge = dot(turned, win[a].reshape(edge_gt.shape[1], wide))
+        keep_ref[:, a * wide : (a + 1) * wide] = tap_terms(gt, xc, a, place, rank) + edge
 
 
 def spread_selector(rows, cols, first):
@@ -447,7 +473,7 @@
     own = ch // count if ch // count % 16 == 0 else None
     outer, middle, _ = stage_sizes(count)
 
-    across, pair, x_edge, cot_edge, field_in, cot_in = pl.pallas_call(
+    across, pair, x_edge, cot_edge, field_in, cot_in, ocean = pl.pallas_call(
         load_kernel,
         out_shape=(
             shape_bf16(*side_columns),
@@ -456,60 +482,50 @@
             shape_bf16(2, *side_columns),
             shape_bf16(*field),
             shape_bf16(*field),
+            jax.ShapeDtypeStruct(land_mask.shape, jnp.int32),
         ),
         in_specs=[HBM] * 3,
-        out_specs=(VMEM,) * 6,
-        scratch_shapes=[
-            pltpu.VMEM((slots, rows, cols), jnp.int32),
-            pltpu.SemaphoreType.DMA((1 + 2 * slots,)),
-        ],
+        out_specs=(VMEM,) * 7,
+        scratch_shapes=[pltpu.SemaphoreType.DMA((1 + 2 * slots,))],
         compiler_params=pltpu.CompilerParams(vmem_limit_bytes=LOAD_BYTES),
         name="load",
     )(input_field, cotangent, land_mask)
     across, pair = swap_halos(across, pair)
 
-    cores = 1 if own is None else 2
-    out_inner, grad_inner, dw_inner = pl.pallas_call(
+    rank = ch if own is None else ch // 2
+    out_inner, grad_inner, dw_inner, windows, turned = pl.pallas_call(
         functools.partial(interior_kernel, own),
         out_shape=(
             shape_bf16(*field),
             shape_bf16(*field),
-            shape_f32(cores, ch // cores, 9 * ch),
+            shape_f32(rank, 9 * ch),
+            shape_bf16(slots, rows + 2 * STEP, cols, 3 * ch),
+            shape_bf16(slots, ch, rows * cols),
         ),
         in_specs=[SMEM] + [VMEM] * 4,
-        out_specs=(VMEM,) * 3,
-        scratch_shapes=[
-            pltpu.VMEM((slots, rows + 2 * STEP, cols, 3 * ch), BF16),
-            pltpu.VMEM(field, BF16),
-            pltpu.VMEM((slots, ch, rows * cols), BF16),
-        ],
+        out_specs=(VMEM,) * 5,
+        scratch_shapes=[pltpu.VMEM(field, BF16)],
         compiler_params=params,
         cost_estimate=pl.CostEstimate(
             flops=4 * 9 * slots * rows * cols * ch * ch, bytes_accessed=8 << 20, transcendentals=0
         ),
         name="interior",
-    )(neighbours, field_in, cot_in, taps, land_mask)
-
-    if own is None:
-        dw_shapes = (shape_f32(ch, 9 * ch),)
-    else:
-        dw_shapes = (shape_f32(ch // 2, 9 * ch), shape_bf16(ch // 2, 9 * ch))
-    grad_across, grad_pair, grad_edge, out_edge, *dw = pl.pallas_call(
+    )(neighbours, field_in, cot_in, taps, ocean)
+
+    grad_across, grad_pair, grad_edge, out_edge, dw, edge_windows, edge_turned = pl.pallas_call(
         functools.partial(edge_kernel, own),
         out_shape=(
             shape_bf16(*side_columns),
             shape_bf16(*side_columns),
             shape_bf16(2, *side_columns),
             shape_bf16(2, *side_columns),
-            *dw_shapes,
+            shape_f32(ch, 9 * ch) if own is None else shape_bf16(rank, 9 * ch),
+            shape_bf16(3, 2, slots, STEP, rows, 3 * ch),
+            shape_bf16(ch, 4 * slots * rows),
         ),
         in_specs=[SMEM] + [VMEM] * 6,
-        out_specs=(VMEM,) * (4 + len(dw_shapes)),
-        scratch_shapes=[
-            pltpu.VMEM((2, *side_columns), BF16),
-            pltpu.VMEM((3, 2, slots, STEP, rows, 3 * ch), BF16),
-            pltpu.VMEM((ch, 4 * slots * rows), BF16),
-        ],
+        out_specs=(VMEM,) * 7,
+        scratch_shapes=[pltpu.VMEM((2, *side_columns), BF16)],
         compiler_params=params,
         cost_estimate=pl.CostEstimate(
             flops=4 * 9 * slots * rows * 4 * ch * ch, bytes_accessed=6 << 20, transcendentals=0
@@ -519,7 +535,7 @@
 
     grad_across, grad_pair = swap_halos(grad_across, grad_pair)
 
-    def input_grad_call():
+    def input_grad_call(grad_edge):
         return pl.pallas_call(
             input_grad_kernel,
             out_shape=(shape_bf16(*field), shape_bf16(*field)),
@@ -541,17 +557,27 @@
             name="input_grad",
         )(
             neighbours, grad_inner, out_inner, grad_edge, out_edge,
-            grad_across, grad_pair, cot_in, taps, land_mask,
+            grad_across, grad_pair, cot_in, taps, ocean,
         )
 
     scale_factor = 1.0 / (rows * math.sqrt(slots * count))
     if own is None:
-        summed = scatter_sum(dw[0], device)
-        return *input_grad_call(), summed * scale_factor
-
-    keep, send = dw
+        summed = scatter_sum(dw, device)
+        return *input_grad_call(grad_edge), summed * scale_factor
+
     wide = 9 * ch
-    recv = permute(send, lambda i, n: i ^ 1)
+    recv = permute(dw, lambda i, n: i ^ 1)
+    (keep,) = pl.pallas_call(
+        keep_kernel,
+        out_shape=(shape_f32(rank, wide),),
+        in_specs=[VMEM] * 4,
+        out_specs=(VMEM,),
+        compiler_params=params,
+        cost_estimate=pl.CostEstimate(
+            flops=9 * slots * rows * (cols + 4) * ch * ch, bytes_accessed=0, transcendentals=0
+        ),
+        name="keep",
+    )(windows, turned, edge_windows, edge_turned)
     whole = (outer, middle, own, wide)
     keep, *sends = small_call(
         functools.partial(split_kernel, 2),
@@ -559,19 +585,17 @@
         "middle_terms", keep.reshape(whole), recv.reshape(whole),
     )
     recvs = [permute(sends[k - 1], lambda i, n, k=k: i ^ (k * 2)) for k in range(1, middle)]
-    layer_output, input_grad = input_grad_call()
-    keep, *recvs, layer_output, input_grad = lax.optimization_barrier(
-        (keep, *recvs, layer_output, input_grad)
-    )
     keep, *sends = small_call(
         functools.partial(split_kernel, 2 * middle),
         (shape_f32(1, own, wide), *[shape_bf16(1, own, wide)] * (outer - 1)),
         "outer_terms", keep[None], *[recv[None] for recv in recvs],
     )
+    keep, grad_edge = lax.optimization_barrier((keep, grad_edge))
     recvs = [
         permute(sends[k - 1], lambda i, n, k=k: i ^ (k * 2 * middle))
         for k in reversed(range(1, outer))
     ]
+    layer_output, input_grad = input_grad_call(grad_edge)
     (summed,) = small_call(
         functools.partial(last_kernel, scale_factor),
         (shape_f32(1, own, wide),),

time: 42.9 us -> 39.5 us (0.921)
  the two profiles are of different devices: /device:TPU:1 before, /device:TPU:0 now
where the time goes in v3:
time: 39.5 us; the launch traced here: 39.3 us
  Pallas kernels  17.2 us (44%)
  starting transfers between devices  12.7 us (32%)
  waiting for transfers between devices  7.91 us (20%)
  local copies, waits for them, and re-layouts  0.76 us (2%)
  between operations  0.74 us (2%)
    ppermute x9, starting transfers between devices, permute(): lax.ppermute(value, 'tiles', [(i, pairs_of(i, count)) for i in range(coun...  12.7 us
    ppermute x9, waiting for transfers between devices, permute(): lax.ppermute(value, 'tiles', [(i, pairs_of(i, count)) for i in range(coun...  7.91 us
    pallas_call x1, Pallas kernels, shards(): pl.pallas_call(functools.partial(interior_kernel, own), out_shape=(shape_...  5.75 us
    pallas_call x1, Pallas kernels, input_grad_call(): pl.pallas_call(input_grad_kernel, out_shape=(shape_bf16(*field), shape_bf...  5.08 us
    pallas_call x1, Pallas kernels, shards(): pl.pallas_call(load_kernel, out_shape=(shape_bf16(*side_columns), shape_b...  2.11 us
    pallas_call x1, Pallas kernels, shards(): pl.pallas_call(functools.partial(edge_kernel, own), out_shape=(shape_bf16...  1.79 us
    pallas_call x1, Pallas kernels, shards(): pl.pallas_call(keep_kernel, out_shape=(shape_f32(rank, wide),), in_specs=...  1.56 us
    pallas_call x3, Pallas kernels, small_call(): pl.pallas_call(kernel, out_shape=out_shapes, in_specs=[VMEM] * len(args),...  0.88 us
  transfers between devices with their start and end apart: 9, of which 2 were waited for; matrix products, arithmetic and copies ran while one was open for 0% of the time, Pallas kernels for 32%

profile of v3, /device:TPU:0, one launch (start us, length us, event | category | flops | bytes accessed | tf_op | source)
XLA Modules:
  0.0 39.3 jit_solution(962195209688920914)
XLA Ops:
  0.6 0.0 copy-start.1
  0.6 0.7 %copy-done.1 = s32[2,32,32]{2,1,0:T(8,128)S(1)} copy-done((s32[2,32,32]{2,1,0:T(8,128)S(1)}, s32[2,32,32]{2,1,0:T(8,128)}, u32[]{:S(2)}) %copy-start.1) | copy-done | bytes 8216
  1.4 0.0 copy-start
  1.4 0.0 copy-start.2
  1.4 2.1 %load.1 = (bf16[2,2,32,256]{3,2,1,0:T(8,128)(2,1)S(1)}, bf16[2,2,32,256]{3,2,1,0:T(8,128)(2,1)S(1)}, bf16[2,8,32,256]{3,2,1,0:T(8,128)(2,1)S(1)}, bf16[2,2,2,32,...) custom-call(bf16[2,32,32,256]{3,2,1,0:T(8,128)(2,1)} %x_hbm.1, ...), custom_call_target="tpu_custom_call" | custom-call | tf_op jit(solution)/shard_map/load/pallas_call | solution.py:476
  3.5 5.5 %collective-permute-start = (bf16[2,2,32,256]{3,2,1,0:T(8,128)(2,1)S(1)}, bf16[2,2,32,256]{3,2,1,0:T(8,128)(2,1)S(1)}, u32[]{:S(2)}, u32[]{:S(2)}) collective-permute-start(bf16[2,2,32,256]{3,2,1,0:T(8,128)(2,1)S(1)} %get-tuple-element.39), channel_id=1, source_target_pairs={{0,15},{1,2},{2,1},{3,4},{4,3},{5,6},{6,5},{7,8},{8,7},{9,10},{10,... | collective-permute-start | bytes 196616 | tf_op jit(solution)/shard_map/ppermute | solution.py:384
  9.0 0.0 collective-permute-start.1
  9.0 0.0 copy-done
  9.0 0.0 copy-done.2
  9.0 5.8 %interior.1 = (bf16[2,32,32,256]{3,2,1,0:T(8,128)(2,1)S(1)}, bf16[2,32,32,256]{3,2,1,0:T(8,128)(2,1)S(1)}, f32[128,2304]{1,0:T(8,128)S(1)}, bf16[2,36,32,768]{3,...) custom-call(s32[2,8]{1,0:T(2,128)S(1)} %copy-done.2, bf16[2,32,32,256]{3,2,1,0:T(8,128)(2,1)S(1)} %get-tuple-element.32.x_ref, ...), custom_call_target="tpu_custom_call" | custom-call | flops 4831838208 | bytes 8388608 | tf_op jit(solution)/shard_map/interior/pallas_call | solution.py:496
  14.8 0.0 collective-permute-done.across_ref
  14.8 0.0 collective-permute-done.1.pair_ref
  14.8 1.8 %edges.1 = (bf16[2,2,32,256]{3,2,1,0:T(8,128)(2,1)S(1)}, bf16[2,2,32,256]{3,2,1,0:T(8,128)(2,1)S(1)}, bf16[2,2,2,32,256]{4,3,2,1,0:T(8,128)(2,1)S(1)}, bf16[2,2,...) custom-call(s32[2,8]{1,0:T(2,128)S(1)} %copy-done.2, ...), custom_call_target="tpu_custom_call" | custom-call | flops 603979776 | bytes 6291456 | tf_op jit(solution)/shard_map/edges/pallas_call | solution.py:515
  16.6 0.6 %collective-permute-start.2 = (bf16[128,2304]{1,0:T(8,128)(2,1)S(1)}, bf16[128,2304]{1,0:T(8,128)(2,1)S(1)}, u32[]{:S(2)}, u32[]{:S(2)}) collective-permute-start(bf16[128,2304]{1,0:T(8,128)(2,1)S(1)} %get-tuple-element.46), channel_id=1, source_target_pairs={{0,1},{1,0},{2,3},{3,2},{4,5},{5,4},{6,7},{7,6},{8,9},{9,8},{10,11... | collective-permute-start | bytes 1769480 | tf_op jit(solution)/shard_map/ppermute | solution.py:384
  17.2 1.6 %keep.1 = f32[128,2304]{1,0:T(8,128)S(1)} custom-call(bf16[2,36,32,768]{3,2,1,0:T(8,128)(2,1)S(1)} %get-tuple-element.37.xc, bf16[2,256,1024]{2,1,0:T(8,128)(2,1)S(1)} %get-tuple-element.38.gt, bf16[3,2,2,2,32,768]{5,4,3,2,1,0:T(8,128)(2,1)S(1)} %get-tuple-element.44.win, bf16[256,256]{1,0:T(8,128)(2,1)S(1)} %get-tuple-element.45.edge_gt), custom_call_target="tpu_custom_call" | custom-call | flops 1358954496 | tf_op jit(solution)/shard_map/keep/pallas_call | solution.py:570
  18.7 0.1 collective-permute-done.2
  18.8 0.1 middle_terms.1
  18.9 0.1 collective-permute-start.3
  19.0 2.0 %collective-permute-start.4 = (bf16[2,2,32,256]{3,2,1,0:T(8,128)(2,1)S(1)}, bf16[2,2,32,256]{3,2,1,0:T(8,128)(2,1)S(1)}, u32[]{:S(2)}, u32[]{:S(2)}) collective-permute-start(bf16[2,2,32,256]{3,2,1,0:T(8,128)(2,1)S(1)} %get-tuple-element.53), channel_id=1, source_target_pairs={{0,15},{1,2},{2,1},{3,4},{4,3},{5,6},{6,5},{7,8},{8,7},{9,10},{10,... | collective-permute-start | bytes 196616 | tf_op jit(solution)/shard_map/ppermute | solution.py:384
  21.0 0.1 collective-permute-start.5
  21.1 7.8 %collective-permute-done.3 = bf16[4,16,2304]{2,1,0:T(8,128)(2,1)S(1)} collective-permute-done((bf16[4,16,2304]{2,1,0:T(8,128)(2,1)S(1)}, bf16[4,16,2304]{2,1,0:T(8,128)(2,1)S(1)}, u32[]{:S(2)}, u32[]{:S(2)}) %collective-permute-start.3) | collective-permute-done | bytes 294944 | tf_op jit(solution)/shard_map/ppermute | solution.py:384
  29.0 0.1 outer_terms.1
  29.0 0.9 %collective-permute-start.6 = (bf16[1,16,2304]{2,1,0:T(8,128)(2,1)S(1)}, bf16[1,16,2304]{2,1,0:T(8,128)(2,1)S(1)}, u32[]{:S(2)}, u32[]{:S(2)}) collective-permute-start(bf16[1,16,2304]{2,1,0:T(8,128)(2,1)S(1)} %get-tuple-element.58), channel_id=1, source_target_pairs={{0,12},{1,13},{2,14},{3,15},{4,8},{5,9},{6,10},{7,11},{8,4},{9,5},... | collective-permute-start | bytes 221192 | tf_op jit(solution)/shard_map/ppermute | solution.py:384
  30.0 0.0 collective-permute-start.7
  30.0 3.5 %collective-permute-start.8 = (bf16[1,16,2304]{2,1,0:T(8,128)(2,1)S(1)}, bf16[1,16,2304]{2,1,0:T(8,128)(2,1)S(1)}, u32[]{:S(2)}, u32[]{:S(2)}) collective-permute-start(bf16[1,16,2304]{2,1,0:T(8,128)(2,1)S(1)} %get-tuple-element.60), channel_id=1, source_target_pairs={{0,4},{1,5},{2,6},{3,7},{4,0},{5,1},{6,2},{7,3},{8,12},{9,13},{10,... | collective-permute-start | bytes 221192 | tf_op jit(solution)/shard_map/ppermute | solution.py:384
  33.5 0.0 collective-permute-done.4.across_ref
  33.5 0.0 collective-permute-done.5.pair_ref
  33.5 5.1 %input_grad.1 = (bf16[2,32,32,256]{3,2,1,0:T(8,128)(2,1)}, bf16[2,32,32,256]{3,2,1,0:T(8,128)(2,1)}) custom-call(s32[2,8]{1,0:T(2,128)S(1)} %copy-done.2, bf16[2,32,32,256]{3,2,1,0:T(8,128)(2,1)S(1)} %get-tuple-element.35.gi_ref, bf16[2,32,32,256]{3,2,1,0:T(8,128)(2,1)S(1)} %get-tuple-element.36.oi_ref, ...), custom_call_target="tpu_custom_call" | custom-call | flops 2415919104 | bytes 8388608 | tf_op jit(solution)/shard_map/input_grad/pallas_call | solution.py:539
  38.6 0.0 collective-permute-done.6.refs_0_
  38.6 0.0 collective-permute-done.7.refs_1_
  38.6 0.0 collective-permute-done.8.refs_2_
  38.6 0.7 %last_sum.1 = f32[1,16,2304]{2,1,0:T(8,128)} custom-call(f32[1,16,2304]{2,1,0:T(8,128)S(1)} %get-tuple-element.57.keep_ref, bf16[1,16,2304]{2,1,0:T(8,128)(2,1)S(1)} %collective-permute-done.6.refs_0_, bf16[1,16,2304]{2,1,0:T(8,128)(2,1)S(1)} %collective-permute-done.7.refs_1_, bf16[1,16,2304]{2,1,0:T(8,128)(2,1)S(1)} %collective-permute-done.8.refs_2_), custom_call_target="tpu_custom_call" | custom-call | tf_op jit(solution)/shard_map/last_sum/pallas_call | solution.py:447
Async XLA Ops:
  0.6 0.8 %copy-start.1 = (s32[2,32,32]{2,1,0:T(8,128)S(1)}, s32[2,32,32]{2,1,0:T(8,128)}, u32[]{:S(2)}) copy-start(s32[2,32,32]{2,1,0:T(8,128)} %mask_hbm.1) | copy-start | bytes 24580
  1.4 7.6 %copy-start = (bf16[9,256,256]{2,1,0:T(8,128)(2,1)S(1)}, bf16[9,256,256]{2,1,0:T(8,128)(2,1)}, u32[]{:S(2)}) copy-start(bf16[9,256,256]{2,1,0:T(8,128)(2,1)} %param.7) | copy-start | bytes 3538948
  1.4 7.6 %copy-start.2 = (s32[2,8]{1,0:T(2,128)S(1)}, s32[2,8]{1,0:T(2,128)}, u32[]{:S(2)}) copy-start(s32[2,8]{1,0:T(2,128)} %nbr_ref.5) | copy-start | bytes 196
  3.5 11.3 %collective-permute-start = (bf16[2,2,32,256]{3,2,1,0:T(8,128)(2,1)S(1)}, bf16[2,2,32,256]{3,2,1,0:T(8,128)(2,1)S(1)}, u32[]{:S(2)}, u32[]{:S(2)}) collective-permute-start(bf16[2,2,32,256]{3,2,1,0:T(8,128)(2,1)S(1)} %get-tuple-element.39), channel_id=1, source_target_pairs={{0,15},{1,2},{2,1},{3,4},{4,3},{5,6},{6,5},{7,8},{8,7},{9,10},{10,... | collective-permute-start | bytes 196616 | tf_op jit(solution)/shard_map/ppermute | solution.py:384
  9.0 5.8 %collective-permute-start.1 = (bf16[2,2,32,256]{3,2,1,0:T(8,128)(2,1)S(1)}, bf16[2,2,32,256]{3,2,1,0:T(8,128)(2,1)S(1)}, u32[]{:S(2)}, u32[]{:S(2)}) collective-permute-start(bf16[2,2,32,256]{3,2,1,0:T(8,128)(2,1)S(1)} %get-tuple-element.40), channel_id=1, source_target_pairs={{0,1},{1,0},{2,3},{3,2},{4,5},{5,4},{6,7},{7,6},{8,9},{9,8},{10,11... | collective-permute-start | bytes 196616 | tf_op jit(solution)/shard_map/ppermute | solution.py:384
  16.6 2.2 %collective-permute-start.2 = (bf16[128,2304]{1,0:T(8,128)(2,1)S(1)}, bf16[128,2304]{1,0:T(8,128)(2,1)S(1)}, u32[]{:S(2)}, u32[]{:S(2)}) collective-permute-start(bf16[128,2304]{1,0:T(8,128)(2,1)S(1)} %get-tuple-element.46), channel_id=1, source_target_pairs={{0,1},{1,0},{2,3},{3,2},{4,5},{5,4},{6,7},{7,6},{8,9},{9,8},{10,11... | collective-permute-start | bytes 1769480 | tf_op jit(solution)/shard_map/ppermute | solution.py:384
  18.9 10.1 %collective-permute-start.3 = (bf16[4,16,2304]{2,1,0:T(8,128)(2,1)S(1)}, bf16[4,16,2304]{2,1,0:T(8,128)(2,1)S(1)}, u32[]{:S(2)}, u32[]{:S(2)}) collective-permute-start(bf16[4,16,2304]{2,1,0:T(8,128)(2,1)S(1)} %get-tuple-element.48), channel_id=1, source_target_pairs={{0,2},{1,3},{2,0},{3,1},{4,6},{5,7},{6,4},{7,5},{8,10},{9,11},{10,... | collective-permute-start | bytes 884744 | tf_op jit(solution)/shard_map/ppermute | solution.py:384
  19.0 14.5 %collective-permute-start.4 = (bf16[2,2,32,256]{3,2,1,0:T(8,128)(2,1)S(1)}, bf16[2,2,32,256]{3,2,1,0:T(8,128)(2,1)S(1)}, u32[]{:S(2)}, u32[]{:S(2)}) collective-permute-start(bf16[2,2,32,256]{3,2,1,0:T(8,128)(2,1)S(1)} %get-tuple-element.53), channel_id=1, source_target_pairs={{0,15},{1,2},{2,1},{3,4},{4,3},{5,6},{6,5},{7,8},{8,7},{9,10},{10,... | collective-permute-start | bytes 196616 | tf_op jit(solution)/shard_map/ppermute | solution.py:384
  21.0 12.5 %collective-permute-start.5 = (bf16[2,2,32,256]{3,2,1,0:T(8,128)(2,1)S(1)}, bf16[2,2,32,256]{3,2,1,0:T(8,128)(2,1)S(1)}, u32[]{:S(2)}, u32[]{:S(2)}) collective-permute-start(bf16[2,2,32,256]{3,2,1,0:T(8,128)(2,1)S(1)} %get-tuple-element.54), channel_id=1, source_target_pairs={{0,1},{1,0},{2,3},{3,2},{4,5},{5,4},{6,7},{7,6},{8,9},{9,8},{10,11... | collective-permute-start | bytes 196616 | tf_op jit(solution)/shard_map/ppermute | solution.py:384
  29.0 9.5 %collective-permute-start.6 = (bf16[1,16,2304]{2,1,0:T(8,128)(2,1)S(1)}, bf16[1,16,2304]{2,1,0:T(8,128)(2,1)S(1)}, u32[]{:S(2)}, u32[]{:S(2)}) collective-permute-start(bf16[1,16,2304]{2,1,0:T(8,128)(2,1)S(1)} %get-tuple-element.58), channel_id=1, source_target_pairs={{0,12},{1,13},{2,14},{3,15},{4,8},{5,9},{6,10},{7,11},{8,4},{9,5},... | collective-permute-start | bytes 221192 | tf_op jit(solution)/shard_map/ppermute | solution.py:384
  30.0 8.6 %collective-permute-start.7 = (bf16[1,16,2304]{2,1,0:T(8,128)(2,1)S(1)}, bf16[1,16,2304]{2,1,0:T(8,128)(2,1)S(1)}, u32[]{:S(2)}, u32[]{:S(2)}) collective-permute-start(bf16[1,16,2304]{2,1,0:T(8,128)(2,1)S(1)} %get-tuple-element.59), channel_id=1, source_target_pairs={{0,8},{1,9},{2,10},{3,11},{4,12},{5,13},{6,14},{7,15},{8,0},{9,1},... | collective-permute-start | bytes 221192 | tf_op jit(solution)/shard_map/ppermute | solution.py:384
  30.0 8.6 %collective-permute-start.8 = (bf16[1,16,2304]{2,1,0:T(8,128)(2,1)S(1)}, bf16[1,16,2304]{2,1,0:T(8,128)(2,1)S(1)}, u32[]{:S(2)}, u32[]{:S(2)}) collective-permute-start(bf16[1,16,2304]{2,1,0:T(8,128)(2,1)S(1)} %get-tuple-element.60), channel_id=1, source_target_pairs={{0,4},{1,5},{2,6},{3,7},{4,0},{5,1},{6,2},{7,3},{8,12},{9,13},{10,... | collective-permute-start | bytes 221192 | tf_op jit(solution)/shard_map/ppermute | solution.py:384

commit v4 on v3

--- a/solution.py
+++ b/solution.py
@@ -292,35 +292,38 @@
     return jnp.where((src == want) & (out % cols >= first) & (out % cols < first + 2), 1.0, 0.0).astype(BF16)
 
 
-def input_grad_kernel(
-    nbr_ref, gi_ref, oi_ref, ge_ref, oe_ref, across_ref, pair_ref, cot_ref, w_ref, mask_ref,
-    out_hbm, ig_hbm,
-    out_ref, ig_ref, gc, mk, hs, sems,
+def spread_edge(sel, edge):
+    _, rows, ch = edge.shape
+    return dot(sel, edge.reshape(2 * rows, ch)).astype(BF16).reshape(rows, -1, ch)
+
+
+def gradient_kernel(
+    nbr_ref, gi_ref, oi_ref, ge_ref, oe_ref, mask_ref, w_ref,
+    out_hbm, gc, mk, wt_ref,
+    out_ref, sems,
 ):
     slots, rows, cols, ch = gi_ref.shape
     half = cols // 2
     zeros = jnp.zeros((rows, STEP, ch), BF16)
     low = spread_selector(rows, half, 0)
     high = spread_selector(rows, half, half - 2)
-    halos = join_sides(across_ref[...], pair_ref[...])
-
-    def spread(sel, edge):
-        return dot(sel, edge.reshape(2 * rows, ch)).astype(BF16).reshape(rows, half, ch)
-
     column = lax.broadcasted_iota(jnp.int32, (rows, half, ch), 1)
+    stores = []
     for s in range(slots):
         for r, line in enumerate(column_masks(mask_ref[s])):
             mk[s, r] = line
-        out_low = jnp.where(column < STEP, spread(low, oe_ref[0, s]), oi_ref[s, :, :half])
+        out_low = jnp.where(column < STEP, spread_edge(low, oe_ref[0, s]), oi_ref[s, :, :half])
         out_ref[s, :, :half] = out_low * mk[s, :, :half]
         out_high = jnp.where(
-            column >= half - STEP, spread(high, oe_ref[1, s]), oi_ref[s, :, half:]
+            column >= half - STEP, spread_edge(high, oe_ref[1, s]), oi_ref[s, :, half:]
         )
         out_ref[s, :, half:] = out_high * mk[s, :, half:]
+        stores += start_all([pltpu.make_async_copy(out_ref.at[s], out_hbm.at[s], sems.at[s])])
+    for s in range(slots):
         g = jnp.concatenate(
             [
-                gi_ref[s, :, :half] + spread(low, ge_ref[0, s]),
-                gi_ref[s, :, half:] + spread(high, ge_ref[1, s]),
+                gi_ref[s, :, :half] + spread_edge(low, ge_ref[0, s]),
+                gi_ref[s, :, half:] + spread_edge(high, ge_ref[1, s]),
             ],
             axis=1,
         )
@@ -329,52 +332,62 @@
             [zeros, g[:, : cols - STEP]], axis=1
         )
         gc[s, STEP : rows + STEP, :, 0:ch] = jnp.concatenate([g[:, STEP:], zeros], axis=1)
-        hs[0, s] = spread(low, halos[0][s])
-        hs[1, s] = spread(high, halos[1][s])
-    stores = start_all(
-        [pltpu.make_async_copy(out_ref.at[s], out_hbm.at[s], sems.at[s]) for s in range(slots)]
-    )
     for s in range(slots):
         north, south = local_id(nbr_ref[s, 0], slots), local_id(nbr_ref[s, 1], slots)
         gc[s, 0:STEP] = gc[jnp.maximum(north, 0), rows : rows + STEP] * present_bf16(north)
         gc[s, rows + STEP :] = gc[jnp.maximum(south, 0), STEP : 2 * STEP] * present_bf16(south)
-    for s in range(slots):
-        for side, (mid, top, low_entry), lanes, lo in (
-            (0, (2, 4, 6), 2 * ch, 0),
-            (1, (3, 5, 7), 0, half),
-        ):
-            def piece(entry, first, count):
-                entry = local_id(nbr_ref[s, entry], slots)
-                return hs[side, jnp.maximum(entry, 0), first : first + count] * present_bf16(entry)
-
-            halo = jnp.concatenate(
-                [piece(top, rows - STEP, STEP), piece(mid, 0, rows), piece(low_entry, 0, STEP)],
-                axis=0,
-            )
-            gc[s, :, lo : lo + half, lanes : lanes + ch] += halo
+    for a in range(3):
+        for b in range(3):
+            lanes = slice(b * ch, (b + 1) * ch)
+            wt_ref[a, lanes] = w_ref[a, lanes].T
+    for copy in stores:
+        copy.wait()
+
+
+def input_grad_kernel(
+    nbr_ref, gc, mk, across_ref, pair_ref, cot_ref, wt_ref,
+    ig_hbm,
+    ig_ref, hs, ht, sems,
+):
+    slots, rows, cols, ch = cot_ref.shape
+    half = cols // 2
+    halos = join_sides(across_ref[...], pair_ref[...])
+    for side in range(2):
+        sel = spread_selector(rows, half, 0 if side == 0 else half - 2)
+        for s in range(slots):
+            hs[side, s] = spread_edge(sel, halos[side][s])
+    for s in range(slots):
+        for side, entries in enumerate(((4, 2, 6), (5, 3, 7))):
+            lo, lanes = (0, 2 * ch) if side == 0 else (half, 0)
+            for column, span, at in zip(
+                entries,
+                (slice(rows - STEP, rows), slice(0, rows), slice(0, STEP)),
+                (slice(0, STEP), slice(STEP, rows + STEP), slice(rows + STEP, None)),
+            ):
+                entry = local_id(nbr_ref[s, column], slots)
+                halo = hs[side, jnp.maximum(entry, 0), span] * present_bf16(entry)
+                ht[side, s, at] = gc[s, at, lo : lo + half, lanes : lanes + ch] + halo
     block = 8
+    stores = []
     for s in range(slots):
         for r0 in range(0, rows, block):
             acc = None
             for a in range(3):
-                first = r0 + STEP * (2 - a)
-                for b in range(3):
-                    window = gc[s, first : first + block, :, b * ch : (b + 1) * ch].reshape(
-                        block * cols, ch
-                    )
-                    term = lax.dot_general(
-                        window,
-                        w_ref[a, b * ch : (b + 1) * ch],
-                        (((1,), (1,)), ((), ())),
-                        preferred_element_type=F32,
-                    )
-                    acc = term if acc is None else acc + term
+                at = slice(r0 + STEP * (2 - a), r0 + STEP * (2 - a) + block)
+                window = jnp.concatenate(
+                    [
+                        jnp.concatenate([gc[s, at, :half, :ch], ht[1, s, at]], axis=1),
+                        gc[s, at, :, ch : 2 * ch],
+                        jnp.concatenate([ht[0, s, at], gc[s, at, half:, 2 * ch :]], axis=1),
+                    ],
+                    axis=2,
+                )
+                term = dot(window.reshape(block * cols, 3 * ch), wt_ref[a])
+                acc = term if acc is None else acc + term
             cot = cot_ref[s, r0 : r0 + block].reshape(block * cols, ch).astype(F32)
             ig = (cot + acc).astype(BF16).reshape(block, cols, ch)
             ig_ref[s, r0 : r0 + block] = ig * mk[s, r0 : r0 + block]
-        stores += start_all(
-            [pltpu.make_async_copy(ig_ref.at[s], ig_hbm.at[s], sems.at[slots + s])]
-        )
+        stores += start_all([pltpu.make_async_copy(ig_ref.at[s], ig_hbm.at[s], sems.at[s])])
     for copy in stores:
         copy.wait()
 
@@ -535,18 +548,34 @@
 
     grad_across, grad_pair = swap_halos(grad_across, grad_pair)
 
-    def input_grad_call(grad_edge):
+    def gradient_call(grad_edge):
+        return pl.pallas_call(
+            gradient_kernel,
+            out_shape=(
+                shape_bf16(*field),
+                shape_bf16(slots, rows + 2 * STEP, cols, 3 * ch),
+                shape_bf16(*field),
+                shape_bf16(3, 3 * ch, ch),
+            ),
+            in_specs=[SMEM] + [VMEM] * 6,
+            out_specs=(HBM, VMEM, VMEM, VMEM),
+            scratch_shapes=[pltpu.VMEM(field, BF16), pltpu.SemaphoreType.DMA((slots,))],
+            compiler_params=params,
+            cost_estimate=pl.CostEstimate(flops=1 << 31, bytes_accessed=0, transcendentals=0),
+            name="gradient",
+        )(neighbours, grad_inner, out_inner, grad_edge, out_edge, ocean, taps)
+
+    def input_grad_call(shifted, masks, turned_taps):
         return pl.pallas_call(
             input_grad_kernel,
-            out_shape=(shape_bf16(*field), shape_bf16(*field)),
-            in_specs=[SMEM] + [VMEM] * 9,
-            out_specs=(HBM, HBM),
-            scratch_shapes=[pltpu.VMEM(field, BF16)] * 2
-            + [
-                pltpu.VMEM((slots, rows + 2 * STEP, cols, 3 * ch), BF16),
+            out_shape=shape_bf16(*field),
+            in_specs=[SMEM] + [VMEM] * 6,
+            out_specs=HBM,
+            scratch_shapes=[
                 pltpu.VMEM(field, BF16),
                 pltpu.VMEM((2, slots, rows, cols // 2, ch), BF16),
-                pltpu.SemaphoreType.DMA((2 * slots,)),
+                pltpu.VMEM((2, slots, rows + 2 * STEP, cols // 2, ch), BF16),
+                pltpu.SemaphoreType.DMA((slots,)),
             ],
             compiler_params=params,
             cost_estimate=pl.CostEstimate(
@@ -555,15 +584,13 @@
                 transcendentals=0,
             ),
             name="input_grad",
-        )(
-            neighbours, grad_inner, out_inner, grad_edge, out_edge,
-            grad_across, grad_pair, cot_in, taps, ocean,
-        )
+        )(neighbours, shifted, masks, grad_across, grad_pair, cot_in, turned_taps)
 
     scale_factor = 1.0 / (rows * math.sqrt(slots * count))
     if own is None:
         summed = scatter_sum(dw, device)
-        return *input_grad_call(grad_edge), summed * scale_factor
+        layer_output, shifted, masks, turned_taps = gradient_call(grad_edge)
+        return layer_output, input_grad_call(shifted, masks, turned_taps), summed * scale_factor
 
     wide = 9 * ch
     recv = permute(dw, lambda i, n: i ^ 1)
@@ -585,17 +612,20 @@
         "middle_terms", keep.reshape(whole), recv.reshape(whole),
     )
     recvs = [permute(sends[k - 1], lambda i, n, k=k: i ^ (k * 2)) for k in range(1, middle)]
+    keep, grad_edge = lax.optimization_barrier((keep, grad_edge))
+    layer_output, shifted, masks, turned_taps = gradient_call(grad_edge)
+    keep, *recvs, shifted = lax.optimization_barrier((keep, *recvs, shifted))
     keep, *sends = small_call(
         functools.partial(split_kernel, 2 * middle),
         (shape_f32(1, own, wide), *[shape_bf16(1, own, wide)] * (outer - 1)),
         "outer_terms", keep[None], *[recv[None] for recv in recvs],
     )
-    keep, grad_edge = lax.optimization_barrier((keep, grad_edge))
+    keep, shifted = lax.optimization_barrier((keep, shifted))
     recvs = [
         permute(sends[k - 1], lambda i, n, k=k: i ^ (k * 2 * middle))
         for k in reversed(range(1, outer))
     ]
-    layer_output, input_grad = input_grad_call(grad_edge)
+    input_grad = input_grad_call(shifted, masks, turned_taps)
     (summed,) = small_call(
         functools.partial(last_kernel, scale_factor),
         (shape_f32(1, own, wide),),

time: 39.5 us -> 38.7 us (0.980)
  waiting for transfers between devices: 7.91 us -> 5.75 us
  Pallas kernels: 17.2 us -> 18.6 us
    ppermute x9, waiting for transfers between devices: 7.91 us -> 5.75 us  [permute(): lax.ppermute(value, 'tiles', [(i, pairs_of(i, count)) for i in range(coun...]
    pallas_call x1 -> x2, Pallas kernels: 5.08 us -> 6.47 us  [the longest x1 4.32 us: input_grad_call(): pl.pallas_call(input_grad_kernel, out_shape=shape_bf16(*field), in_specs=...]
  transfers between devices with their start and end apart: 9 -> 9, of which waited for: 2 -> 2; matrix products, arithmetic and copies ran while one was open for 0% -> 0% of each run, Pallas kernels for 32% -> 36%
where the time goes in v4:
time: 38.7 us; the launch traced here: 38.6 us
  Pallas kernels  18.6 us (48%)
  starting transfers between devices  12.7 us (33%)
  waiting for transfers between devices  5.75 us (15%)
  local copies, waits for them, and re-layouts  0.76 us (2%)
  between operations  0.75 us (2%)
    ppermute x9, starting transfers between devices, permute(): lax.ppermute(value, 'tiles', [(i, pairs_of(i, count)) for i in range(coun...  12.7 us
    pallas_call x1, Pallas kernels, shards(): pl.pallas_call(functools.partial(interior_kernel, own), out_shape=(shape_...  5.75 us
    ppermute x9, waiting for transfers between devices, permute(): lax.ppermute(value, 'tiles', [(i, pairs_of(i, count)) for i in range(coun...  5.75 us
    pallas_call x1, Pallas kernels, input_grad_call(): pl.pallas_call(input_grad_kernel, out_shape=shape_bf16(*field), in_specs=...  4.32 us
    pallas_call x1, Pallas kernels, gradient_call(): pl.pallas_call(gradient_kernel, out_shape=(shape_bf16(*field), shape_bf16...  2.15 us
    pallas_call x1, Pallas kernels, shards(): pl.pallas_call(load_kernel, out_shape=(shape_bf16(*side_columns), shape_b...  2.11 us
    pallas_call x1, Pallas kernels, shards(): pl.pallas_call(functools.partial(edge_kernel, own), out_shape=(shape_bf16...  1.79 us
    pallas_call x1, Pallas kernels, shards(): pl.pallas_call(keep_kernel, out_shape=(shape_f32(rank, wide),), in_specs=...  1.56 us
  transfers between devices with their start and end apart: 9, of which 2 were waited for; matrix products, arithmetic and copies ran while one was open for 0% of the time, Pallas kernels for 36%

profile of v4, /device:TPU:0, one launch (start us, length us, event | category | flops | bytes accessed | tf_op | source)
XLA Modules:
  0.0 38.6 jit_solution(8435006306839959524)
XLA Ops:
  0.6 0.0 copy-start.1
  0.6 0.7 %copy-done.1 = s32[2,32,32]{2,1,0:T(8,128)S(1)} copy-done((s32[2,32,32]{2,1,0:T(8,128)S(1)}, s32[2,32,32]{2,1,0:T(8,128)}, u32[]{:S(2)}) %copy-start.1) | copy-done | bytes 8216
  1.4 0.0 copy-start
  1.4 0.0 copy-start.2
  1.4 2.1 %load.1 = (bf16[2,2,32,256]{3,2,1,0:T(8,128)(2,1)S(1)}, bf16[2,2,32,256]{3,2,1,0:T(8,128)(2,1)S(1)}, bf16[2,8,32,256]{3,2,1,0:T(8,128)(2,1)S(1)}, bf16[2,2,2,32,...) custom-call(bf16[2,32,32,256]{3,2,1,0:T(8,128)(2,1)} %x_hbm.1, ...), custom_call_target="tpu_custom_call" | custom-call | tf_op jit(solution)/shard_map/load/pallas_call | solution.py:489
  3.5 5.5 %collective-permute-start = (bf16[2,2,32,256]{3,2,1,0:T(8,128)(2,1)S(1)}, bf16[2,2,32,256]{3,2,1,0:T(8,128)(2,1)S(1)}, u32[]{:S(2)}, u32[]{:S(2)}) collective-permute-start(bf16[2,2,32,256]{3,2,1,0:T(8,128)(2,1)S(1)} %get-tuple-element.46), channel_id=1, source_target_pairs={{0,15},{1,2},{2,1},{3,4},{4,3},{5,6},{6,5},{7,8},{8,7},{9,10},{10,... | collective-permute-start | bytes 196616 | tf_op jit(solution)/shard_map/ppermute | solution.py:397
  9.0 0.0 collective-permute-start.1
  9.0 0.0 copy-done
  9.0 0.0 copy-done.2
  9.0 5.8 %interior.1 = (bf16[2,32,32,256]{3,2,1,0:T(8,128)(2,1)S(1)}, bf16[2,32,32,256]{3,2,1,0:T(8,128)(2,1)S(1)}, f32[128,2304]{1,0:T(8,128)S(1)}, bf16[2,36,32,768]{3,...) custom-call(s32[2,8]{1,0:T(2,128)S(1)} %copy-done.2, bf16[2,32,32,256]{3,2,1,0:T(8,128)(2,1)S(1)} %get-tuple-element.39.x_ref, ...), custom_call_target="tpu_custom_call" | custom-call | flops 4831838208 | bytes 8388608 | tf_op jit(solution)/shard_map/interior/pallas_call | solution.py:509
  14.8 0.0 collective-permute-done.across_ref
  14.8 0.0 collective-permute-done.1.pair_ref
  14.8 1.8 %edges.1 = (bf16[2,2,32,256]{3,2,1,0:T(8,128)(2,1)S(1)}, bf16[2,2,32,256]{3,2,1,0:T(8,128)(2,1)S(1)}, bf16[2,2,2,32,256]{4,3,2,1,0:T(8,128)(2,1)S(1)}, bf16[2,2,...) custom-call(s32[2,8]{1,0:T(2,128)S(1)} %copy-done.2, ...), custom_call_target="tpu_custom_call" | custom-call | flops 603979776 | bytes 6291456 | tf_op jit(solution)/shard_map/edges/pallas_call | solution.py:528
  16.6 0.6 %collective-permute-start.2 = (bf16[128,2304]{1,0:T(8,128)(2,1)S(1)}, bf16[128,2304]{1,0:T(8,128)(2,1)S(1)}, u32[]{:S(2)}, u32[]{:S(2)}) collective-permute-start(bf16[128,2304]{1,0:T(8,128)(2,1)S(1)} %get-tuple-element.53), channel_id=1, source_target_pairs={{0,1},{1,0},{2,3},{3,2},{4,5},{5,4},{6,7},{7,6},{8,9},{9,8},{10,11... | collective-permute-start | bytes 1769480 | tf_op jit(solution)/shard_map/ppermute | solution.py:397
  17.2 1.6 %keep.1 = f32[128,2304]{1,0:T(8,128)S(1)} custom-call(bf16[2,36,32,768]{3,2,1,0:T(8,128)(2,1)S(1)} %get-tuple-element.44.xc, bf16[2,256,1024]{2,1,0:T(8,128)(2,1)S(1)} %get-tuple-element.45.gt, bf16[3,2,2,2,32,768]{5,4,3,2,1,0:T(8,128)(2,1)S(1)} %get-tuple-element.51.win, bf16[256,256]{1,0:T(8,128)(2,1)S(1)} %get-tuple-element.52.edge_gt), custom_call_target="tpu_custom_call" | custom-call | flops 1358954496 | tf_op jit(solution)/shard_map/keep/pallas_call | solution.py:597
  18.7 0.1 collective-permute-done.2
  18.8 0.1 middle_terms.1
  18.9 0.1 collective-permute-start.3
  19.0 2.0 %collective-permute-start.4 = (bf16[2,2,32,256]{3,2,1,0:T(8,128)(2,1)S(1)}, bf16[2,2,32,256]{3,2,1,0:T(8,128)(2,1)S(1)}, u32[]{:S(2)}, u32[]{:S(2)}) collective-permute-start(bf16[2,2,32,256]{3,2,1,0:T(8,128)(2,1)S(1)} %get-tuple-element.68), channel_id=1, source_target_pairs={{0,15},{1,2},{2,1},{3,4},{4,3},{5,6},{6,5},{7,8},{8,7},{9,10},{10,... | collective-permute-start | bytes 196616 | tf_op jit(solution)/shard_map/ppermute | solution.py:397
  21.0 0.1 collective-permute-start.5
  21.1 2.2 %gradient.1 = (bf16[2,32,32,256]{3,2,1,0:T(8,128)(2,1)}, bf16[2,36,32,768]{3,2,1,0:T(8,128)(2,1)S(1)}, bf16[2,32,32,256]{3,2,1,0:T(8,128)(2,1)S(1)}, bf16[3,768,256]{2,1,0:T(8,128)(2,1)S(1)}) custom-call(s32[2,8]{1,0:T(2,128)S(1)} %copy-done.2, bf16[2,32,32,256]{3,2,1,0:T(8,128)(2,1)S(1)} %get-tuple-element.42.gi_ref, ...), custom_call_target="tpu_custom_call" | custom-call | flops 2147483648 | tf_op jit(solution)/shard_map/gradient/pallas_call | solution.py:552
  23.3 5.7 %collective-permute-done.3 = bf16[4,16,2304]{2,1,0:T(8,128)(2,1)S(1)} collective-permute-done((bf16[4,16,2304]{2,1,0:T(8,128)(2,1)S(1)}, bf16[4,16,2304]{2,1,0:T(8,128)(2,1)S(1)}, u32[]{:S(2)}, u32[]{:S(2)}) %collective-permute-start.3) | collective-permute-done | bytes 294944 | tf_op jit(solution)/shard_map/ppermute | solution.py:397
  29.0 0.1 outer_terms.1
  29.0 0.9 %collective-permute-start.6 = (bf16[1,16,2304]{2,1,0:T(8,128)(2,1)S(1)}, bf16[1,16,2304]{2,1,0:T(8,128)(2,1)S(1)}, u32[]{:S(2)}, u32[]{:S(2)}) collective-permute-start(bf16[1,16,2304]{2,1,0:T(8,128)(2,1)S(1)} %get-tuple-element.72), channel_id=1, source_target_pairs={{0,12},{1,13},{2,14},{3,15},{4,8},{5,9},{6,10},{7,11},{8,4},{9,5},... | collective-permute-start | bytes 221192 | tf_op jit(solution)/shard_map/ppermute | solution.py:397
  30.0 0.0 collective-permute-start.7
  30.0 3.5 %collective-permute-start.8 = (bf16[1,16,2304]{2,1,0:T(8,128)(2,1)S(1)}, bf16[1,16,2304]{2,1,0:T(8,128)(2,1)S(1)}, u32[]{:S(2)}, u32[]{:S(2)}) collective-permute-start(bf16[1,16,2304]{2,1,0:T(8,128)(2,1)S(1)} %get-tuple-element.74), channel_id=1, source_target_pairs={{0,4},{1,5},{2,6},{3,7},{4,0},{5,1},{6,2},{7,3},{8,12},{9,13},{10,... | collective-permute-start | bytes 221192 | tf_op jit(solution)/shard_map/ppermute | solution.py:397
  33.5 0.0 collective-permute-done.4.across_ref
  33.5 0.0 collective-permute-done.5.pair_ref
  33.5 4.3 %input_grad.1 = bf16[2,32,32,256]{3,2,1,0:T(8,128)(2,1)} custom-call(s32[2,8]{1,0:T(2,128)S(1)} %copy-done.2, bf16[2,36,32,768]{3,2,1,0:T(8,128)(2,1)S(1)} %get-tuple-element.66.gc, bf16[2,32,32,256]{3,2,1,0:T(8,128)(2,1)S(1)} %get-tuple-element.67.mk, bf16[2,2,32,256]{3,2,1,0:T(8,128)(2,1)S(1)} %collective-permute-done.4.across_ref, ...), custom_call_target="tpu_custom_call" | custom-call | flops 2415919104 | bytes 8388608 | tf_op jit(solution)/shard_map/input_grad/pallas_call | solution.py:569
  37.8 0.0 collective-permute-done.6.refs_0_
  37.8 0.0 collective-permute-done.7.refs_1_
  37.8 0.0 collective-permute-done.8.refs_2_
  37.9 0.7 %last_sum.1 = f32[1,16,2304]{2,1,0:T(8,128)} custom-call(f32[1,16,2304]{2,1,0:T(8,128)S(1)} %get-tuple-element.71.keep_ref, bf16[1,16,2304]{2,1,0:T(8,128)(2,1)S(1)} %collective-permute-done.6.refs_0_, bf16[1,16,2304]{2,1,0:T(8,128)(2,1)S(1)} %collective-permute-done.7.refs_1_, bf16[1,16,2304]{2,1,0:T(8,128)(2,1)S(1)} %collective-permute-done.8.refs_2_), custom_call_target="tpu_custom_call" | custom-call | tf_op jit(solution)/shard_map/last_sum/pallas_call | solution.py:460
Async XLA Ops:
  0.6 0.8 %copy-start.1 = (s32[2,32,32]{2,1,0:T(8,128)S(1)}, s32[2,32,32]{2,1,0:T(8,128)}, u32[]{:S(2)}) copy-start(s32[2,32,32]{2,1,0:T(8,128)} %mask_hbm.1) | copy-start | bytes 24580
  1.4 7.6 %copy-start = (bf16[9,256,256]{2,1,0:T(8,128)(2,1)S(1)}, bf16[9,256,256]{2,1,0:T(8,128)(2,1)}, u32[]{:S(2)}) copy-start(bf16[9,256,256]{2,1,0:T(8,128)(2,1)} %param.7) | copy-start | bytes 3538948
  1.4 7.6 %copy-start.2 = (s32[2,8]{1,0:T(2,128)S(1)}, s32[2,8]{1,0:T(2,128)}, u32[]{:S(2)}) copy-start(s32[2,8]{1,0:T(2,128)} %nbr_ref.7) | copy-start | bytes 196
  3.5 11.3 %collective-permute-start = (bf16[2,2,32,256]{3,2,1,0:T(8,128)(2,1)S(1)}, bf16[2,2,32,256]{3,2,1,0:T(8,128)(2,1)S(1)}, u32[]{:S(2)}, u32[]{:S(2)}) collective-permute-start(bf16[2,2,32,256]{3,2,1,0:T(8,128)(2,1)S(1)} %get-tuple-element.46), channel_id=1, source_target_pairs={{0,15},{1,2},{2,1},{3,4},{4,3},{5,6},{6,5},{7,8},{8,7},{9,10},{10,... | collective-permute-start | bytes 196616 | tf_op jit(solution)/shard_map/ppermute | solution.py:397
  9.0 5.8 %collective-permute-start.1 = (bf16[2,2,32,256]{3,2,1,0:T(8,128)(2,1)S(1)}, bf16[2,2,32,256]{3,2,1,0:T(8,128)(2,1)S(1)}, u32[]{:S(2)}, u32[]{:S(2)}) collective-permute-start(bf16[2,2,32,256]{3,2,1,0:T(8,128)(2,1)S(1)} %get-tuple-element.47), channel_id=1, source_target_pairs={{0,1},{1,0},{2,3},{3,2},{4,5},{5,4},{6,7},{7,6},{8,9},{9,8},{10,11... | collective-permute-start | bytes 196616 | tf_op jit(solution)/shard_map/ppermute | solution.py:397
  16.6 2.2 %collective-permute-start.2 = (bf16[128,2304]{1,0:T(8,128)(2,1)S(1)}, bf16[128,2304]{1,0:T(8,128)(2,1)S(1)}, u32[]{:S(2)}, u32[]{:S(2)}) collective-permute-start(bf16[128,2304]{1,0:T(8,128)(2,1)S(1)} %get-tuple-element.53), channel_id=1, source_target_pairs={{0,1},{1,0},{2,3},{3,2},{4,5},{5,4},{6,7},{7,6},{8,9},{9,8},{10,11... | collective-permute-start | bytes 1769480 | tf_op jit(solution)/shard_map/ppermute | solution.py:397
  18.9 10.1 %collective-permute-start.3 = (bf16[4,16,2304]{2,1,0:T(8,128)(2,1)S(1)}, bf16[4,16,2304]{2,1,0:T(8,128)(2,1)S(1)}, u32[]{:S(2)}, u32[]{:S(2)}) collective-permute-start(bf16[4,16,2304]{2,1,0:T(8,128)(2,1)S(1)} %get-tuple-element.60), channel_id=1, source_target_pairs={{0,2},{1,3},{2,0},{3,1},{4,6},{5,7},{6,4},{7,5},{8,10},{9,11},{10,... | collective-permute-start | bytes 884744 | tf_op jit(solution)/shard_map/ppermute | solution.py:397
  19.0 14.5 %collective-permute-start.4 = (bf16[2,2,32,256]{3,2,1,0:T(8,128)(2,1)S(1)}, bf16[2,2,32,256]{3,2,1,0:T(8,128)(2,1)S(1)}, u32[]{:S(2)}, u32[]{:S(2)}) collective-permute-start(bf16[2,2,32,256]{3,2,1,0:T(8,128)(2,1)S(1)} %get-tuple-element.68), channel_id=1, source_target_pairs={{0,15},{1,2},{2,1},{3,4},{4,3},{5,6},{6,5},{7,8},{8,7},{9,10},{10,... | collective-permute-start | bytes 196616 | tf_op jit(solution)/shard_map/ppermute | solution.py:397
  21.0 12.5 %collective-permute-start.5 = (bf16[2,2,32,256]{3,2,1,0:T(8,128)(2,1)S(1)}, bf16[2,2,32,256]{3,2,1,0:T(8,128)(2,1)S(1)}, u32[]{:S(2)}, u32[]{:S(2)}) collective-permute-start(bf16[2,2,32,256]{3,2,1,0:T(8,128)(2,1)S(1)} %get-tuple-element.69), channel_id=1, source_target_pairs={{0,1},{1,0},{2,3},{3,2},{4,5},{5,4},{6,7},{7,6},{8,9},{9,8},{10,11... | collective-permute-start | bytes 196616 | tf_op jit(solution)/shard_map/ppermute | solution.py:397
  29.0 8.8 %collective-permute-start.6 = (bf16[1,16,2304]{2,1,0:T(8,128)(2,1)S(1)}, bf16[1,16,2304]{2,1,0:T(8,128)(2,1)S(1)}, u32[]{:S(2)}, u32[]{:S(2)}) collective-permute-start(bf16[1,16,2304]{2,1,0:T(8,128)(2,1)S(1)} %get-tuple-element.72), channel_id=1, source_target_pairs={{0,12},{1,13},{2,14},{3,15},{4,8},{5,9},{6,10},{7,11},{8,4},{9,5},... | collective-permute-start | bytes 221192 | tf_op jit(solution)/shard_map/ppermute | solution.py:397
  30.0 7.9 %collective-permute-start.7 = (bf16[1,16,2304]{2,1,0:T(8,128)(2,1)S(1)}, bf16[1,16,2304]{2,1,0:T(8,128)(2,1)S(1)}, u32[]{:S(2)}, u32[]{:S(2)}) collective-permute-start(bf16[1,16,2304]{2,1,0:T(8,128)(2,1)S(1)} %get-tuple-element.73), channel_id=1, source_target_pairs={{0,8},{1,9},{2,10},{3,11},{4,12},{5,13},{6,14},{7,15},{8,0},{9,1},... | collective-permute-start | bytes 221192 | tf_op jit(solution)/shard_map/ppermute | solution.py:397
  30.0 7.9 %collective-permute-start.8 = (bf16[1,16,2304]{2,1,0:T(8,128)(2,1)S(1)}, bf16[1,16,2304]{2,1,0:T(8,128)(2,1)S(1)}, u32[]{:S(2)}, u32[]{:S(2)}) collective-permute-start(bf16[1,16,2304]{2,1,0:T(8,128)(2,1)S(1)} %get-tuple-element.74), channel_id=1, source_target_pairs={{0,4},{1,5},{2,6},{3,7},{4,0},{5,1},{6,2},{7,3},{8,12},{9,13},{10,... | collective-permute-start | bytes 221192 | tf_op jit(solution)/shard_map/ppermute | solution.py:397

commit v5 on v4

--- a/solution.py
+++ b/solution.py
@@ -14,7 +14,7 @@
 GELU_SCALE = math.sqrt(2.0 / math.pi)
 GELU_CUBIC = 0.044715
 VMEM_BYTES = 16 << 20
-LOAD_BYTES = 101 << 19
+LOAD_BYTES = 102 << 19
 
 SMEM = pl.BlockSpec(memory_space=pltpu.SMEM)
 VMEM = pl.BlockSpec(memory_space=pltpu.VMEM)
@@ -83,18 +83,13 @@
     return jnp.where(even, across, pair), jnp.where(even, pair, across)
 
 
-def load_kernel(
-    x_hbm, cot_hbm, mask_hbm,
-    across_ref, pair_ref, xe_ref, cote_ref, x_ref, cot_ref, ms,
-    sems,
-):
+def load_kernel(x_hbm, cot_hbm, xe_ref, cote_ref, x_ref, cot_ref, sems):
     slots, rows, cols, ch = x_ref.shape
     half = cols // 2
-    mask_in = start_all([pltpu.make_async_copy(mask_hbm, ms, sems.at[0])])
     x_in, cot_in = (
         start_all(
             [
-                pltpu.make_async_copy(src.at[s], dst.at[s], sems.at[1 + i * slots + s])
+                pltpu.make_async_copy(src.at[s], dst.at[s], sems.at[i * slots + s])
                 for s in range(slots)
             ]
         )
@@ -104,33 +99,35 @@
         edge_selector(rows, half, list(range(0, 4))),
         edge_selector(rows, half, list(range(half - 4, half))),
     ]
-    mask_in[0].wait()
-    oceans = {}
-    for s in range(slots):
-        mask = ms[s].astype(F32)
-        for side in range(2):
-            lo = 0 if side == 0 else cols - 4
-            oceans[s, side] = jnp.stack(
-                [
-                    jnp.broadcast_to(mask[:, lo + k : lo + k + 1], (rows, ch)).astype(BF16)
-                    for k in range(4)
-                ]
-            )
     for s in range(slots):
         x_in[s].wait()
         for side in range(2):
             tiles = slice(side * half, side * half + half)
             x = dot(sel[side], x_ref[s, :, tiles].reshape(rows * half, ch)).astype(BF16)
-            xe_ref[s, side * 4 : side * 4 + 4] = x.reshape(4, rows, ch) * oceans[s, side]
-    split_sides(xe_ref[:, 0:2], xe_ref[:, 6:8], across_ref, pair_ref)
+            xe_ref[s, side * 4 : side * 4 + 4] = x.reshape(4, rows, ch)
     for s in range(slots):
         cot_in[s].wait()
         for side in range(2):
             tiles = slice(side * half, side * half + half)
-            outer = slice(0, 2) if side == 0 else slice(2, 4)
             pick = sel[side][: 2 * rows] if side == 0 else sel[side][2 * rows :]
             c = dot(pick, cot_ref[s, :, tiles].reshape(rows * half, ch)).astype(BF16)
-            cote_ref[side, s] = c.reshape(2, rows, ch) * oceans[s, side][outer]
+            cote_ref[side, s] = c.reshape(2, rows, ch)
+
+
+def mask_kernel(raw_ref, raw_cot_ref, ms, across_ref, pair_ref, xe_ref, cote_ref):
+    slots, _, rows, ch = raw_ref.shape
+    cols = ms.shape[2]
+    for s in range(slots):
+        mask = ms[s].astype(F32)
+        for side in range(2):
+            for k in range(4):
+                at = k if side == 0 else cols - 4 + k
+                ocean = jnp.broadcast_to(mask[:, at : at + 1], (rows, ch)).astype(BF16)
+                xe_ref[s, side * 4 + k] = raw_ref[s, side * 4 + k] * ocean
+                outer = k if side == 0 else k - 2
+                if 0 <= outer < 2:
+                    cote_ref[side, s, outer] = raw_cot_ref[side, s, outer] * ocean
+    split_sides(xe_ref[:, 0:2], xe_ref[:, 6:8], across_ref, pair_ref)
 
 
 def interior_kernel(
@@ -486,23 +483,30 @@
     own = ch // count if ch // count % 16 == 0 else None
     outer, middle, _ = stage_sizes(count)
 
-    across, pair, x_edge, cot_edge, field_in, cot_in, ocean = pl.pallas_call(
+    raw_edge, raw_cot, field_in, cot_in = pl.pallas_call(
         load_kernel,
         out_shape=(
+            shape_bf16(slots, 8, rows, ch),
+            shape_bf16(2, *side_columns),
+            shape_bf16(*field),
+            shape_bf16(*field),
+        ),
+        in_specs=[HBM] * 2,
+        out_specs=(VMEM,) * 4,
+        scratch_shapes=[pltpu.SemaphoreType.DMA((2 * slots,))],
+        compiler_params=pltpu.CompilerParams(vmem_limit_bytes=LOAD_BYTES),
+        name="load",
+    )(input_field, cotangent)
+    across, pair, x_edge, cot_edge = small_call(
+        mask_kernel,
+        (
             shape_bf16(*side_columns),
             shape_bf16(*side_columns),
             shape_bf16(slots, 8, rows, ch),
             shape_bf16(2, *side_columns),
-            shape_bf16(*field),
-            shape_bf16(*field),
-            jax.ShapeDtypeStruct(land_mask.shape, jnp.int32),
-        ),
-        in_specs=[HBM] * 3,
-        out_specs=(VMEM,) * 7,
-        scratch_shapes=[pltpu.SemaphoreType.DMA((1 + 2 * slots,))],
-        compiler_params=pltpu.CompilerParams(vmem_limit_bytes=LOAD_BYTES),
-        name="load",
-    )(input_field, cotangent, land_mask)
+        ),
+        "mask_edges", raw_edge, raw_cot, land_mask,
+    )
     across, pair = swap_halos(across, pair)
 
     rank = ch if own is None else ch // 2
@@ -523,7 +527,7 @@
             flops=4 * 9 * slots * rows * cols * ch * ch, bytes_accessed=8 << 20, transcendentals=0
         ),
         name="interior",
-    )(neighbours, field_in, cot_in, taps, ocean)
+    )(neighbours, field_in, cot_in, taps, land_mask)
 
     grad_across, grad_pair, grad_edge, out_edge, dw, edge_windows, edge_turned = pl.pallas_call(
         functools.partial(edge_kernel, own),
@@ -563,7 +567,7 @@
             compiler_params=params,
             cost_estimate=pl.CostEstimate(flops=1 << 31, bytes_accessed=0, transcendentals=0),
             name="gradient",
-        )(neighbours, grad_inner, out_inner, grad_edge, out_edge, ocean, taps)
+        )(neighbours, grad_inner, out_inner, grad_edge, out_edge, land_mask, taps)
 
     def input_grad_call(shifted, masks, turned_taps):
         return pl.pallas_call(

time: 38.7 us -> 38.1 us (0.984)
  local copies, waits for them, and re-layouts: 0.76 us -> 0.01 us
    unnamed x6, local copies, waits for them, and re-layouts: 0.76 us -> 0.01 us
    pallas_call x3 -> x4, Pallas kernels: 0.88 us -> 1 us  [small_call(): pl.pallas_call(kernel, out_shape=out_shapes, in_specs=[VMEM] * len(args),...]
  transfers between devices with their start and end apart: 9 -> 9, of which waited for: 2 -> 2; matrix products, arithmetic and copies ran while one was open for 0% -> 0% of each run, Pallas kernels for 36% -> 37%
where the time goes in v5:
time: 38.1 us; the launch traced here: 37.9 us
  Pallas kernels  18.7 us (49%)
  starting transfers between devices  12.7 us (33%)
  waiting for transfers between devices  5.75 us (15%)
  between operations  0.77 us (2%)
    ppermute x9, starting transfers between devices, permute(): lax.ppermute(value, 'tiles', [(i, pairs_of(i, count)) for i in range(coun...  12.7 us
    pallas_call x1, Pallas kernels, shards(): pl.pallas_call(functools.partial(interior_kernel, own), out_shape=(shape_...  5.75 us
    ppermute x9, waiting for transfers between devices, permute(): lax.ppermute(value, 'tiles', [(i, pairs_of(i, count)) for i in range(coun...  5.75 us
    pallas_call x1, Pallas kernels, input_grad_call(): pl.pallas_call(input_grad_kernel, out_shape=shape_bf16(*field), in_specs=...  4.33 us
    pallas_call x1, Pallas kernels, gradient_call(): pl.pallas_call(gradient_kernel, out_shape=(shape_bf16(*field), shape_bf16...  2.15 us
    pallas_call x1, Pallas kernels, shards(): pl.pallas_call(load_kernel, out_shape=(shape_bf16(slots, 8, rows, ch), sh...  2.07 us
    pallas_call x1, Pallas kernels, shards(): pl.pallas_call(functools.partial(edge_kernel, own), out_shape=(shape_bf16...  1.8 us
    pallas_call x1, Pallas kernels, shards(): pl.pallas_call(keep_kernel, out_shape=(shape_f32(rank, wide),), in_specs=...  1.56 us
  transfers between devices with their start and end apart: 9, of which 2 were waited for; matrix products, arithmetic and copies ran while one was open for 0% of the time, Pallas kernels for 37%

profile of v5, /device:TPU:0, one launch (start us, length us, event | category | flops | bytes accessed | tf_op | source)
XLA Modules:
  0.0 37.9 jit_solution(15642657603931320022)
XLA Ops:
  0.6 0.0 copy-start.1
  0.6 0.0 copy-start.2
  0.7 0.0 copy-start
  0.7 2.1 %load.1 = (bf16[2,8,32,256]{3,2,1,0:T(8,128)(2,1)S(1)}, bf16[2,2,2,32,256]{4,3,2,1,0:T(8,128)(2,1)S(1)}, bf16[2,32,32,256]{3,2,1,0:T(8,128)(2,1)S(1)}, bf16[2,32,32,256]{3,2,1,0:T(8,128)(2,1)S(1)}) custom-call(bf16[2,32,32,256]{3,2,1,0:T(8,128)(2,1)} %x_hbm.1, bf16[2,32,32,256]{3,2,1,0:T(8,128)(2,1)} %cot_hbm.1), custom_call_target="tpu_custom_call" | custom-call | tf_op jit(solution)/shard_map/load/pallas_call | solution.py:486
  2.7 0.0 copy-done.1
  2.7 0.1 mask_edges.1
  2.9 5.5 %collective-permute-start = (bf16[2,2,32,256]{3,2,1,0:T(8,128)(2,1)S(1)}, bf16[2,2,32,256]{3,2,1,0:T(8,128)(2,1)S(1)}, u32[]{:S(2)}, u32[]{:S(2)}) collective-permute-start(bf16[2,2,32,256]{3,2,1,0:T(8,128)(2,1)S(1)} %get-tuple-element.48), channel_id=1, source_target_pairs={{0,15},{1,2},{2,1},{3,4},{4,3},{5,6},{6,5},{7,8},{8,7},{9,10},{10,... | collective-permute-start | bytes 196616 | tf_op jit(solution)/shard_map/ppermute | solution.py:394
  8.4 0.0 collective-permute-start.1
  8.4 0.0 copy-done.2
  8.4 0.0 copy-done
  8.4 5.8 %interior.1 = (bf16[2,32,32,256]{3,2,1,0:T(8,128)(2,1)S(1)}, bf16[2,32,32,256]{3,2,1,0:T(8,128)(2,1)S(1)}, f32[128,2304]{1,0:T(8,128)S(1)}, bf16[2,36,32,768]{3,...) custom-call(s32[2,8]{1,0:T(2,128)S(1)} %copy-done.2, bf16[2,32,32,256]{3,2,1,0:T(8,128)(2,1)S(1)} %get-tuple-element.40.x_ref, ...), custom_call_target="tpu_custom_call" | custom-call | flops 4831838208 | bytes 8388608 | tf_op jit(solution)/shard_map/interior/pallas_call | solution.py:513
  14.2 0.0 collective-permute-done.across_ref
  14.2 0.0 collective-permute-done.1.pair_ref
  14.2 1.8 %edges.1 = (bf16[2,2,32,256]{3,2,1,0:T(8,128)(2,1)S(1)}, bf16[2,2,32,256]{3,2,1,0:T(8,128)(2,1)S(1)}, bf16[2,2,2,32,256]{4,3,2,1,0:T(8,128)(2,1)S(1)}, bf16[2,2,...) custom-call(s32[2,8]{1,0:T(2,128)S(1)} %copy-done.2, ...), custom_call_target="tpu_custom_call" | custom-call | flops 603979776 | bytes 6291456 | tf_op jit(solution)/shard_map/edges/pallas_call | solution.py:532
  16.0 0.6 %collective-permute-start.2 = (bf16[128,2304]{1,0:T(8,128)(2,1)S(1)}, bf16[128,2304]{1,0:T(8,128)(2,1)S(1)}, u32[]{:S(2)}, u32[]{:S(2)}) collective-permute-start(bf16[128,2304]{1,0:T(8,128)(2,1)S(1)} %get-tuple-element.55), channel_id=1, source_target_pairs={{0,1},{1,0},{2,3},{3,2},{4,5},{5,4},{6,7},{7,6},{8,9},{9,8},{10,11... | collective-permute-start | bytes 1769480 | tf_op jit(solution)/shard_map/ppermute | solution.py:394
  16.5 1.6 %keep.1 = f32[128,2304]{1,0:T(8,128)S(1)} custom-call(bf16[2,36,32,768]{3,2,1,0:T(8,128)(2,1)S(1)} %get-tuple-element.44.xc, bf16[2,256,1024]{2,1,0:T(8,128)(2,1)S(1)} %get-tuple-element.45.gt, bf16[3,2,2,2,32,768]{5,4,3,2,1,0:T(8,128)(2,1)S(1)} %get-tuple-element.53.win, bf16[256,256]{1,0:T(8,128)(2,1)S(1)} %get-tuple-element.54.edge_gt), custom_call_target="tpu_custom_call" | custom-call | flops 1358954496 | tf_op jit(solution)/shard_map/keep/pallas_call | solution.py:601
  18.1 0.1 collective-permute-done.2
  18.2 0.1 middle_terms.1
  18.3 0.1 collective-permute-start.3
  18.4 2.0 %collective-permute-start.4 = (bf16[2,2,32,256]{3,2,1,0:T(8,128)(2,1)S(1)}, bf16[2,2,32,256]{3,2,1,0:T(8,128)(2,1)S(1)}, u32[]{:S(2)}, u32[]{:S(2)}) collective-permute-start(bf16[2,2,32,256]{3,2,1,0:T(8,128)(2,1)S(1)} %get-tuple-element.70), channel_id=1, source_target_pairs={{0,15},{1,2},{2,1},{3,4},{4,3},{5,6},{6,5},{7,8},{8,7},{9,10},{10,... | collective-permute-start | bytes 196616 | tf_op jit(solution)/shard_map/ppermute | solution.py:394
  20.4 0.1 collective-permute-start.5
  20.5 2.2 %gradient.1 = (bf16[2,32,32,256]{3,2,1,0:T(8,128)(2,1)}, bf16[2,36,32,768]{3,2,1,0:T(8,128)(2,1)S(1)}, bf16[2,32,32,256]{3,2,1,0:T(8,128)(2,1)S(1)}, bf16[3,768,256]{2,1,0:T(8,128)(2,1)S(1)}) custom-call(s32[2,8]{1,0:T(2,128)S(1)} %copy-done.2, bf16[2,32,32,256]{3,2,1,0:T(8,128)(2,1)S(1)} %get-tuple-element.42.gi_ref, ...), custom_call_target="tpu_custom_call" | custom-call | flops 2147483648 | tf_op jit(solution)/shard_map/gradient/pallas_call | solution.py:556
  22.7 5.7 %collective-permute-done.3 = bf16[4,16,2304]{2,1,0:T(8,128)(2,1)S(1)} collective-permute-done((bf16[4,16,2304]{2,1,0:T(8,128)(2,1)S(1)}, bf16[4,16,2304]{2,1,0:T(8,128)(2,1)S(1)}, u32[]{:S(2)}, u32[]{:S(2)}) %collective-permute-start.3) | collective-permute-done | bytes 294944 | tf_op jit(solution)/shard_map/ppermute | solution.py:394
  28.3 0.1 outer_terms.1
  28.4 0.9 %collective-permute-start.6 = (bf16[1,16,2304]{2,1,0:T(8,128)(2,1)S(1)}, bf16[1,16,2304]{2,1,0:T(8,128)(2,1)S(1)}, u32[]{:S(2)}, u32[]{:S(2)}) collective-permute-start(bf16[1,16,2304]{2,1,0:T(8,128)(2,1)S(1)} %get-tuple-element.74), channel_id=1, source_target_pairs={{0,12},{1,13},{2,14},{3,15},{4,8},{5,9},{6,10},{7,11},{8,4},{9,5},... | collective-permute-start | bytes 221192 | tf_op jit(solution)/shard_map/ppermute | solution.py:394
  29.4 0.0 collective-permute-start.7
  29.4 3.5 %collective-permute-start.8 = (bf16[1,16,2304]{2,1,0:T(8,128)(2,1)S(1)}, bf16[1,16,2304]{2,1,0:T(8,128)(2,1)S(1)}, u32[]{:S(2)}, u32[]{:S(2)}) collective-permute-start(bf16[1,16,2304]{2,1,0:T(8,128)(2,1)S(1)} %get-tuple-element.76), channel_id=1, source_target_pairs={{0,4},{1,5},{2,6},{3,7},{4,0},{5,1},{6,2},{7,3},{8,12},{9,13},{10,... | collective-permute-start | bytes 221192 | tf_op jit(solution)/shard_map/ppermute | solution.py:394
  32.9 0.0 collective-permute-done.4.across_ref
  32.9 0.0 collective-permute-done.5.pair_ref
  32.9 4.3 %input_grad.1 = bf16[2,32,32,256]{3,2,1,0:T(8,128)(2,1)} custom-call(s32[2,8]{1,0:T(2,128)S(1)} %copy-done.2, bf16[2,36,32,768]{3,2,1,0:T(8,128)(2,1)S(1)} %get-tuple-element.68.gc, bf16[2,32,32,256]{3,2,1,0:T(8,128)(2,1)S(1)} %get-tuple-element.69.mk, bf16[2,2,32,256]{3,2,1,0:T(8,128)(2,1)S(1)} %collective-permute-done.4.across_ref, ...), custom_call_target="tpu_custom_call" | custom-call | flops 2415919104 | bytes 8388608 | tf_op jit(solution)/shard_map/input_grad/pallas_call | solution.py:573
  37.2 0.0 collective-permute-done.6.refs_0_
  37.2 0.0 collective-permute-done.7.refs_1_
  37.2 0.0 collective-permute-done.8.refs_2_
  37.2 0.7 %last_sum.1 = f32[1,16,2304]{2,1,0:T(8,128)} custom-call(f32[1,16,2304]{2,1,0:T(8,128)S(1)} %get-tuple-element.73.keep_ref, bf16[1,16,2304]{2,1,0:T(8,128)(2,1)S(1)} %collective-permute-done.6.refs_0_, bf16[1,16,2304]{2,1,0:T(8,128)(2,1)S(1)} %collective-permute-done.7.refs_1_, bf16[1,16,2304]{2,1,0:T(8,128)(2,1)S(1)} %collective-permute-done.8.refs_2_), custom_call_target="tpu_custom_call" | custom-call | tf_op jit(solution)/shard_map/last_sum/pallas_call | solution.py:457
Async XLA Ops:
  0.6 2.1 %copy-start.1 = (s32[2,32,32]{2,1,0:T(8,128)S(1)}, s32[2,32,32]{2,1,0:T(8,128)}, u32[]{:S(2)}) copy-start(s32[2,32,32]{2,1,0:T(8,128)} %mask_ref.1) | copy-start | bytes 24580
  0.6 7.8 %copy-start.2 = (s32[2,8]{1,0:T(2,128)S(1)}, s32[2,8]{1,0:T(2,128)}, u32[]{:S(2)}) copy-start(s32[2,8]{1,0:T(2,128)} %nbr_ref.7) | copy-start | bytes 196
  0.7 7.7 %copy-start = (bf16[9,256,256]{2,1,0:T(8,128)(2,1)S(1)}, bf16[9,256,256]{2,1,0:T(8,128)(2,1)}, u32[]{:S(2)}) copy-start(bf16[9,256,256]{2,1,0:T(8,128)(2,1)} %param.7) | copy-start | bytes 3538948
  2.9 11.3 %collective-permute-start = (bf16[2,2,32,256]{3,2,1,0:T(8,128)(2,1)S(1)}, bf16[2,2,32,256]{3,2,1,0:T(8,128)(2,1)S(1)}, u32[]{:S(2)}, u32[]{:S(2)}) collective-permute-start(bf16[2,2,32,256]{3,2,1,0:T(8,128)(2,1)S(1)} %get-tuple-element.48), channel_id=1, source_target_pairs={{0,15},{1,2},{2,1},{3,4},{4,3},{5,6},{6,5},{7,8},{8,7},{9,10},{10,... | collective-permute-start | bytes 196616 | tf_op jit(solution)/shard_map/ppermute | solution.py:394
  8.4 5.8 %collective-permute-start.1 = (bf16[2,2,32,256]{3,2,1,0:T(8,128)(2,1)S(1)}, bf16[2,2,32,256]{3,2,1,0:T(8,128)(2,1)S(1)}, u32[]{:S(2)}, u32[]{:S(2)}) collective-permute-start(bf16[2,2,32,256]{3,2,1,0:T(8,128)(2,1)S(1)} %get-tuple-element.49), channel_id=1, source_target_pairs={{0,1},{1,0},{2,3},{3,2},{4,5},{5,4},{6,7},{7,6},{8,9},{9,8},{10,11... | collective-permute-start | bytes 196616 | tf_op jit(solution)/shard_map/ppermute | solution.py:394
  16.0 2.2 %collective-permute-start.2 = (bf16[128,2304]{1,0:T(8,128)(2,1)S(1)}, bf16[128,2304]{1,0:T(8,128)(2,1)S(1)}, u32[]{:S(2)}, u32[]{:S(2)}) collective-permute-start(bf16[128,2304]{1,0:T(8,128)(2,1)S(1)} %get-tuple-element.55), channel_id=1, source_target_pairs={{0,1},{1,0},{2,3},{3,2},{4,5},{5,4},{6,7},{7,6},{8,9},{9,8},{10,11... | collective-permute-start | bytes 1769480 | tf_op jit(solution)/shard_map/ppermute | solution.py:394
  18.3 10.1 %collective-permute-start.3 = (bf16[4,16,2304]{2,1,0:T(8,128)(2,1)S(1)}, bf16[4,16,2304]{2,1,0:T(8,128)(2,1)S(1)}, u32[]{:S(2)}, u32[]{:S(2)}) collective-permute-start(bf16[4,16,2304]{2,1,0:T(8,128)(2,1)S(1)} %get-tuple-element.62), channel_id=1, source_target_pairs={{0,2},{1,3},{2,0},{3,1},{4,6},{5,7},{6,4},{7,5},{8,10},{9,11},{10,... | collective-permute-start | bytes 884744 | tf_op jit(solution)/shard_map/ppermute | solution.py:394
  18.4 14.5 %collective-permute-start.4 = (bf16[2,2,32,256]{3,2,1,0:T(8,128)(2,1)S(1)}, bf16[2,2,32,256]{3,2,1,0:T(8,128)(2,1)S(1)}, u32[]{:S(2)}, u32[]{:S(2)}) collective-permute-start(bf16[2,2,32,256]{3,2,1,0:T(8,128)(2,1)S(1)} %get-tuple-element.70), channel_id=1, source_target_pairs={{0,15},{1,2},{2,1},{3,4},{4,3},{5,6},{6,5},{7,8},{8,7},{9,10},{10,... | collective-permute-start | bytes 196616 | tf_op jit(solution)/shard_map/ppermute | solution.py:394
  20.4 12.5 %collective-permute-start.5 = (bf16[2,2,32,256]{3,2,1,0:T(8,128)(2,1)S(1)}, bf16[2,2,32,256]{3,2,1,0:T(8,128)(2,1)S(1)}, u32[]{:S(2)}, u32[]{:S(2)}) collective-permute-start(bf16[2,2,32,256]{3,2,1,0:T(8,128)(2,1)S(1)} %get-tuple-element.71), channel_id=1, source_target_pairs={{0,1},{1,0},{2,3},{3,2},{4,5},{5,4},{6,7},{7,6},{8,9},{9,8},{10,11... | collective-permute-start | bytes 196616 | tf_op jit(solution)/shard_map/ppermute | solution.py:394
  28.4 8.8 %collective-permute-start.6 = (bf16[1,16,2304]{2,1,0:T(8,128)(2,1)S(1)}, bf16[1,16,2304]{2,1,0:T(8,128)(2,1)S(1)}, u32[]{:S(2)}, u32[]{:S(2)}) collective-permute-start(bf16[1,16,2304]{2,1,0:T(8,128)(2,1)S(1)} %get-tuple-element.74), channel_id=1, source_target_pairs={{0,12},{1,13},{2,14},{3,15},{4,8},{5,9},{6,10},{7,11},{8,4},{9,5},... | collective-permute-start | bytes 221192 | tf_op jit(solution)/shard_map/ppermute | solution.py:394
  29.4 7.9 %collective-permute-start.7 = (bf16[1,16,2304]{2,1,0:T(8,128)(2,1)S(1)}, bf16[1,16,2304]{2,1,0:T(8,128)(2,1)S(1)}, u32[]{:S(2)}, u32[]{:S(2)}) collective-permute-start(bf16[1,16,2304]{2,1,0:T(8,128)(2,1)S(1)} %get-tuple-element.75), channel_id=1, source_target_pairs={{0,8},{1,9},{2,10},{3,11},{4,12},{5,13},{6,14},{7,15},{8,0},{9,1},... | collective-permute-start | bytes 221192 | tf_op jit(solution)/shard_map/ppermute | solution.py:394
  29.4 7.9 %collective-permute-start.8 = (bf16[1,16,2304]{2,1,0:T(8,128)(2,1)S(1)}, bf16[1,16,2304]{2,1,0:T(8,128)(2,1)S(1)}, u32[]{:S(2)}, u32[]{:S(2)}) collective-permute-start(bf16[1,16,2304]{2,1,0:T(8,128)(2,1)S(1)} %get-tuple-element.76), channel_id=1, source_target_pairs={{0,4},{1,5},{2,6},{3,7},{4,0},{5,1},{6,2},{7,3},{8,12},{9,13},{10,... | collective-permute-start | bytes 221192 | tf_op jit(solution)/shard_map/ppermute | solution.py:394

commit v6 on v5

--- a/solution.py
+++ b/solution.py
@@ -384,7 +384,14 @@
             cot = cot_ref[s, r0 : r0 + block].reshape(block * cols, ch).astype(F32)
             ig = (cot + acc).astype(BF16).reshape(block, cols, ch)
             ig_ref[s, r0 : r0 + block] = ig * mk[s, r0 : r0 + block]
-        stores += start_all([pltpu.make_async_copy(ig_ref.at[s], ig_hbm.at[s], sems.at[s])])
+            done = pl.ds(r0, block)
+            stores += start_all(
+                [
+                    pltpu.make_async_copy(
+                        ig_ref.at[s, done], ig_hbm.at[s, done], sems.at[s, r0 // block]
+                    )
+                ]
+            )
     for copy in stores:
         copy.wait()
 
@@ -579,7 +586,7 @@
                 pltpu.VMEM(field, BF16),
                 pltpu.VMEM((2, slots, rows, cols // 2, ch), BF16),
                 pltpu.VMEM((2, slots, rows + 2 * STEP, cols // 2, ch), BF16),
-                pltpu.SemaphoreType.DMA((slots,)),
+                pltpu.SemaphoreType.DMA((slots, rows // 8)),
             ],
             compiler_params=params,
             cost_estimate=pl.CostEstimate(

time: 38.1 us -> 38 us (level)
  transfers between devices with their start and end apart: 9 -> 9, of which waited for: 2 -> 2; matrix products, arithmetic and copies ran while one was open for 0% -> 0% of each run, Pallas kernels for 37% -> 36%
where the time goes in v6:
time: 38 us; the launch traced here: 37.9 us
  Pallas kernels  18.6 us (49%)
  starting transfers between devices  12.7 us (33%)
  waiting for transfers between devices  5.75 us (15%)
  between operations  0.77 us (2%)
    ppermute x9, starting transfers between devices, permute(): lax.ppermute(value, 'tiles', [(i, pairs_of(i, count)) for i in range(coun...  12.7 us
    pallas_call x1, Pallas kernels, shards(): pl.pallas_call(functools.partial(interior_kernel, own), out_shape=(shape_...  5.75 us
    ppermute x9, waiting for transfers between devices, permute(): lax.ppermute(value, 'tiles', [(i, pairs_of(i, count)) for i in range(coun...  5.75 us
    pallas_call x1, Pallas kernels, input_grad_call(): pl.pallas_call(input_grad_kernel, out_shape=shape_bf16(*field), in_specs=...  4.27 us
    pallas_call x1, Pallas kernels, gradient_call(): pl.pallas_call(gradient_kernel, out_shape=(shape_bf16(*field), shape_bf16...  2.15 us
    pallas_call x1, Pallas kernels, shards(): pl.pallas_call(load_kernel, out_shape=(shape_bf16(slots, 8, rows, ch), sh...  2.07 us
    pallas_call x1, Pallas kernels, shards(): pl.pallas_call(functools.partial(edge_kernel, own), out_shape=(shape_bf16...  1.8 us
    pallas_call x1, Pallas kernels, shards(): pl.pallas_call(keep_kernel, out_shape=(shape_f32(rank, wide),), in_specs=...  1.56 us
  transfers between devices with their start and end apart: 9, of which 2 were waited for; matrix products, arithmetic and copies ran while one was open for 0% of the time, Pallas kernels for 36%

profile of v6, /device:TPU:0, one launch (start us, length us, event | category | flops | bytes accessed | tf_op | source)
XLA Modules:
  0.0 37.9 jit_solution(9010332218712482415)
XLA Ops:
  0.6 0.0 copy-start.1
  0.6 0.0 copy-start.2
  0.7 0.0 copy-start
  0.7 2.1 %load.1 = (bf16[2,8,32,256]{3,2,1,0:T(8,128)(2,1)S(1)}, bf16[2,2,2,32,256]{4,3,2,1,0:T(8,128)(2,1)S(1)}, bf16[2,32,32,256]{3,2,1,0:T(8,128)(2,1)S(1)}, bf16[2,32,32,256]{3,2,1,0:T(8,128)(2,1)S(1)}) custom-call(bf16[2,32,32,256]{3,2,1,0:T(8,128)(2,1)} %x_hbm.1, bf16[2,32,32,256]{3,2,1,0:T(8,128)(2,1)} %cot_hbm.1), custom_call_target="tpu_custom_call" | custom-call | tf_op jit(solution)/shard_map/load/pallas_call | solution.py:493
  2.7 0.0 copy-done.1
  2.7 0.1 mask_edges.1
  2.9 5.5 %collective-permute-start = (bf16[2,2,32,256]{3,2,1,0:T(8,128)(2,1)S(1)}, bf16[2,2,32,256]{3,2,1,0:T(8,128)(2,1)S(1)}, u32[]{:S(2)}, u32[]{:S(2)}) collective-permute-start(bf16[2,2,32,256]{3,2,1,0:T(8,128)(2,1)S(1)} %get-tuple-element.48), channel_id=1, source_target_pairs={{0,15},{1,2},{2,1},{3,4},{4,3},{5,6},{6,5},{7,8},{8,7},{9,10},{10,... | collective-permute-start | bytes 196616 | tf_op jit(solution)/shard_map/ppermute | solution.py:401
  8.4 0.0 collective-permute-start.1
  8.4 0.0 copy-done.2
  8.4 0.0 copy-done
  8.4 5.8 %interior.1 = (bf16[2,32,32,256]{3,2,1,0:T(8,128)(2,1)S(1)}, bf16[2,32,32,256]{3,2,1,0:T(8,128)(2,1)S(1)}, f32[128,2304]{1,0:T(8,128)S(1)}, bf16[2,36,32,768]{3,...) custom-call(s32[2,8]{1,0:T(2,128)S(1)} %copy-done.2, bf16[2,32,32,256]{3,2,1,0:T(8,128)(2,1)S(1)} %get-tuple-element.40.x_ref, ...), custom_call_target="tpu_custom_call" | custom-call | flops 4831838208 | bytes 8388608 | tf_op jit(solution)/shard_map/interior/pallas_call | solution.py:520
  14.2 0.0 collective-permute-done.across_ref
  14.2 0.0 collective-permute-done.1.pair_ref
  14.2 1.8 %edges.1 = (bf16[2,2,32,256]{3,2,1,0:T(8,128)(2,1)S(1)}, bf16[2,2,32,256]{3,2,1,0:T(8,128)(2,1)S(1)}, bf16[2,2,2,32,256]{4,3,2,1,0:T(8,128)(2,1)S(1)}, bf16[2,2,...) custom-call(s32[2,8]{1,0:T(2,128)S(1)} %copy-done.2, ...), custom_call_target="tpu_custom_call" | custom-call | flops 603979776 | bytes 6291456 | tf_op jit(solution)/shard_map/edges/pallas_call | solution.py:539
  16.0 0.6 %collective-permute-start.2 = (bf16[128,2304]{1,0:T(8,128)(2,1)S(1)}, bf16[128,2304]{1,0:T(8,128)(2,1)S(1)}, u32[]{:S(2)}, u32[]{:S(2)}) collective-permute-start(bf16[128,2304]{1,0:T(8,128)(2,1)S(1)} %get-tuple-element.55), channel_id=1, source_target_pairs={{0,1},{1,0},{2,3},{3,2},{4,5},{5,4},{6,7},{7,6},{8,9},{9,8},{10,11... | collective-permute-start | bytes 1769480 | tf_op jit(solution)/shard_map/ppermute | solution.py:401
  16.5 1.6 %keep.1 = f32[128,2304]{1,0:T(8,128)S(1)} custom-call(bf16[2,36,32,768]{3,2,1,0:T(8,128)(2,1)S(1)} %get-tuple-element.44.xc, bf16[2,256,1024]{2,1,0:T(8,128)(2,1)S(1)} %get-tuple-element.45.gt, bf16[3,2,2,2,32,768]{5,4,3,2,1,0:T(8,128)(2,1)S(1)} %get-tuple-element.53.win, bf16[256,256]{1,0:T(8,128)(2,1)S(1)} %get-tuple-element.54.edge_gt), custom_call_target="tpu_custom_call" | custom-call | flops 1358954496 | tf_op jit(solution)/shard_map/keep/pallas_call | solution.py:608
  18.1 0.1 collective-permute-done.2
  18.2 0.1 middle_terms.1
  18.3 0.1 collective-permute-start.3
  18.4 2.0 %collective-permute-start.4 = (bf16[2,2,32,256]{3,2,1,0:T(8,128)(2,1)S(1)}, bf16[2,2,32,256]{3,2,1,0:T(8,128)(2,1)S(1)}, u32[]{:S(2)}, u32[]{:S(2)}) collective-permute-start(bf16[2,2,32,256]{3,2,1,0:T(8,128)(2,1)S(1)} %get-tuple-element.70), channel_id=1, source_target_pairs={{0,15},{1,2},{2,1},{3,4},{4,3},{5,6},{6,5},{7,8},{8,7},{9,10},{10,... | collective-permute-start | bytes 196616 | tf_op jit(solution)/shard_map/ppermute | solution.py:401
  20.4 0.1 collective-permute-start.5
  20.5 2.2 %gradient.1 = (bf16[2,32,32,256]{3,2,1,0:T(8,128)(2,1)}, bf16[2,36,32,768]{3,2,1,0:T(8,128)(2,1)S(1)}, bf16[2,32,32,256]{3,2,1,0:T(8,128)(2,1)S(1)}, bf16[3,768,256]{2,1,0:T(8,128)(2,1)S(1)}) custom-call(s32[2,8]{1,0:T(2,128)S(1)} %copy-done.2, bf16[2,32,32,256]{3,2,1,0:T(8,128)(2,1)S(1)} %get-tuple-element.42.gi_ref, ...), custom_call_target="tpu_custom_call" | custom-call | flops 2147483648 | tf_op jit(solution)/shard_map/gradient/pallas_call | solution.py:563
  22.7 5.7 %collective-permute-done.3 = bf16[4,16,2304]{2,1,0:T(8,128)(2,1)S(1)} collective-permute-done((bf16[4,16,2304]{2,1,0:T(8,128)(2,1)S(1)}, bf16[4,16,2304]{2,1,0:T(8,128)(2,1)S(1)}, u32[]{:S(2)}, u32[]{:S(2)}) %collective-permute-start.3) | collective-permute-done | bytes 294944 | tf_op jit(solution)/shard_map/ppermute | solution.py:401
  28.3 0.1 outer_terms.1
  28.4 0.9 %collective-permute-start.6 = (bf16[1,16,2304]{2,1,0:T(8,128)(2,1)S(1)}, bf16[1,16,2304]{2,1,0:T(8,128)(2,1)S(1)}, u32[]{:S(2)}, u32[]{:S(2)}) collective-permute-start(bf16[1,16,2304]{2,1,0:T(8,128)(2,1)S(1)} %get-tuple-element.74), channel_id=1, source_target_pairs={{0,12},{1,13},{2,14},{3,15},{4,8},{5,9},{6,10},{7,11},{8,4},{9,5},... | collective-permute-start | bytes 221192 | tf_op jit(solution)/shard_map/ppermute | solution.py:401
  29.4 0.0 collective-permute-start.7
  29.4 3.5 %collective-permute-start.8 = (bf16[1,16,2304]{2,1,0:T(8,128)(2,1)S(1)}, bf16[1,16,2304]{2,1,0:T(8,128)(2,1)S(1)}, u32[]{:S(2)}, u32[]{:S(2)}) collective-permute-start(bf16[1,16,2304]{2,1,0:T(8,128)(2,1)S(1)} %get-tuple-element.76), channel_id=1, source_target_pairs={{0,4},{1,5},{2,6},{3,7},{4,0},{5,1},{6,2},{7,3},{8,12},{9,13},{10,... | collective-permute-start | bytes 221192 | tf_op jit(solution)/shard_map/ppermute | solution.py:401
  32.9 0.0 collective-permute-done.4.across_ref
  32.9 0.0 collective-permute-done.5.pair_ref
  32.9 4.3 %input_grad.1 = bf16[2,32,32,256]{3,2,1,0:T(8,128)(2,1)} custom-call(s32[2,8]{1,0:T(2,128)S(1)} %copy-done.2, bf16[2,36,32,768]{3,2,1,0:T(8,128)(2,1)S(1)} %get-tuple-element.68.gc, bf16[2,32,32,256]{3,2,1,0:T(8,128)(2,1)S(1)} %get-tuple-element.69.mk, bf16[2,2,32,256]{3,2,1,0:T(8,128)(2,1)S(1)} %collective-permute-done.4.across_ref, ...), custom_call_target="tpu_custom_call" | custom-call | flops 2415919104 | bytes 8388608 | tf_op jit(solution)/shard_map/input_grad/pallas_call | solution.py:580
  37.1 0.0 collective-permute-done.6.refs_0_
  37.2 0.0 collective-permute-done.7.refs_1_
  37.2 0.0 collective-permute-done.8.refs_2_
  37.2 0.7 %last_sum.1 = f32[1,16,2304]{2,1,0:T(8,128)} custom-call(f32[1,16,2304]{2,1,0:T(8,128)S(1)} %get-tuple-element.73.keep_ref, bf16[1,16,2304]{2,1,0:T(8,128)(2,1)S(1)} %collective-permute-done.6.refs_0_, bf16[1,16,2304]{2,1,0:T(8,128)(2,1)S(1)} %collective-permute-done.7.refs_1_, bf16[1,16,2304]{2,1,0:T(8,128)(2,1)S(1)} %collective-permute-done.8.refs_2_), custom_call_target="tpu_custom_call" | custom-call | tf_op jit(solution)/shard_map/last_sum/pallas_call | solution.py:464
Async XLA Ops:
  0.6 2.1 %copy-start.1 = (s32[2,32,32]{2,1,0:T(8,128)S(1)}, s32[2,32,32]{2,1,0:T(8,128)}, u32[]{:S(2)}) copy-start(s32[2,32,32]{2,1,0:T(8,128)} %mask_ref.1) | copy-start | bytes 24580
  0.6 7.8 %copy-start.2 = (s32[2,8]{1,0:T(2,128)S(1)}, s32[2,8]{1,0:T(2,128)}, u32[]{:S(2)}) copy-start(s32[2,8]{1,0:T(2,128)} %nbr_ref.7) | copy-start | bytes 196
  0.7 7.7 %copy-start = (bf16[9,256,256]{2,1,0:T(8,128)(2,1)S(1)}, bf16[9,256,256]{2,1,0:T(8,128)(2,1)}, u32[]{:S(2)}) copy-start(bf16[9,256,256]{2,1,0:T(8,128)(2,1)} %param.7) | copy-start | bytes 3538948
  2.9 11.3 %collective-permute-start = (bf16[2,2,32,256]{3,2,1,0:T(8,128)(2,1)S(1)}, bf16[2,2,32,256]{3,2,1,0:T(8,128)(2,1)S(1)}, u32[]{:S(2)}, u32[]{:S(2)}) collective-permute-start(bf16[2,2,32,256]{3,2,1,0:T(8,128)(2,1)S(1)} %get-tuple-element.48), channel_id=1, source_target_pairs={{0,15},{1,2},{2,1},{3,4},{4,3},{5,6},{6,5},{7,8},{8,7},{9,10},{10,... | collective-permute-start | bytes 196616 | tf_op jit(solution)/shard_map/ppermute | solution.py:401
  8.4 5.8 %collective-permute-start.1 = (bf16[2,2,32,256]{3,2,1,0:T(8,128)(2,1)S(1)}, bf16[2,2,32,256]{3,2,1,0:T(8,128)(2,1)S(1)}, u32[]{:S(2)}, u32[]{:S(2)}) collective-permute-start(bf16[2,2,32,256]{3,2,1,0:T(8,128)(2,1)S(1)} %get-tuple-element.49), channel_id=1, source_target_pairs={{0,1},{1,0},{2,3},{3,2},{4,5},{5,4},{6,7},{7,6},{8,9},{9,8},{10,11... | collective-permute-start | bytes 196616 | tf_op jit(solution)/shard_map/ppermute | solution.py:401
  16.0 2.2 %collective-permute-start.2 = (bf16[128,2304]{1,0:T(8,128)(2,1)S(1)}, bf16[128,2304]{1,0:T(8,128)(2,1)S(1)}, u32[]{:S(2)}, u32[]{:S(2)}) collective-permute-start(bf16[128,2304]{1,0:T(8,128)(2,1)S(1)} %get-tuple-element.55), channel_id=1, source_target_pairs={{0,1},{1,0},{2,3},{3,2},{4,5},{5,4},{6,7},{7,6},{8,9},{9,8},{10,11... | collective-permute-start | bytes 1769480 | tf_op jit(solution)/shard_map/ppermute | solution.py:401
  18.3 10.1 %collective-permute-start.3 = (bf16[4,16,2304]{2,1,0:T(8,128)(2,1)S(1)}, bf16[4,16,2304]{2,1,0:T(8,128)(2,1)S(1)}, u32[]{:S(2)}, u32[]{:S(2)}) collective-permute-start(bf16[4,16,2304]{2,1,0:T(8,128)(2,1)S(1)} %get-tuple-element.62), channel_id=1, source_target_pairs={{0,2},{1,3},{2,0},{3,1},{4,6},{5,7},{6,4},{7,5},{8,10},{9,11},{10,... | collective-permute-start | bytes 884744 | tf_op jit(solution)/shard_map/ppermute | solution.py:401
  18.4 14.5 %collective-permute-start.4 = (bf16[2,2,32,256]{3,2,1,0:T(8,128)(2,1)S(1)}, bf16[2,2,32,256]{3,2,1,0:T(8,128)(2,1)S(1)}, u32[]{:S(2)}, u32[]{:S(2)}) collective-permute-start(bf16[2,2,32,256]{3,2,1,0:T(8,128)(2,1)S(1)} %get-tuple-element.70), channel_id=1, source_target_pairs={{0,15},{1,2},{2,1},{3,4},{4,3},{5,6},{6,5},{7,8},{8,7},{9,10},{10,... | collective-permute-start | bytes 196616 | tf_op jit(solution)/shard_map/ppermute | solution.py:401
  20.4 12.5 %collective-permute-start.5 = (bf16[2,2,32,256]{3,2,1,0:T(8,128)(2,1)S(1)}, bf16[2,2,32,256]{3,2,1,0:T(8,128)(2,1)S(1)}, u32[]{:S(2)}, u32[]{:S(2)}) collective-permute-start(bf16[2,2,32,256]{3,2,1,0:T(8,128)(2,1)S(1)} %get-tuple-element.71), channel_id=1, source_target_pairs={{0,1},{1,0},{2,3},{3,2},{4,5},{5,4},{6,7},{7,6},{8,9},{9,8},{10,11... | collective-permute-start | bytes 196616 | tf_op jit(solution)/shard_map/ppermute | solution.py:401
  28.4 8.7 %collective-permute-start.6 = (bf16[1,16,2304]{2,1,0:T(8,128)(2,1)S(1)}, bf16[1,16,2304]{2,1,0:T(8,128)(2,1)S(1)}, u32[]{:S(2)}, u32[]{:S(2)}) collective-permute-start(bf16[1,16,2304]{2,1,0:T(8,128)(2,1)S(1)} %get-tuple-element.74), channel_id=1, source_target_pairs={{0,12},{1,13},{2,14},{3,15},{4,8},{5,9},{6,10},{7,11},{8,4},{9,5},... | collective-permute-start | bytes 221192 | tf_op jit(solution)/shard_map/ppermute | solution.py:401
  29.4 7.8 %collective-permute-start.7 = (bf16[1,16,2304]{2,1,0:T(8,128)(2,1)S(1)}, bf16[1,16,2304]{2,1,0:T(8,128)(2,1)S(1)}, u32[]{:S(2)}, u32[]{:S(2)}) collective-permute-start(bf16[1,16,2304]{2,1,0:T(8,128)(2,1)S(1)} %get-tuple-element.75), channel_id=1, source_target_pairs={{0,8},{1,9},{2,10},{3,11},{4,12},{5,13},{6,14},{7,15},{8,0},{9,1},... | collective-permute-start | bytes 221192 | tf_op jit(solution)/shard_map/ppermute | solution.py:401
  29.4 7.8 %collective-permute-start.8 = (bf16[1,16,2304]{2,1,0:T(8,128)(2,1)S(1)}, bf16[1,16,2304]{2,1,0:T(8,128)(2,1)S(1)}, u32[]{:S(2)}, u32[]{:S(2)}) collective-permute-start(bf16[1,16,2304]{2,1,0:T(8,128)(2,1)S(1)} %get-tuple-element.76), channel_id=1, source_target_pairs={{0,4},{1,5},{2,6},{3,7},{4,0},{5,1},{6,2},{7,3},{8,12},{9,13},{10,... | collective-permute-start | bytes 221192 | tf_op jit(solution)/shard_map/ppermute | solution.py:401
